TPU v7x, 512 devices: a whole 4x8x8 slice. The times are simulated.
512 devices in a mesh: gx: 8 (over z_hi, x), gy: 16 (over y, core), ma: 4 (over z_lo).
Axes of the slice: x: 4, y: 8, z: 8 (z_hi: 2, z_lo: 4; z = z_hi * 4 + z_lo), core: 2. Of those that a mesh axis runs over, the one named last changes fastest.
Arguments:
- pod_modes: bfloat16 [256, 4, 16, 128, 128], P('ma', None, 'gx', 'gy'), may hold values from -6 to 6
- velocity: float32 [3, 16, 128, 128], P(None, 'gx', 'gy'), may hold values from -1 to 1
- region: int32 [16, 128, 128], P('gx', 'gy'), may hold values from 0 to 7
- partner: int32 [128], replicated, may hold values from 0 to 127, each once
- coupling_table: float32 [8, 4, 4], replicated, may hold values from -3 to 3
Outputs:
- reduced: float32 [4, 256, 256], P(None, None, 'ma')
Inputs may be any that keep to these rules, and one draw needn't show every extreme that they name: `partner`: each of the 128 plane numbers appears once.
All inputs are finite; a program needn't handle non-finite values.
Results may differ from a plain program's by a relative error of at most 0.0029.
Values may be sent and summed in bfloat16 or wider, within the bound.
No kernel may reach another device: no remote copies, remote signals or barrier semaphores. Data moves between devices by JAX's collectives and lax.ppermute only.
A program may use at most 64 MiB of HBM per device.

v0:
```python
import math

import jax
import jax.numpy as jnp
from jax import lax
from jax.sharding import PartitionSpec as P


def extended(cells, sides, width):
    for axis, dim in sides:
        count = lax.axis_size(axis)
        ends = count - 1
        head = lax.slice_in_dim(cells, 0, width, axis=dim)
        tail = lax.slice_in_dim(cells, cells.shape[dim] - width, cells.shape[dim], axis=dim)
        cells = jnp.concatenate(
            [
                lax.ppermute(tail, axis, [(i, (i + 1) % count) for i in range(ends)]),
                cells,
                lax.ppermute(head, axis, [((i + 1) % count, i) for i in range(ends)]),
            ],
            axis=dim,
        )
    return cells


def coupling_terms(centre, coefficients):
    outputs = []
    for field_out in range(centre.shape[1]):
        running = coefficients[field_out, 0] * centre[:, 0]
        for field_in in range(1, centre.shape[1]):
            running = running + coefficients[field_out, field_in] * centre[:, field_in]
        outputs.append(running)
    return jnp.stack(outputs, axis=1)


def cell_coupling(region, coupling_table):
    fields = coupling_table.shape[1]
    off_diagonal = 1.0 - jnp.eye(fields, dtype=jnp.float32)
    masked = coupling_table * off_diagonal[None]
    coefficients = jnp.zeros((fields, fields) + region.shape, jnp.float32)
    for region_id in range(coupling_table.shape[0]):
        coefficients = jnp.where(
            region[None, None] == region_id, masked[region_id][:, :, None, None, None], coefficients
        )
    return coefficients


def face_terms(padded, speeds, coefficients):
    centre = padded[:, :, 1:-1, 1:-1].astype(jnp.float32)
    upper_cells = padded[:, :, 2:, 1:-1].astype(jnp.float32)
    lower_cells = padded[:, :, :-2, 1:-1].astype(jnp.float32)
    term_x = speeds[0] * (0.5 * (upper_cells - lower_cells))
    right_cells = padded[:, :, 1:-1, 2:].astype(jnp.float32)
    left_cells = padded[:, :, 1:-1, :-2].astype(jnp.float32)
    term_y = speeds[1] * (0.5 * (right_cells - left_cells))
    term_c = coupling_terms(centre, coefficients)
    return (term_x.astype(jnp.bfloat16), term_y.astype(jnp.bfloat16), term_c.astype(jnp.bfloat16))


def jump_term(block, speed_z, partner):
    centre = block.astype(jnp.float32)
    return (speed_z * (jnp.take(centre, partner, axis=4) - centre)).astype(jnp.bfloat16)


def on_device(pod_modes, velocity, region, partner, coupling_table):
    blocks, fields, cells_x, cells_y, planes = pod_modes.shape
    cell_total = fields * cells_x * lax.axis_size("gx") * cells_y * lax.axis_size("gy") * planes
    scaling = 1.0 / math.sqrt(cell_total)
    coefficients = cell_coupling(region, coupling_table)
    padded = extended(pod_modes, (("gx", 2), ("gy", 3)), 1)
    image_x, image_y, image_c = face_terms(padded, velocity, coefficients)
    jump_images = jump_term(pod_modes, velocity[2], partner)
    stacked = jnp.stack((image_x, image_y, jump_images, image_c)).reshape(4, blocks, -1)
    portion = lax.all_gather(pod_modes, "ma", axis=0, tiled=True)
    flattened = portion.reshape(portion.shape[0], -1)
    partial_sums = jnp.einsum("ik,qjk->qij", flattened, stacked, preferred_element_type=jnp.float32)
    summed = lax.psum(partial_sums, ("gx", "gy"))
    return summed * scaling


def solution(mesh):
    placed = (
        P("ma", None, "gx", "gy", None),
        P(None, "gx", "gy", None),
        P("gx", "gy", None),
        P(),
        P(),
    )
    return jax.shard_map(
        on_device, mesh=mesh, in_specs=placed, out_specs=P(None, None, "ma"), check_vma=False
    )
```

profile of v0, /device:TPU:1, one launch (start us, length us, event | category | flops | bytes accessed | tf_op | source)
XLA Modules:
  0.0 1557.1 jit_solution(10789021940769803880)
XLA Ops:
  6.5 2.9 copy.14
  9.5 1.4 fusion.31
  10.9 4.0 collective-permute-start.1
  14.9 1.3 collective-permute-start
  16.2 0.1 broadcast_multiply_fusion.1
  16.3 0.2 slice_reduce_fusion.7
  16.6 0.6 multiply_bitcast_fusion.1
  17.2 0.2 select_select_fusion
  17.4 0.5 compare_and_fusion
  17.9 0.6 pad_clamp_fusion
  18.5 3.6 collective-permute-done.1
  22.1 0.8 copy-done.5
  23.0 0.8 constant_dynamic-update-slice_fusion.1
  23.7 2.3 collective-permute-done
  26.1 1.4 copy-done.3
  27.5 0.9 fusion.30
  28.3 7.0 collective-permute-start.2
  35.4 3.1 collective-permute-start.3
  38.5 2.8 copy.19
  41.3 5.4 gather_fusion
  46.6 4.8 copy.20
  51.4 1.2 fusion.25
  52.6 0.6 copy-done.2
  53.2 1.8 fusion.24
  55.0 0.4 fusion.22
  55.5 1.2 fusion.27
  56.7 0.5 copy-done.4
  57.3 1.3 fusion.23
  58.5 51.8 %all-gather.2.cloned.1.call-done = bf16[256,4,2,8,128]{4,0,3,2,1:T(8,128)(2,1)} async-done(((bf16[64,4,2,8,128]{4,0,3,2,1:T(8,128)(2,1)}), bf16[256,4,2,8,128]{4,0,3,2,1:T(8,128)(2,1)}) %all-gather.2.cloned.1.call-update) | async-done | bytes 4194320 | tf_op jit(solution)/shard_map/all_gather | solution.py:74
  110.3 4.5 fusion.17
  114.8 1433.8 %all-reduce.2.cloned.1.call-done = f32[4,256,64]{1,2,0:T(8,128)} async-done(((f32[4,256,64]{1,2,0:T(8,128)}), f32[4,256,64]{1,2,0:T(8,128)}) %all-reduce.2.cloned.1.call-update) | async-done | bytes 262160 | tf_op jit(solution)/shard_map/psum | solution.py:77
  1548.6 1.7 broadcast_multiply_fusion
  (40 shorter events, 0.3 us)
Async XLA Ops:
  6.5 103.8 %all-gather.2.cloned.1.call-start = ((), (), s32[]{:S(2)}) async-start(), calls=%async_computation | async-start | bytes 5242880 | tf_op jit(solution)/shard_map/all_gather | solution.py:74
  9.4 6.8 copy-start.13
  9.4 7.1 copy-start.15
  9.4 7.1 copy-start.12
  9.4 7.1 copy-start.11
  9.5 13.5 copy-start.1
  9.5 1539.2 %all-reduce.2.cloned.1.call-start = ((), (), s32[]{:S(2)}) async-start(), calls=%async_computation.1 | async-start | bytes 524288 | tf_op jit(solution)/shard_map/psum | solution.py:77
  10.9 11.2 collective-permute-start.1
  14.9 11.1 collective-permute-start
  22.1 0.8 copy-start.5
  26.0 2.3 copy-start.7
  26.1 1.4 copy-start.3
  28.3 28.4 %collective-permute-start.2 = (bf16[64,4,4,1,128]{4,0,3,2,1:T(8,128)(2,1)}, bf16[64,4,4,1,128]{4,0,3,2,1:T(8,128)(2,1)S(1)}, u32[]{:S(2)}, u32[]{:S(2)}) collective-permute-start(bf16[64,4,4,1,128]{4,0,3,2,1:T(8,128)(2,1)} %get-tuple-element.13), channel_id=1, source_target_pairs={{4,0},{8,4},{12,8},{16,12},{20,16},{24,20},{28,24},{32,28},{36,32}... | collective-permute-start | bytes 786440 | tf_op jit(solution)/shard_map/ppermute | solution.py:19
  35.4 21.3 %collective-permute-start.3 = (bf16[64,4,4,1,128]{4,0,3,2,1:T(8,128)(2,1)}, bf16[64,4,4,1,128]{4,0,3,2,1:T(8,128)(2,1)}, u32[]{:S(2)}, u32[]{:S(2)}) collective-permute-start(bf16[64,4,4,1,128]{4,0,3,2,1:T(8,128)(2,1)} %get-tuple-element.14), channel_id=1, source_target_pairs={{0,4},{4,8},{8,12},{12,16},{16,20},{20,24},{24,28},{28,32},{32,36}... | collective-permute-start | bytes 786440 | tf_op jit(solution)/shard_map/ppermute | solution.py:17
  51.4 1.8 copy-start.2
  51.4 1.8 copy-start.10
  51.4 1.8 copy-start.14
  53.2 1.8 copy-start
  53.2 1.8 copy-start.6
  53.2 1.8 copy-start.8
  55.5 1.8 copy-start.4
  56.7 53.6 %copy-start.9 = (bf16[1,64,4,2,8,128]{5,1,4,3,2,0:T(8,128)(2,1)S(1)}, bf16[1,64,4,2,8,128]{5,1,4,3,2,0:T(8,128)(2,1)}, u32[]{:S(2)}) copy-start(bf16[1,64,4,2,8,128]{5,1,4,3,2,0:T(8,128)(2,1)} %fusion.24) | copy-start | bytes 3145732
Sparse Core Ops, SparseCore 0:
  9.6 100.6 all-gather.1
  115.0 1433.6 all-reduce.1
where the time goes:
time: 1560 us
  waiting for transfers between devices  1490 us (96%)
  local copies, waits for them, and re-layouts  21.7 us (1%)
    psum x1, waiting for transfers between devices, on_device(): summed = lax.psum(partial_sums, ('gx', 'gy'))  1430 us
    all_gather x1, waiting for transfers between devices, on_device(): portion = lax.all_gather(pod_modes, 'ma', axis=0, tiled=True)  51.8 us
  transfers between devices with their start and end apart: 6, of which 4 were waited for; matrix products, arithmetic and copies ran while one was open for 2% of the time, Pallas kernels for 0%

commit v1 on v0

--- a/solution.py
+++ b/solution.py
@@ -62,6 +62,19 @@
     return (speed_z * (jnp.take(centre, partner, axis=4) - centre)).astype(jnp.bfloat16)
 
 
+def summed_over_cells(partial_sums, shares, scaling):
+    terms, columns, rows = partial_sums.shape
+    lanes = 128
+    pieces = partial_sums.reshape(terms, columns, rows // lanes, lanes).transpose(2, 0, 1, 3)
+    pieces = pieces.reshape(shares, -1, lanes).astype(jnp.bfloat16)
+    received = lax.all_to_all(pieces, ("gx", "gy"), 0, 0)
+    share = jnp.sum(received.astype(jnp.float32), axis=0) * scaling
+    spread = jnp.broadcast_to(share.astype(jnp.bfloat16)[None], received.shape)
+    whole = lax.all_to_all(spread, ("gx", "gy"), 0, 0)
+    whole = whole.reshape(rows // lanes, terms, columns, lanes).transpose(1, 0, 3, 2)
+    return whole.reshape(terms, rows, columns).astype(jnp.float32)
+
+
 def on_device(pod_modes, velocity, region, partner, coupling_table):
     blocks, fields, cells_x, cells_y, planes = pod_modes.shape
     cell_total = fields * cells_x * lax.axis_size("gx") * cells_y * lax.axis_size("gy") * planes
@@ -73,9 +86,9 @@
     stacked = jnp.stack((image_x, image_y, jump_images, image_c)).reshape(4, blocks, -1)
     portion = lax.all_gather(pod_modes, "ma", axis=0, tiled=True)
     flattened = portion.reshape(portion.shape[0], -1)
-    partial_sums = jnp.einsum("ik,qjk->qij", flattened, stacked, preferred_element_type=jnp.float32)
-    summed = lax.psum(partial_sums, ("gx", "gy"))
-    return summed * scaling
+    shares = lax.axis_size("gx") * lax.axis_size("gy")
+    partial_sums = jnp.einsum("qjk,ik->qji", stacked, flattened, preferred_element_type=jnp.float32)
+    return summed_over_cells(partial_sums, shares, scaling)
 
 
 def solution(mesh):

time: 1560 us -> 189 us (0.12)
  waiting for transfers between devices: 1490 us -> 53 us
  blocking collectives: 0 us -> 59.1 us
  local copies, waits for them, and re-layouts: 21.7 us -> 39.2 us
    psum x1 -> x0, waiting for transfers between devices: 1430 us -> none  [on_device(): summed = lax.psum(partial_sums, ('gx', 'gy'))]
    all_to_all x0 -> x2, blocking collectives: none -> 59.1 us  [the longest x1 38.4 us: summed_over_cells(): received = lax.all_to_all(pieces, ('gx', 'gy'), 0, 0)]
  transfers between devices with their start and end apart: 6 -> 5, of which waited for: 4 -> 1; matrix products, arithmetic and copies ran while one was open for 2% -> 19% of each run, Pallas kernels for 0% -> 0%
where the time goes in v1:
time: 189 us; the launch traced here: 188 us
  blocking collectives  59.1 us (31%)
  waiting for transfers between devices  53 us (28%)
  local copies, waits for them, and re-layouts  39.2 us (21%)
  starting transfers between devices  13.9 us (7%)
  between operations  13.7 us (7%)
  other arithmetic  5.54 us (3%)
  matrix products  3.79 us (2%)
    all_gather x1, waiting for transfers between devices, on_device(): portion = lax.all_gather(pod_modes, 'ma', axis=0, tiled=True)  52.2 us
    all_to_all x1, blocking collectives, summed_over_cells(): received = lax.all_to_all(pieces, ('gx', 'gy'), 0, 0)  38.4 us
    all_to_all x1, blocking collectives, summed_over_cells(): whole = lax.all_to_all(spread, ('gx', 'gy'), 0, 0)  20.7 us
    gather x2, local copies, waits for them, and re-layouts, jump_term(): jnp.take(centre, partner, axis=4) - centre  9.96 us
    dot_general x1, local copies, waits for them, and re-layouts, on_device(): jnp.einsum('qjk,ik->qji', stacked, flattened, preferred_element_type=jnp....  7.31 us
    ppermute x2, starting transfers between devices, extended(): lax.ppermute(head, axis, [((i + 1) % count, i) for i in range(ends)])  7.29 us
    ppermute x2, starting transfers between devices, extended(): lax.ppermute(tail, axis, [(i, (i + 1) % count) for i in range(ends)])  6.65 us
    unnamed x26, local copies, waits for them, and re-layouts  5.23 us
  transfers between devices with their start and end apart: 5, of which 1 were waited for; matrix products, arithmetic and copies ran while one was open for 19% of the time, Pallas kernels for 0%

profile of v1, /device:TPU:1, one launch (start us, length us, event | category | flops | bytes accessed | tf_op | source)
XLA Modules:
  0.0 188.2 jit_solution(948319793681001157)
XLA Ops:
  6.5 0.7 all-gather.2.cloned.1.call-update
  7.3 1.4 fusion.24
  8.6 1.0 copy.127
  9.6 4.7 %collective-permute-start.1 = (bf16[64,4,1,8,128]{4,0,3,2,1:T(8,128)(2,1)}, bf16[64,4,1,8,128]{4,0,3,2,1:T(8,128)(2,1)}, u32[]{:S(2)}, u32[]{:S(2)}) collective-permute-start(bf16[64,4,1,8,128]{4,0,3,2,1:T(8,128)(2,1)} %copy.127), channel_id=1, source_target_pairs={{0,64},{64,128},{128,192},{192,256},{256,320},{320,384},{384,448},... | collective-permute-start | bytes 1572872 | tf_op jit(solution)/shard_map/ppermute | solution.py:17
  14.4 1.0 copy.128
  15.4 1.3 collective-permute-start
  17.0 2.9 %copy.108 = f32[64,4,2,8,128]{0,3,4,2,1:T(8,128)} copy(bf16[64,4,2,8,128]{4,3,2,1,0:T(8,128)(2,1)S(1)} %copy-done) | data formatting | bytes 3145728 | tf_op jit(solution)/shard_map/convert_element_type | solution.py:61
  21.2 0.3 copy.117
  21.5 1.3 convert_element_type.84
  22.9 5.2 %gather_fusion = f32[128,64,4,2,8]{1,4,3,2,0:T(8,128)} fusion(f32[64,4,2,8,128]{0,3,4,2,1:T(8,128)} %copy.108, s32[1024]{0:T(1024)S(1)} %pad_clamp_fusion), kind=kCustom, calls=%fused_computation | custom fusion | bytes 4194816 | tf_op jit(solution)/shard_map/jit(_take)/gather | solution.py:62
  28.1 4.7 %copy.109 = f32[128,64,4,2,8]{0,4,3,2,1:T(8,128)S(1)} copy(f32[128,64,4,2,8]{1,4,3,2,0:T(8,128)} %gather_fusion) | data formatting | bytes 4194304 | tf_op jit(solution)/shard_map/jit(_take)/gather | solution.py:62
  32.9 1.1 constant_dynamic-update-slice_fusion.2
  34.0 0.7 constant_dynamic-update-slice_fusion.1
  34.7 1.1 constant_dynamic-update-slice_fusion
  35.9 1.3 copy-done.1
  37.2 0.8 fusion.23
  38.0 6.0 %collective-permute-start.2 = (bf16[64,4,4,1,128]{4,0,3,2,1:T(8,128)(2,1)}, bf16[64,4,4,1,128]{4,0,3,2,1:T(8,128)(2,1)S(1)}, u32[]{:S(2)}, u32[]{:S(2)}) collective-permute-start(bf16[64,4,4,1,128]{4,0,3,2,1:T(8,128)(2,1)} %get-tuple-element.13), channel_id=1, source_target_pairs={{4,0},{8,4},{12,8},{16,12},{20,16},{24,20},{28,24},{32,28},{36,32}... | collective-permute-start | bytes 786440 | tf_op jit(solution)/shard_map/ppermute | solution.py:19
  44.0 1.9 %collective-permute-start.3 = (bf16[64,4,4,1,128]{4,0,3,2,1:T(8,128)(2,1)}, bf16[64,4,4,1,128]{4,0,3,2,1:T(8,128)(2,1)}, u32[]{:S(2)}, u32[]{:S(2)}) collective-permute-start(bf16[64,4,4,1,128]{4,0,3,2,1:T(8,128)(2,1)} %get-tuple-element.14), channel_id=1, source_target_pairs={{0,4},{4,8},{8,12},{12,16},{16,20},{20,24},{24,28},{28,32},{32,36}... | collective-permute-start | bytes 786440 | tf_op jit(solution)/shard_map/ppermute | solution.py:17
  46.0 1.4 copy.103
  47.4 1.4 copy.105
  48.8 2.1 %multiply_convert_fusion.1 = (bf16[64,4,2,8,128]{4,3,2,1,0:T(8,128)(2,1)}, bf16[64,4,2,8,128]{4,3,2,1,0:T(8,128)(2,1)}) fusion(bf16[64,4,2,8,128]{4,3,2,1,0:T(8,128)(2,1)S(1)} %copy-done, bf16[64,4,1,8,128]{4,3,2,1,0:T(8,128)(2,1)S(1)} %copy.105, bf16[64,4,1,8,128]{4,3,2,1,0:T(8,128)(2,1)S(1)} %copy.103, f32[2,8,128]{2,1,0:T(8,128)S(1)} %get-tuple-element.37, ...), kind=kLoop, calls=%fused_computation.13 | loop fusion | flops 6291456 | bytes 6307968 | tf_op jit(solution)/shard_map/convert_element_type | solution.py:57
  50.9 2.5 %stack.28 = bf16[1,64,8192]{2,1,0:T(8,128)(2,1)} reshape(bf16[64,4,2,8,128]{4,3,2,1,0:T(8,128)(2,1)} %get-tuple-element.17) | data formatting | bytes 2097152 | tf_op jit(solution)/shard_map/stack | solution.py:86
  53.4 1.3 stack.30
  54.6 1.3 multiply_convert_fusion
  55.9 0.7 copy.107
  56.6 1.3 stack.29
  57.9 52.2 %all-gather.2.cloned.1.call-done = bf16[256,4,2,8,128]{4,3,2,1,0:T(8,128)(2,1)} async-done(((bf16[64,4,2,8,128]{4,3,2,1,0:T(8,128)(2,1)}), bf16[256,4,2,8,128]{4,3,2,1,0:T(8,128)(2,1)}) %all-gather.2.cloned.1.call-update) | async-done | bytes 4194320 | tf_op jit(solution)/shard_map/all_gather | solution.py:87
  110.2 7.3 %reshape.116 = bf16[2,128,8192,1]{2,1,0,3:T(8,128)(2,1)} reshape(bf16[256,4,2,8,128]{4,3,2,1,0:T(8,128)(2,1)} %all-gather.2.cloned.1.call-done) | data formatting | bytes 8388608 | tf_op jit(solution)/shard_map/qjk,ik->qji/dot_general | solution.py:90
  117.5 3.8 %fusion.10 = bf16[2,4,64,128]{3,2,0,1:T(8,128)(2,1)S(1)} fusion(bf16[2,128,8192,1]{2,1,0,3:T(8,128)(2,1)} %reshape.116, bf16[1,64,8192]{2,1,0:T(8,128)(2,1)S(1)} %copy-done.4, bf16[1,64,8192]{2,1,0:T(8,128)(2,1)S(1)} %copy-done.6, bf16[1,64,8192]{2,1,0:T(8,128)(2,1)} %stack.29, bf16[1,64,8192]{2,1,0:T(8,128)(2,1)S(1)} %copy-done.5), kind=kOutput, calls=%fused_computation.15 | convolution fusion | flops 1090584576 | bytes 8519680 | tf_op jit(solution)/shard_map/qjk,ik->qji/dot_general | solution.py:90
  121.3 38.4 %all_to_all.10 = bf16[128,4,128]{2,1,0:T(4,128)(2,1)S(1)} all-to-all(bf16[128,4,128]{2,1,0:T(4,128)(2,1)S(1)} %bitcast.168), channel_id=1, replica_groups=mesh['gx'=8,'gy'=16,'ma'=4] {'gx','gy'}, dimensions={0} | all-to-all | bytes 262144 | tf_op jit(solution)/shard_map/all_to_all | solution.py:70
  159.9 20.7 %all_to_all.11 = bf16[128,4,128]{2,1,0:T(4,128)(2,1)S(1)} all-to-all(bf16[128,4,128]{2,1,0:T(4,128)(2,1)S(1)} %broadcast_in_dim.160), channel_id=1, replica_groups=mesh['gx'=8,'gy'=16,'ma'=4] {'gx','gy'}, dimensions={0} | all-to-all | bytes 262144 | tf_op jit(solution)/shard_map/all_to_all | solution.py:73
  180.6 0.7 copy_bitcast_fusion
  (45 shorter events, 1.8 us)
Async XLA Ops:
  6.5 103.6 %all-gather.2.cloned.1.call-start = ((), (), s32[]{:S(2)}) async-start(), calls=%async_computation.2 | async-start | bytes 5242880 | tf_op jit(solution)/shard_map/all_gather | solution.py:87
  7.3 9.4 %copy-start = (bf16[64,4,2,8,128]{4,3,2,1,0:T(8,128)(2,1)S(1)}, bf16[64,4,2,8,128]{4,3,2,1,0:T(8,128)(2,1)}, u32[]{:S(2)}) copy-start(bf16[64,4,2,8,128]{4,3,2,1,0:T(8,128)(2,1)} %param.5) | copy-start | bytes 3145732
  9.6 23.2 %collective-permute-start.1 = (bf16[64,4,1,8,128]{4,0,3,2,1:T(8,128)(2,1)}, bf16[64,4,1,8,128]{4,0,3,2,1:T(8,128)(2,1)}, u32[]{:S(2)}, u32[]{:S(2)}) collective-permute-start(bf16[64,4,1,8,128]{4,0,3,2,1:T(8,128)(2,1)} %copy.127), channel_id=1, source_target_pairs={{0,64},{64,128},{128,192},{192,256},{256,320},{320,384},{384,448},... | collective-permute-start | bytes 1572872 | tf_op jit(solution)/shard_map/ppermute | solution.py:17
  15.4 19.3 %collective-permute-start = (bf16[64,4,1,8,128]{4,0,3,2,1:T(8,128)(2,1)}, bf16[64,4,1,8,128]{4,0,3,2,1:T(8,128)(2,1)}, u32[]{:S(2)}, u32[]{:S(2)}) collective-permute-start(bf16[64,4,1,8,128]{4,0,3,2,1:T(8,128)(2,1)} %copy.128), channel_id=1, source_target_pairs={{64,0},{128,64},{192,128},{256,192},{320,256},{384,320},{448,384},... | collective-permute-start | bytes 1572872 | tf_op jit(solution)/shard_map/ppermute | solution.py:19
  16.9 3.0 %copy-start.9 = (f32[8,4,4]{0,2,1:T(4,128)S(1)}, f32[8,4,4]{0,2,1:T(4,128)}, u32[]{:S(2)}) copy-start(f32[8,4,4]{0,2,1:T(4,128)} %param.9) | copy-start | bytes 1540
  17.0 3.2 %copy-start.8 = (s32[2,8,128]{2,1,0:T(8,128)S(1)}, s32[2,8,128]{2,1,0:T(8,128)}, u32[]{:S(2)}) copy-start(s32[2,8,128]{2,1,0:T(8,128)} %param.7) | copy-start | bytes 24580
  21.2 1.7 copy-start.10
  28.1 4.7 %copy-start.7 = (f32[3,2,8,128]{3,2,1,0:T(8,128)S(1)}, f32[3,2,8,128]{3,2,1,0:T(8,128)}, u32[]{:S(2)}) copy-start(f32[3,2,8,128]{3,2,1,0:T(8,128)} %param.6) | copy-start | bytes 73732
  35.9 1.3 copy-start.1
  38.0 16.6 %collective-permute-start.2 = (bf16[64,4,4,1,128]{4,0,3,2,1:T(8,128)(2,1)}, bf16[64,4,4,1,128]{4,0,3,2,1:T(8,128)(2,1)S(1)}, u32[]{:S(2)}, u32[]{:S(2)}) collective-permute-start(bf16[64,4,4,1,128]{4,0,3,2,1:T(8,128)(2,1)} %get-tuple-element.13), channel_id=1, source_target_pairs={{4,0},{8,4},{12,8},{16,12},{20,16},{24,20},{28,24},{32,28},{36,32}... | collective-permute-start | bytes 786440 | tf_op jit(solution)/shard_map/ppermute | solution.py:19
  44.0 10.6 %collective-permute-start.3 = (bf16[64,4,4,1,128]{4,0,3,2,1:T(8,128)(2,1)}, bf16[64,4,4,1,128]{4,0,3,2,1:T(8,128)(2,1)}, u32[]{:S(2)}, u32[]{:S(2)}) collective-permute-start(bf16[64,4,4,1,128]{4,0,3,2,1:T(8,128)(2,1)} %get-tuple-element.14), channel_id=1, source_target_pairs={{0,4},{4,8},{8,12},{12,16},{16,20},{20,24},{24,28},{28,32},{32,36}... | collective-permute-start | bytes 786440 | tf_op jit(solution)/shard_map/ppermute | solution.py:17
  50.8 2.5 %copy-start.3 = (bf16[64,4,2,8,128]{4,3,2,1,0:T(8,128)(2,1)S(1)}, bf16[64,4,2,8,128]{4,3,2,1,0:T(8,128)(2,1)}, u32[]{:S(2)}) copy-start(bf16[64,4,2,8,128]{4,3,2,1,0:T(8,128)(2,1)} %get-tuple-element.18) | copy-start | bytes 3145732
  50.9 3.8 %copy-start.2 = (bf16[64,4,4,8,128]{4,0,3,2,1:T(8,128)(2,1)S(1)}, bf16[64,4,4,8,128]{4,0,3,2,1:T(8,128)(2,1)}, u32[]{:S(2)}) copy-start(bf16[64,4,4,8,128]{4,0,3,2,1:T(8,128)(2,1)} %copy-done.1) | copy-start | bytes 6291460
  57.9 59.6 %copy-start.4 = (bf16[1,64,8192]{2,1,0:T(8,128)(2,1)S(1)}, bf16[1,64,8192]{2,1,0:T(8,128)(2,1)}, u32[]{:S(2)}) copy-start(bf16[1,64,8192]{2,1,0:T(8,128)(2,1)} %convert_element_type.84) | copy-start | bytes 3145732
  57.9 59.6 %copy-start.5 = (bf16[1,64,8192]{2,1,0:T(8,128)(2,1)S(1)}, bf16[1,64,8192]{2,1,0:T(8,128)(2,1)}, u32[]{:S(2)}) copy-start(bf16[1,64,8192]{2,1,0:T(8,128)(2,1)} %stack.28) | copy-start | bytes 3145732
  57.9 59.6 %copy-start.6 = (bf16[1,64,8192]{2,1,0:T(8,128)(2,1)S(1)}, bf16[1,64,8192]{2,1,0:T(8,128)(2,1)}, u32[]{:S(2)}) copy-start(bf16[1,64,8192]{2,1,0:T(8,128)(2,1)} %stack.30) | copy-start | bytes 3145732
Sparse Core Ops, SparseCore 0:
  9.5 100.6 all-gather.1

commit v2 on v0

v2 whole, which is shorter than its diff:
```python
import math

import jax
import jax.numpy as jnp
from jax import lax
from jax.experimental import pallas as pl
from jax.experimental.pallas import tpu as pltpu
from jax.sharding import Mesh, PartitionSpec as P

LANES = 128
BF16 = jnp.bfloat16
F32 = jnp.float32
CONTRACT_LAST = (((1,), (1,)), ((), ()))


def shift(cells, axis, step, count):
    return lax.ppermute(cells, axis, [(i, (i + step) % count) for i in range(count)])


def by_pair(cells, swap):
    return jnp.where(swap, cells[::-1], cells)


def local_kernel(table, partner, cells, a, out, modes, z_image, c_image):
    pairs, fields, block = a.shape[0] // 4, a.shape[2], a.shape[3]
    planes = lax.broadcasted_iota(jnp.int32, (LANES, LANES), 0)
    pick = (planes == partner[...]).astype(F32).astype(BF16)
    speed_z, region = cells[0], cells[1]
    coupling = {}
    for f in range(fields):
        for g in range(fields):
            if f != g:
                chosen = jnp.zeros_like(region)
                for number in range(table.shape[0]):
                    chosen = jnp.where(region == float(number), table[number, f * fields + g], chosen)
                coupling[f, g] = chosen
    for p in range(pairs):
        for xi in range(2):
            col = 2 * p + xi
            for j in range(4):
                rows = slice(j * block, (j + 1) * block)
                here = [a[4 * p + j, xi, f] for f in range(fields)]
                moved = jnp.dot(jnp.concatenate(here, axis=0), pick, preferred_element_type=F32)
                centre = [cells_f.astype(F32) for cells_f in here]
                for f in range(fields):
                    chunk = slice((col * fields + f) * LANES, (col * fields + f + 1) * LANES)
                    modes[rows, chunk] = here[f]
                    jump = speed_z[col : col + 1] * (moved[f * block : (f + 1) * block] - centre[f])
                    z_image[rows, chunk] = jump.astype(BF16)
                    running = None
                    for g in range(fields):
                        if g != f:
                            term = coupling[f, g][col : col + 1] * centre[g]
                            running = term if running is None else running + term
                    c_image[rows, chunk] = running.astype(BF16)
    for q, image in enumerate((z_image, c_image)):
        total = lax.dot_general(image[...], modes[...], CONTRACT_LAST, preferred_element_type=F32)
        place(out, q, total, block)


def place(out, q, total, block):
    for j in range(4):
        for half in range(2):
            start = (2 * q + half) * block
            piece = total[j * block : (j + 1) * block, half * LANES : (half + 1) * LANES]
            out[j, start : start + block, :] = piece.astype(BF16)


def edge_kernel(coef, modes, xr, xl, yr, yl, zc, out, x_image, x_edge, x_side, y_image, y_edge, y_side):
    pairs, block = xr.shape[0] // 4, xr.shape[2]
    fields = 2 * xr.shape[1]

    def weight(row):
        return coef[row : row + 1, :]

    for p in range(pairs):
        for j in range(4):
            rows = slice(j * block, (j + 1) * block)
            for f in range(fields):
                def lane_chunk(index):
                    return slice(index * LANES, (index + 1) * LANES)

                first, second = (lane_chunk((2 * p + xi) * fields + f) for xi in range(2))
                side = lane_chunk(p * fields + f)
                m0 = modes[rows, first].astype(F32)
                m1 = modes[rows, second].astype(F32)
                half = f % 2
                to_second = weight(2 * p) * m1
                to_first = -weight(2 * p + 1) * m0
                if f < 2:
                    beside = xr[4 * p + j, half]
                    to_first = weight(4 + p) * beside.astype(F32) + to_first
                    edge = weight(6 + p) * m1
                else:
                    beside = xl[4 * p + j, half]
                    to_second = to_second - weight(8 + p) * beside.astype(F32)
                    edge = weight(10 + p) * m0
                x_image[rows, first] = to_second.astype(BF16)
                x_image[rows, second] = to_first.astype(BF16)
                x_edge[rows, side] = edge.astype(BF16)
                x_side[rows, side] = beside
                for xi, chunk, centre in ((0, first, m0), (1, second, m1)):
                    col = 2 * p + xi
                    next_to = yr[4 * p + j, xi, half] if f < 2 else yl[4 * p + j, xi, half]
                    base = 12 if f < 2 else 20
                    y_image[rows, chunk] = (weight(base + col) * next_to.astype(F32)).astype(BF16)
                    y_edge[rows, chunk] = (weight(base + 4 + col) * centre).astype(BF16)
                    y_side[rows, chunk] = next_to
    for q, (image, edge, side) in enumerate(((x_image, x_edge, x_side), (y_image, y_edge, y_side))):
        total = lax.dot_general(image[...], modes[...], CONTRACT_LAST, preferred_element_type=F32)
        total += lax.dot_general(edge[...], side[...], CONTRACT_LAST, preferred_element_type=F32)
        place(out, q, total, block)
    out[:, 4 * block :, :] = zc[...]


def on_device(pod_modes, velocity, region, partner, coupling_table):
    block, fields, cells_x, cells_y, planes = pod_modes.shape
    zh_count, x_count, gy_count, ma_count = (lax.axis_size(name) for name in ("zh", "x", "gy", "ma"))
    cell_total = fields * cells_x * zh_count * x_count * cells_y * gy_count * planes
    scaling = 1.0 / math.sqrt(cell_total)
    zh, x, gy, ma = (lax.axis_index(name) for name in ("zh", "x", "gy", "ma"))
    row = zh * ma_count + ma
    kinds = block * ma_count

    pieces = jnp.transpose(pod_modes, (3, 2, 1, 0, 4))
    a = lax.all_to_all(pieces, ("zh", "ma"), 0, 0)

    own = jnp.concatenate([velocity, region.astype(F32)[None]])
    other = shift(own, "zh", 1, zh_count)
    cells = jnp.stack([jnp.where(zh == 0, own, other), jnp.where(zh == 0, other, own)], axis=1)
    vx_right = shift(by_pair(cells[0, :, 0], x == 0), "x", -1, x_count)
    vx_left = shift(by_pair(cells[0, :, 1], x == x_count - 1), "x", 1, x_count)
    vy_above = shift(cells[1, :, :, :1], "gy", -1, gy_count)
    vy_below = shift(cells[1, :, :, -1:], "gy", 1, gy_count)
    vy = jnp.concatenate([vy_below, cells[1], vy_above], axis=2).reshape(4, cells_y + 2, planes)
    at_row = lax.dynamic_index_in_dim(cells, row, 3, keepdims=False).reshape(4, 4, planes)
    vx_right = lax.dynamic_index_in_dim(vx_right, row, 1, keepdims=False)
    vx_left = lax.dynamic_index_in_dim(vx_left, row, 1, keepdims=False)
    vy_down, vy_here, vy_up = (lax.dynamic_index_in_dim(vy, row + k, 1, keepdims=False) for k in range(3))
    right = jnp.stack([jnp.ones((), F32), jnp.where(x == x_count - 1, 0.0, 1.0)])[:, None]
    left = jnp.stack([jnp.where(x == 0, 0.0, 1.0), jnp.ones((), F32)])[:, None]
    up = jnp.where((gy == gy_count - 1) & (row == cells_y - 1), 0.0, 1.0)
    down = jnp.where((gy == 0) & (row == 0), 0.0, 1.0)
    vx = at_row[0]
    coef = 0.5 * jnp.concatenate(
        [
            vx,
            vx[1::2] * right,
            -vx_right * right,
            vx[0::2] * left,
            vx_left * left,
            vy_here * up,
            -vy_up * up,
            -vy_here * down,
            vy_down * down,
            jnp.zeros((4, planes), F32),
        ]
    )

    vmem = pl.BlockSpec(memory_space=pltpu.VMEM)
    smem = pl.BlockSpec(memory_space=pltpu.SMEM)
    width = 4 * fields * planes
    wide = pltpu.VMEM((kinds, width), BF16)
    narrow = pltpu.VMEM((kinds, width // 2), BF16)
    zc, modes = pl.pallas_call(
        local_kernel,
        out_shape=(
            jax.ShapeDtypeStruct((ma_count, 4 * block, LANES), BF16),
            jax.ShapeDtypeStruct((kinds, width), BF16),
        ),
        in_specs=[smem, vmem, vmem, vmem],
        out_specs=(vmem, vmem),
        scratch_shapes=[wide, wide],
        compiler_params=pltpu.CompilerParams(vmem_limit_bytes=40 * 2**20),
        cost_estimate=pl.CostEstimate(flops=2 * 2 * kinds * kinds * width, bytes_accessed=4 * 2**20, transcendentals=0),
    )(coupling_table.reshape(-1, fields * fields), partner[None], at_row[2:4], a)

    def pair_swapped(part, swap):
        return by_pair(part.reshape((2, ma_count) + part.shape[1:]), swap).reshape(part.shape)

    def number(grid_row):
        grid_row = grid_row % (gy_count * zh_count * ma_count)
        outer, inner = divmod(grid_row, zh_count * ma_count)
        return (inner // ma_count * gy_count + outer) * ma_count + inner % ma_count

    def row_shift(part, step):
        pairs = [(number(i), number(i + step)) for i in range(gy_count * zh_count * ma_count)]
        return lax.ppermute(part, ("zh", "gy", "ma"), pairs)

    xr = shift(pair_swapped(a[:, 0, :2], x == 0), "x", -1, x_count)
    yr = row_shift(a[:, :, :2], -1)
    xl = shift(pair_swapped(a[:, 1, 2:], x == x_count - 1), "x", 1, x_count)
    yl = row_shift(a[:, :, 2:], 1)

    partial_sums = pl.pallas_call(
        edge_kernel,
        out_shape=jax.ShapeDtypeStruct((ma_count, 8 * block, LANES), BF16),
        in_specs=[vmem] * 7,
        out_specs=vmem,
        scratch_shapes=[wide, narrow, narrow, wide, wide, wide],
        compiler_params=pltpu.CompilerParams(vmem_limit_bytes=40 * 2**20),
        cost_estimate=pl.CostEstimate(flops=2 * 4 * kinds * kinds * width, bytes_accessed=6 * 2**20, transcendentals=0),
    )(coef, modes, xr, xl, yr, yl, zc)

    shares = zh_count * x_count * gy_count
    received = lax.all_to_all(partial_sums.reshape(ma_count * shares, -1, LANES), ("ma", "zh", "x", "gy"), 0, 0)
    share = jnp.sum(received.astype(F32), axis=0) * scaling
    spread = jnp.broadcast_to(share[None], (shares,) + share.shape)
    whole = lax.all_to_all(spread, ("zh", "x", "gy"), 0, 0)
    whole = whole.reshape(4, kinds // LANES, block, LANES).transpose(0, 1, 3, 2)
    return whole.reshape(4, kinds, block)


def solution(mesh):
    gx, gy, ma = (mesh.shape[name] for name in ("gx", "gy", "ma"))
    split = Mesh(mesh.devices.reshape(2, gx // 2, gy, ma), ("zh", "x", "gy", "ma"))
    placed = (
        P("ma", None, ("zh", "x"), "gy", None),
        P(None, ("zh", "x"), "gy", None),
        P(("zh", "x"), "gy", None),
        P(),
        P(),
    )
    return jax.shard_map(
        on_device, mesh=split, in_specs=placed, out_specs=P(None, None, "ma"), check_vma=False
    )
```

time: 1560 us -> 132 us (0.08)
  waiting for transfers between devices: 1490 us -> 22.9 us
  blocking collectives: 0 us -> 59.1 us
  starting transfers between devices: 15.5 us -> 36.3 us
  local copies, waits for them, and re-layouts: 21.7 us -> 5.95 us
    psum x1 -> x0, waiting for transfers between devices: 1430 us -> none  [on_device(): summed = lax.psum(partial_sums, ('gx', 'gy'))]
    all_to_all x0 -> x2, blocking collectives: none -> 59.1 us  [the longest x1 35.1 us: on_device(): lax.all_to_all(partial_sums.reshape(ma_count * shares, -1, LANES), ('ma',...]
    all_gather x1 -> x0, waiting for transfers between devices: 51.8 us -> none  [on_device(): portion = lax.all_gather(pod_modes, 'ma', axis=0, tiled=True)]
    all_to_all x0 -> x1, waiting for transfers between devices: none -> 17 us  [on_device(): a = lax.all_to_all(pieces, ('zh', 'ma'), 0, 0)]
    ppermute x4 -> x9, starting transfers between devices: 15.4 us -> 32 us  [the longest x7 26.7 us: shift(): lax.ppermute(cells, axis, [(i, (i + step) % count) for i in range(count)])]
  transfers between devices with their start and end apart: 6 -> 10, of which waited for: 4 -> 4; matrix products, arithmetic and copies ran while one was open for 2% -> 3% of each run, Pallas kernels for 0% -> 2%
where the time goes in v2:
time: 132 us; the launch traced here: 131 us
  blocking collectives  59.1 us (45%)
  starting transfers between devices  36.3 us (27%)
  waiting for transfers between devices  22.9 us (17%)
  local copies, waits for them, and re-layouts  5.95 us (5%)
  Pallas kernels  4.16 us (3%)
  other arithmetic  2.52 us (2%)
    all_to_all x1, blocking collectives, on_device(): lax.all_to_all(partial_sums.reshape(ma_count * shares, -1, LANES), ('ma',...  35.1 us
    ppermute x7, starting transfers between devices, shift(): lax.ppermute(cells, axis, [(i, (i + step) % count) for i in range(count)])  26.7 us
    all_to_all x1, blocking collectives, on_device(): whole = lax.all_to_all(spread, ('zh', 'x', 'gy'), 0, 0)  24 us
    all_to_all x1, waiting for transfers between devices, on_device(): a = lax.all_to_all(pieces, ('zh', 'ma'), 0, 0)  17 us
    ppermute x7, waiting for transfers between devices, shift(): lax.ppermute(cells, axis, [(i, (i + step) % count) for i in range(count)])  5.8 us
    ppermute x2, starting transfers between devices, row_shift(): return lax.ppermute(part, ('zh', 'gy', 'ma'), pairs)  5.28 us
    unnamed x9, local copies, waits for them, and re-layouts  4.78 us
    all_to_all x1, starting transfers between devices, on_device(): a = lax.all_to_all(pieces, ('zh', 'ma'), 0, 0)  4.29 us
  transfers between devices with their start and end apart: 10, of which 4 were waited for; matrix products, arithmetic and copies ran while one was open for 3% of the time, Pallas kernels for 2%

profile of v2, /device:TPU:1, one launch (start us, length us, event | category | flops | bytes accessed | tf_op | source)
XLA Modules:
  0.0 131.2 jit_solution(143417870284873019)
XLA Ops:
  0.0 0.7 convert_bitcast_fusion
  0.7 0.7 pad_maximum_fusion
  1.4 11.5 %collective-permute-start = (f32[4,2,8,128]{3,2,1,0:T(8,128)S(1)}, f32[4,2,8,128]{3,2,1,0:T(8,128)S(1)}, u32[]{:S(2)}, u32[]{:S(2)}) collective-permute-start(f32[4,2,8,128]{3,2,1,0:T(8,128)S(1)} %pad_maximum_fusion), channel_id=1, source_target_pairs={{0,256},{256,0},{1,257},{257,1},{2,258},{258,2},{3,259},{259,3},{4... | collective-permute-start | bytes 98312 | tf_op jit(solution)/shard_map/ppermute | solution.py:17
  12.9 2.9 %copy.33 = bf16[64,4,2,8,128]{4,0,1,2,3:T(8,128)(2,1)} copy(bf16[64,4,2,8,128]{4,3,2,1,0:T(8,128)(2,1)} %param.5) | data formatting | bytes 2097152 | tf_op args[0]
  15.8 4.3 %all-to-all-start = ((bf16[8,2,4,64,128]{4,3,2,1,0:T(8,128)(2,1)}), bf16[8,2,4,64,128]{4,3,2,1,0:T(8,128)(2,1)S(1)}, u32[]{:S(2)}, u32[]{:S(2)}) async-start(bf16[8,2,4,64,128]{4,3,2,1,0:T(8,128)(2,1)} %bitcast.52), calls=%async_computation | async-start | bytes 2097152 | tf_op jit(solution)/shard_map/all_to_all | solution.py:126
  20.1 0.1 pad_maximum_fusion.4
  20.2 0.1 pad_maximum_fusion.3
  20.2 0.7 copy-done.3
  20.9 0.1 copy.28.table
  21.1 0.5 copy-done.2
  21.7 2.4 %collective-permute-start.3 = (f32[2,2,1,128]{3,0,1,2:T(2,128)S(1)}, f32[2,2,1,128]{3,0,1,2:T(2,128)S(1)}, u32[]{:S(2)}, u32[]{:S(2)}) collective-permute-start(f32[2,2,1,128]{3,0,1,2:T(2,128)S(1)} %get-tuple-element.13), channel_id=1, source_target_pairs={{0,4},{4,8},{8,12},{12,16},{16,20},{20,24},{24,28},{28,32},{32,36}... | collective-permute-start | bytes 6152 | tf_op jit(solution)/shard_map/ppermute | solution.py:17
  24.2 3.1 %collective-permute-start.2 = (f32[2,8,128]{2,0,1:T(2,128)S(1)}, f32[2,8,128]{2,0,1:T(2,128)S(1)}, u32[]{:S(2)}, u32[]{:S(2)}) collective-permute-start(f32[2,8,128]{2,0,1:T(2,128)S(1)} %bitcast.85), channel_id=1, source_target_pairs={{0,64},{64,128},{128,192},{192,0},{1,65},{65,129},{129,193},{193,1... | collective-permute-start | bytes 24584 | tf_op jit(solution)/shard_map/ppermute | solution.py:17
  27.4 3.4 %collective-permute-start.1 = (f32[2,8,128]{2,0,1:T(2,128)S(1)}, f32[2,8,128]{2,0,1:T(2,128)S(1)}, u32[]{:S(2)}, u32[]{:S(2)}) collective-permute-start(f32[2,8,128]{2,0,1:T(2,128)S(1)} %bitcast.84), channel_id=1, source_target_pairs={{0,192},{64,0},{128,64},{192,128},{1,193},{65,1},{129,65},{193,129... | collective-permute-start | bytes 24584 | tf_op jit(solution)/shard_map/ppermute | solution.py:17
  30.9 0.1 fusion.13
  31.0 1.1 collective-permute-done.1
  32.1 0.1 fusion.11
  32.2 0.1 concatenate.21
  32.2 17.0 %all-to-all-done.a = bf16[8,2,4,64,128]{4,3,2,1,0:T(8,128)(2,1)S(1)} async-done(((bf16[8,2,4,64,128]{4,3,2,1,0:T(8,128)(2,1)}), bf16[8,2,4,64,128]{4,3,2,1,0:T(8,128)(2,1)S(1)}, u32[]{:S(2)}, u32[]{:S(2)}) %all-to-all-start) | async-done | bytes 1048608 | tf_op jit(solution)/shard_map/all_to_all | solution.py:126
  49.3 0.1 fusion.14
  49.4 1.9 %collective-permute-start.7 = (bf16[8,2,2,64,128]{4,3,2,1,0:T(8,128)(2,1)S(1)}, bf16[8,2,2,64,128]{4,3,2,1,0:T(8,128)(2,1)S(1)}, u32[]{:S(2)}, u32[]{:S(2)}) collective-permute-start(bf16[8,2,2,64,128]{4,3,2,1,0:T(8,128)(2,1)S(1)} %get-tuple-element.10), channel_id=1, source_target_pairs={{0,319},{1,0},{2,1},{3,2},{256,3},{257,256},{258,257},{259,258},{4... | collective-permute-start | bytes 1572872 | tf_op jit(solution)/shard_map/ppermute | solution.py:188
  51.3 3.4 %collective-permute-start.8 = (bf16[8,2,2,64,128]{4,3,2,1,0:T(8,128)(2,1)S(1)}, bf16[8,2,2,64,128]{4,3,2,1,0:T(8,128)(2,1)S(1)}, u32[]{:S(2)}, u32[]{:S(2)}) collective-permute-start(bf16[8,2,2,64,128]{4,3,2,1,0:T(8,128)(2,1)S(1)} %get-tuple-element.9), channel_id=1, source_target_pairs={{0,1},{1,2},{2,3},{3,256},{256,257},{257,258},{258,259},{259,4},{4... | collective-permute-start | bytes 1572872 | tf_op jit(solution)/shard_map/ppermute | solution.py:188
  54.8 4.4 %collective-permute-start.5 = (bf16[8,2,64,128]{3,2,1,0:T(8,128)(2,1)S(1)}, bf16[8,2,64,128]{3,2,1,0:T(8,128)(2,1)S(1)}, u32[]{:S(2)}, u32[]{:S(2)}) collective-permute-start(bf16[8,2,64,128]{3,2,1,0:T(8,128)(2,1)S(1)} %bitcast.74), channel_id=1, source_target_pairs={{0,192},{64,0},{128,64},{192,128},{1,193},{65,1},{129,65},{193,129... | collective-permute-start | bytes 786440 | tf_op jit(solution)/shard_map/ppermute | solution.py:17
  59.2 1.9 %collective-permute-start.6 = (bf16[8,2,64,128]{3,2,1,0:T(8,128)(2,1)S(1)}, bf16[8,2,64,128]{3,2,1,0:T(8,128)(2,1)S(1)}, u32[]{:S(2)}, u32[]{:S(2)}) collective-permute-start(bf16[8,2,64,128]{3,2,1,0:T(8,128)(2,1)S(1)} %bitcast.75), channel_id=1, source_target_pairs={{0,64},{64,128},{128,192},{192,0},{1,65},{65,129},{129,193},{193,1... | collective-permute-start | bytes 786440 | tf_op jit(solution)/shard_map/ppermute | solution.py:17
  61.2 0.6 copy-done
  61.8 2.3 %shard_map.55 = (bf16[4,256,128]{2,1,0:T(8,128)(2,1)S(1)}, bf16[256,2048]{1,0:T(8,128)(2,1)S(1)}) custom-call(f32[8,16]{1,0:T(8,128)S(1)} %copy.28.table, s32[1,128]{1,0:T(1,128)S(1)} %bitcast.62, f32[2,4,128]{2,1,0:T(4,128)S(1)} %bitcast.61, bf16[8,2,4,64,128]{4,3,2,1,0:T(8,128)(2,1)S(1)} %all-to-all-done.a), custom_call_target="tpu_custom_call" | custom-call | flops 536870912 | bytes 4194304 | tf_op jit(solution)/shard_map/pallas_call | solution.py:165
  64.2 4.7 %collective-permute-done.6.xl = bf16[8,2,64,128]{3,2,1,0:T(8,128)(2,1)S(1)} collective-permute-done((bf16[8,2,64,128]{3,2,1,0:T(8,128)(2,1)S(1)}, bf16[8,2,64,128]{3,2,1,0:T(8,128)(2,1)S(1)}, u32[]{:S(2)}, u32[]{:S(2)}) %collective-permute-start.6) | collective-permute-done | bytes 262176 | tf_op jit(solution)/shard_map/ppermute | solution.py:17
  68.8 0.1 collective-permute-done.8.yl
  68.9 1.9 %shard_map.56 = bf16[4,512,128]{2,1,0:T(8,128)(2,1)S(1)} custom-call(f32[32,128]{1,0:T(8,128)S(1)} %broadcast_multiply_fusion.coef, bf16[256,2048]{1,0:T(8,128)(2,1)S(1)} %get-tuple-element.7.modes, bf16[8,2,64,128]{3,2,1,0:T(8,128)(2,1)S(1)} %collective-permute-done.5.xr, bf16[8,2,64,128]{3,2,1,0:T(8,128)(2,1)S(1)} %collective-permute-done.6.xl, ...), custom_call_target="tpu_custom_call" | custom-call | flops 1073741824 | bytes 6291456 | tf_op jit(solution)/shard_map/pallas_call | solution.py:195
  70.8 35.1 %all_to_all.15 = bf16[512,4,128]{2,1,0:T(4,128)(2,1)S(1)} all-to-all(bf16[512,4,128]{2,1,0:T(4,128)(2,1)S(1)} %bitcast.60), channel_id=1, replica_groups=mesh['zh'=2,'x'=4,'gy'=16,'ma'=4] {'ma','zh','x','gy'}, dimensions={0} | all-to-all | bytes 1048576 | tf_op jit(solution)/shard_map/all_to_all | solution.py:206
  105.9 0.5 convert_reduce_fusion
  106.5 24.0 %all_to_all.16 = f32[128,4,128]{2,1,0:T(4,128)S(1)} all-to-all(f32[128,4,128]{2,1,0:T(4,128)S(1)} %broadcast_in_dim.20), channel_id=1, replica_groups=mesh['zh'=2,'x'=4,'gy'=16,'ma'=4] {'zh','x','gy'}, dimensions={0} | all-to-all | bytes 524288 | tf_op jit(solution)/shard_map/all_to_all | solution.py:209
  130.5 0.7 copy.34
  (40 shorter events, 0.5 us)
Async XLA Ops:
  1.4 19.6 %collective-permute-start = (f32[4,2,8,128]{3,2,1,0:T(8,128)S(1)}, f32[4,2,8,128]{3,2,1,0:T(8,128)S(1)}, u32[]{:S(2)}, u32[]{:S(2)}) collective-permute-start(f32[4,2,8,128]{3,2,1,0:T(8,128)S(1)} %pad_maximum_fusion), channel_id=1, source_target_pairs={{0,256},{256,0},{1,257},{257,1},{2,258},{258,2},{3,259},{259,3},{4... | collective-permute-start | bytes 98312 | tf_op jit(solution)/shard_map/ppermute | solution.py:17
  15.8 33.5 %all-to-all-start = ((bf16[8,2,4,64,128]{4,3,2,1,0:T(8,128)(2,1)}), bf16[8,2,4,64,128]{4,3,2,1,0:T(8,128)(2,1)S(1)}, u32[]{:S(2)}, u32[]{:S(2)}) async-start(bf16[8,2,4,64,128]{4,3,2,1,0:T(8,128)(2,1)} %bitcast.52), calls=%async_computation | async-start | bytes 2097152 | tf_op jit(solution)/shard_map/all_to_all | solution.py:126
  20.2 0.8 copy-start.1
  20.2 0.7 copy-start.3
  21.1 0.6 copy-start.2
  21.7 9.1 %collective-permute-start.3 = (f32[2,2,1,128]{3,0,1,2:T(2,128)S(1)}, f32[2,2,1,128]{3,0,1,2:T(2,128)S(1)}, u32[]{:S(2)}, u32[]{:S(2)}) collective-permute-start(f32[2,2,1,128]{3,0,1,2:T(2,128)S(1)} %get-tuple-element.13), channel_id=1, source_target_pairs={{0,4},{4,8},{8,12},{12,16},{16,20},{20,24},{24,28},{28,32},{32,36}... | collective-permute-start | bytes 6152 | tf_op jit(solution)/shard_map/ppermute | solution.py:17
  24.1 6.7 %collective-permute-start.4 = (f32[2,2,1,128]{3,0,1,2:T(2,128)S(1)}, f32[2,2,1,128]{3,0,1,2:T(2,128)S(1)}, u32[]{:S(2)}, u32[]{:S(2)}) collective-permute-start(f32[2,2,1,128]{3,0,1,2:T(2,128)S(1)} %get-tuple-element.14), channel_id=1, source_target_pairs={{0,60},{4,0},{8,4},{12,8},{16,12},{20,16},{24,20},{28,24},{32,28},... | collective-permute-start | bytes 6152 | tf_op jit(solution)/shard_map/ppermute | solution.py:17
  24.2 6.7 %collective-permute-start.2 = (f32[2,8,128]{2,0,1:T(2,128)S(1)}, f32[2,8,128]{2,0,1:T(2,128)S(1)}, u32[]{:S(2)}, u32[]{:S(2)}) collective-permute-start(f32[2,8,128]{2,0,1:T(2,128)S(1)} %bitcast.85), channel_id=1, source_target_pairs={{0,64},{64,128},{128,192},{192,0},{1,65},{65,129},{129,193},{193,1... | collective-permute-start | bytes 24584 | tf_op jit(solution)/shard_map/ppermute | solution.py:17
  27.4 3.4 %slice-start = ((f32[4,2,2,1,128]{4,1,3,2,0:T(2,128)}), f32[2,2,2,1,128]{4,1,3,2,0:T(2,128)S(1)}, s32[]{:S(2)}) async-start(f32[4,2,2,1,128]{4,1,3,2,0:T(2,128)} %copy-done.2), calls=%async_computation.3 | async-start | bytes 8192 | tf_op jit(solution)/shard_map/slice | solution.py:176
  27.4 4.7 %collective-permute-start.1 = (f32[2,8,128]{2,0,1:T(2,128)S(1)}, f32[2,8,128]{2,0,1:T(2,128)S(1)}, u32[]{:S(2)}, u32[]{:S(2)}) collective-permute-start(f32[2,8,128]{2,0,1:T(2,128)S(1)} %bitcast.84), channel_id=1, source_target_pairs={{0,192},{64,0},{128,64},{192,128},{1,193},{65,1},{129,65},{193,129... | collective-permute-start | bytes 24584 | tf_op jit(solution)/shard_map/ppermute | solution.py:17
  49.4 19.5 %collective-permute-start.7 = (bf16[8,2,2,64,128]{4,3,2,1,0:T(8,128)(2,1)S(1)}, bf16[8,2,2,64,128]{4,3,2,1,0:T(8,128)(2,1)S(1)}, u32[]{:S(2)}, u32[]{:S(2)}) collective-permute-start(bf16[8,2,2,64,128]{4,3,2,1,0:T(8,128)(2,1)S(1)} %get-tuple-element.10), channel_id=1, source_target_pairs={{0,319},{1,0},{2,1},{3,2},{256,3},{257,256},{258,257},{259,258},{4... | collective-permute-start | bytes 1572872 | tf_op jit(solution)/shard_map/ppermute | solution.py:188
  51.3 17.6 %collective-permute-start.8 = (bf16[8,2,2,64,128]{4,3,2,1,0:T(8,128)(2,1)S(1)}, bf16[8,2,2,64,128]{4,3,2,1,0:T(8,128)(2,1)S(1)}, u32[]{:S(2)}, u32[]{:S(2)}) collective-permute-start(bf16[8,2,2,64,128]{4,3,2,1,0:T(8,128)(2,1)S(1)} %get-tuple-element.9), channel_id=1, source_target_pairs={{0,1},{1,2},{2,3},{3,256},{256,257},{257,258},{258,259},{259,4},{4... | collective-permute-start | bytes 1572872 | tf_op jit(solution)/shard_map/ppermute | solution.py:188
  54.8 9.4 %collective-permute-start.5 = (bf16[8,2,64,128]{3,2,1,0:T(8,128)(2,1)S(1)}, bf16[8,2,64,128]{3,2,1,0:T(8,128)(2,1)S(1)}, u32[]{:S(2)}, u32[]{:S(2)}) collective-permute-start(bf16[8,2,64,128]{3,2,1,0:T(8,128)(2,1)S(1)} %bitcast.74), channel_id=1, source_target_pairs={{0,192},{64,0},{128,64},{192,128},{1,193},{65,1},{129,65},{193,129... | collective-permute-start | bytes 786440 | tf_op jit(solution)/shard_map/ppermute | solution.py:17
  59.2 9.6 %collective-permute-start.6 = (bf16[8,2,64,128]{3,2,1,0:T(8,128)(2,1)S(1)}, bf16[8,2,64,128]{3,2,1,0:T(8,128)(2,1)S(1)}, u32[]{:S(2)}, u32[]{:S(2)}) collective-permute-start(bf16[8,2,64,128]{3,2,1,0:T(8,128)(2,1)S(1)} %bitcast.75), channel_id=1, source_target_pairs={{0,64},{64,128},{128,192},{192,0},{1,65},{65,129},{129,193},{193,1... | collective-permute-start | bytes 786440 | tf_op jit(solution)/shard_map/ppermute | solution.py:17
  61.2 0.7 copy-start

commit v3 on v0

v3 whole, which is shorter than its diff:
```python
import math

import jax
import jax.numpy as jnp
from jax import lax
from jax.experimental import pallas as pl
from jax.experimental.pallas import tpu as pltpu
from jax.sharding import Mesh, PartitionSpec as P

LANES = 128
BF16 = jnp.bfloat16
F32 = jnp.float32
CONTRACT_LAST = (((1,), (1,)), ((), ()))


def steps_along_x(shape, step):
    gx_count, y_count, core_count, ma_count = shape
    half = gx_count // 2
    pairs = []
    for gx in range(gx_count):
        to = gx + step
        if 0 <= to < gx_count:
            for ma in range(ma_count):
                to_ma = ma if gx // half == to // half else ma_count - 1 - ma
                pairs.append((gx * ma_count + ma, to * ma_count + to_ma))
    return pairs


def steps_along_y(shape, step):
    gx_count, y_count, core_count, ma_count = shape
    half = gx_count // 2
    gy_count = y_count * core_count

    def number(gx, place):
        gy, k = divmod(place, ma_count)
        ma = ma_count - 1 - k if (gx // half + gy) % 2 else k
        return (gx * gy_count + gy) * ma_count + ma

    places = gy_count * ma_count
    return [
        (number(gx, place), number(gx, place + step))
        for gx in range(gx_count)
        for place in range(places)
        if 0 <= place + step < places
    ]


def local_kernel(core, table, partner, cells, a, keep, send, modes, z_image, c_image):
    fields, block = a.shape[3], a.shape[4]
    planes = lax.broadcasted_iota(jnp.int32, (LANES, LANES), 0)
    pick = (planes == partner[...]).astype(F32).astype(BF16)
    speed_z, region = cells[0], cells[1]
    coupling = {}
    for f in range(fields):
        for g in range(fields):
            if f != g:
                chosen = jnp.zeros_like(region)
                for number in range(table.shape[0]):
                    chosen = jnp.where(region == float(number), table[number, f * fields + g], chosen)
                coupling[f, g] = chosen
    for col in range(4):
        for j in range(4):
            rows = slice(j * block, (j + 1) * block)
            here = [a[j, col // 2, col % 2, f] for f in range(fields)]
            moved = jnp.dot(jnp.concatenate(here, axis=0), pick, preferred_element_type=F32)
            centre = [cells_f.astype(F32) for cells_f in here]
            for f in range(fields):
                chunk = slice((col * fields + f) * LANES, (col * fields + f + 1) * LANES)
                modes[rows, chunk] = here[f]
                jump = speed_z[col : col + 1] * (moved[f * block : (f + 1) * block] - centre[f])
                z_image[rows, chunk] = jump.astype(BF16)
                running = None
                for g in range(fields):
                    if g != f:
                        term = coupling[f, g][col : col + 1] * centre[g]
                        running = term if running is None else running + term
                c_image[rows, chunk] = running.astype(BF16)
    for q, image in enumerate((z_image, c_image)):
        total = lax.dot_general(image[...], modes[...], CONTRACT_LAST, preferred_element_type=F32)
        place(core, keep, send, q, total, block)


def place(core, keep, send, q, total, block):
    for j in range(4):
        first = total[j * block : (j + 1) * block, :LANES]
        second = total[j * block : (j + 1) * block, LANES:]
        rows = slice(q * block, (q + 1) * block)
        keep[j, rows, :] = jnp.where(core[0] == 0, first, second)
        send[j, rows, :] = jnp.where(core[0] == 0, second, first).astype(BF16)


def edge_kernel(core, coef, modes, xr, xl, yr, yl, zc_keep, zc_send, keep, send, x_image, x_edge, x_side, y_image, y_edge, y_side):
    block, fields = xr.shape[3], 2 * xr.shape[2]

    def weight(row):
        return coef[row : row + 1, :]

    def lane_chunk(index):
        return slice(index * LANES, (index + 1) * LANES)

    axes = (
        (0, xr, xl, x_image, x_edge, x_side, lambda line, end: 2 * line + end),
        (12, yr, yl, y_image, y_edge, y_side, lambda line, end: 2 * end + line),
    )
    for j in range(4):
        rows = slice(j * block, (j + 1) * block)
        for f in range(fields):
            for base, after, before, image, edge, side, col in axes:
                for line in range(2):
                    near, far = (lane_chunk(col(line, end) * fields + f) for end in range(2))
                    extra = lane_chunk(line * fields + f)
                    m0 = modes[rows, near].astype(F32)
                    m1 = modes[rows, far].astype(F32)
                    at_near = weight(base + col(line, 0)) * m1
                    at_far = -weight(base + col(line, 1)) * m0
                    if f < 2:
                        beside = after[j, line, f]
                        at_far = weight(base + 4 + line) * beside.astype(F32) + at_far
                        at_side = weight(base + 6 + line) * m1
                    else:
                        beside = before[j, line, f - 2]
                        at_near = at_near - weight(base + 8 + line) * beside.astype(F32)
                        at_side = weight(base + 10 + line) * m0
                    image[rows, near] = at_near.astype(BF16)
                    image[rows, far] = at_far.astype(BF16)
                    edge[rows, extra] = at_side.astype(BF16)
                    side[rows, extra] = beside
    for q, (_, _, _, image, edge, side, _) in enumerate(axes):
        total = lax.dot_general(image[...], modes[...], CONTRACT_LAST, preferred_element_type=F32)
        total += lax.dot_general(edge[...], side[...], CONTRACT_LAST, preferred_element_type=F32)
        place(core, keep, send, q, total, block)
    keep[:, 2 * block :, :] = zc_keep[...]
    send[:, 2 * block :, :] = zc_send[...]


def on_device(pod_modes, velocity, region, partner, coupling_table):
    block, fields, cells_x, cells_y, planes = pod_modes.shape
    names = ("gx", "y", "core", "ma")
    shape = tuple(lax.axis_size(name) for name in names)
    gx_count, y_count, core_count, ma_count = shape
    gx, y, core, ma = (lax.axis_index(name) for name in names)
    gy_count, gy = y_count * core_count, y * core_count + core
    cell_total = fields * cells_x * gx_count * cells_y * gy_count * planes
    scaling = 1.0 / math.sqrt(cell_total)
    kinds = block * ma_count
    reverse = (gx // (gx_count // 2) + gy) % 2 == 1
    k = jnp.where(reverse, ma_count - 1 - ma, ma)

    pieces = jnp.transpose(pod_modes, (3, 2, 1, 0, 4)).reshape(ma_count, 2, cells_x, fields, block, planes)
    pieces = jnp.where(reverse, pieces[::-1], pieces)
    a = lax.all_to_all(pieces, "ma", 0, 0)

    nothing = 0.0 * pieces[0, 0, 0, 0, 0, :1].astype(F32)
    vx, vy = velocity[0] + nothing, velocity[1] + nothing

    def from_gx(part, step):
        return lax.ppermute(part, "gx", [(i, i + step) for i in range(gx_count) if 0 <= i + step < gx_count])

    def from_gy(part, step):
        pairs = [(i, i + step) for i in range(gy_count) if 0 <= i + step < gy_count]
        return lax.ppermute(part, ("y", "core"), pairs)

    def pair_of(part, axis):
        return lax.dynamic_slice_in_dim(part, 2 * k, 2, axis)

    vx_after = pair_of(from_gx(vx[0], -1), 0)
    vx_before = pair_of(from_gx(vx[-1], 1), 0)
    vy_above = from_gy(vy[:, :1], -1)
    vy_below = from_gy(vy[:, -1:], 1)
    vy_all = jnp.concatenate([vy_below, vy, vy_above], axis=1)
    vy_before = lax.dynamic_index_in_dim(vy_all, 2 * k, 1, keepdims=False)
    vy_after = lax.dynamic_index_in_dim(vy_all, 2 * k + 3, 1, keepdims=False)

    def columns(part):
        return pair_of(part, 1).transpose(1, 0, 2).reshape(4, planes)

    vx, vy = columns(vx), columns(vy)
    right = jnp.where(gx == gx_count - 1, 0.0, 1.0)
    left = jnp.where(gx == 0, 0.0, 1.0)
    up = jnp.where((gy == gy_count - 1) & (k == ma_count - 1), 0.0, 1.0)
    down = jnp.where((gy == 0) & (k == 0), 0.0, 1.0)
    coef = 0.5 * jnp.concatenate(
        [
            vx,
            vx[1::2] * right,
            -vx_after * right,
            vx[0::2] * left,
            vx_before * left,
            vy,
            vy[2:] * up,
            -vy_after * up,
            vy[:2] * down,
            vy_before * down,
        ]
    )
    cells = jnp.stack([columns(velocity[2]), columns(region.astype(F32))])

    vmem = pl.BlockSpec(memory_space=pltpu.VMEM)
    smem = pl.BlockSpec(memory_space=pltpu.SMEM)
    width = 4 * fields * planes
    wide = pltpu.VMEM((kinds, width), BF16)
    narrow = pltpu.VMEM((kinds, width // 2), BF16)

    def sums(terms):
        rows = (ma_count, terms * block, LANES)
        return jax.ShapeDtypeStruct(rows, F32), jax.ShapeDtypeStruct(rows, BF16)

    params = pltpu.CompilerParams(vmem_limit_bytes=40 * 2**20)
    core_here = core.astype(jnp.int32)[None]
    zc_keep, zc_send, modes = pl.pallas_call(
        local_kernel,
        out_shape=(*sums(2), jax.ShapeDtypeStruct((kinds, width), BF16)),
        in_specs=[smem, smem, vmem, vmem, vmem],
        out_specs=(vmem, vmem, vmem),
        scratch_shapes=[wide, wide],
        compiler_params=params,
        cost_estimate=pl.CostEstimate(flops=2 * 2 * kinds * kinds * width, bytes_accessed=4 * 2**20, transcendentals=0),
    )(core_here, coupling_table.reshape(-1, fields * fields), partner[None], cells, a)

    def along_x(part, step):
        return lax.ppermute(part, ("gx", "ma"), steps_along_x(shape, step))

    def along_y(part, step):
        return lax.ppermute(part, names, steps_along_y(shape, step))

    yr = along_y(a[:, 0, :, :2], -1)
    yl = along_y(a[:, 1, :, 2:], 1)
    xr = along_x(a[:, :, 0, :2], -1)
    xl = along_x(a[:, :, 1, 2:], 1)

    keep, send = pl.pallas_call(
        edge_kernel,
        out_shape=sums(4),
        in_specs=[smem] + [vmem] * 8,
        out_specs=(vmem, vmem),
        scratch_shapes=[wide, narrow, narrow, wide, narrow, narrow],
        compiler_params=params,
        cost_estimate=pl.CostEstimate(flops=2 * 3 * kinds * kinds * width, bytes_accessed=6 * 2**20, transcendentals=0),
    )(core_here, coef, modes, xr, xl, yr, yl, zc_keep, zc_send)

    def core_swap(part):
        return lax.ppermute(part, "core", [(i, 1 - i) for i in range(core_count)])

    shares = gx_count * y_count
    both = (keep + core_swap(send).astype(F32)).astype(BF16).reshape(ma_count * shares, -1, LANES)
    received = lax.all_to_all(both, ("ma", "gx", "y"), 0, 0)
    share = jnp.sum(received.astype(F32), axis=0) * scaling
    spread = jnp.broadcast_to(share[None], (shares,) + share.shape)
    mine = lax.all_to_all(spread, ("gx", "y"), 0, 0).reshape(4, block, LANES)
    other = core_swap(mine)
    halves = [jnp.where(core == 0, mine, other), jnp.where(core == 0, other, mine)]
    return jnp.concatenate(halves, axis=2).transpose(0, 2, 1)


def solution(mesh):
    gx, gy, ma = (mesh.shape[name] for name in ("gx", "gy", "ma"))
    split = Mesh(mesh.devices.reshape(gx, gy // 2, 2, ma), ("gx", "y", "core", "ma"))
    placed = (
        P("ma", None, "gx", ("y", "core"), None),
        P(None, "gx", ("y", "core"), None),
        P("gx", ("y", "core"), None),
        P(),
        P(),
    )
    return jax.shard_map(
        on_device, mesh=split, in_specs=placed, out_specs=P(None, None, "ma"), check_vma=False
    )
```

time: 1560 us -> 121 us (0.08)
  waiting for transfers between devices: 1490 us -> 13.1 us
  blocking collectives: 0 us -> 54.6 us
  starting transfers between devices: 15.5 us -> 40 us
  local copies, waits for them, and re-layouts: 21.7 us -> 4.77 us
    psum x1 -> x0, waiting for transfers between devices: 1430 us -> none  [on_device(): summed = lax.psum(partial_sums, ('gx', 'gy'))]
    all_to_all x0 -> x2, blocking collectives: none -> 54.6 us  [the longest x1 34.6 us: on_device(): received = lax.all_to_all(both, ('ma', 'gx', 'y'), 0, 0)]
    all_gather x1 -> x0, waiting for transfers between devices: 51.8 us -> none  [on_device(): portion = lax.all_gather(pod_modes, 'ma', axis=0, tiled=True)]
    ppermute x4 -> x10, starting transfers between devices: 15.4 us -> 32.1 us  [the longest x2 7.47 us: core_swap(): return lax.ppermute(part, 'core', [(i, 1 - i) for i in range(core_count)])]
  transfers between devices with their start and end apart: 6 -> 11, of which waited for: 4 -> 4; matrix products, arithmetic and copies ran while one was open for 2% -> 2% of each run, Pallas kernels for 0% -> 2%
where the time goes in v3:
time: 121 us
  blocking collectives  54.6 us (45%)
  starting transfers between devices  40 us (33%)
  waiting for transfers between devices  13.1 us (11%)
  local copies, waits for them, and re-layouts  4.77 us (4%)
  Pallas kernels  4.07 us (3%)
  other arithmetic  3.21 us (3%)
    all_to_all x1, blocking collectives, on_device(): received = lax.all_to_all(both, ('ma', 'gx', 'y'), 0, 0)  34.6 us
    all_to_all x1, blocking collectives, on_device(): mine = lax.all_to_all(spread, ('gx', 'y'), 0, 0).reshape(4, block, LANES)  20 us
    all_to_all x1, waiting for transfers between devices, on_device(): a = lax.all_to_all(pieces, 'ma', 0, 0)  9.29 us
    all_to_all x1, starting transfers between devices, on_device(): a = lax.all_to_all(pieces, 'ma', 0, 0)  7.94 us
    ppermute x2, starting transfers between devices, core_swap(): return lax.ppermute(part, 'core', [(i, 1 - i) for i in range(core_count)])  7.47 us
    ppermute x2, starting transfers between devices, along_y(): return lax.ppermute(part, names, steps_along_y(shape, step))  7.03 us
    ppermute x2, starting transfers between devices, from_gy(): return lax.ppermute(part, ('y', 'core'), pairs)  6.98 us
    ppermute x2, starting transfers between devices, along_x(): return lax.ppermute(part, ('gx', 'ma'), steps_along_x(shape, step))  5.29 us
  transfers between devices with their start and end apart: 11, of which 4 were waited for; matrix products, arithmetic and copies ran while one was open for 2% of the time, Pallas kernels for 2%

profile of v3, /device:TPU:1, one launch (start us, length us, event | category | flops | bytes accessed | tf_op | source)
XLA Modules:
  0.0 120.8 jit_solution(15780792068809492230)
XLA Ops:
  0.0 1.9 %copy.27 = bf16[64,4,2,8,128]{4,0,1,2,3:T(8,128)(2,1)S(1)} copy(bf16[64,4,2,8,128]{4,3,2,1,0:T(8,128)(2,1)} %param.5) | data formatting | bytes 2097152 | tf_op args[0]
  1.9 1.3 %reverse_select_fusion = bf16[4,2,2,4,64,128]{5,4,3,2,1,0:T(8,128)(2,1)} fusion(bf16[4,2,2,4,64,128]{5,4,3,2,1,0:T(8,128)(2,1)S(1)} %bitcast.63, pred[]{:T(512)S(6)} %eq.28), kind=kLoop, calls=%fused_computation | loop fusion | flops 524288 | bytes 2097153 | tf_op jit(solution)/shard_map/jit(_where)/select_n | solution.py:150
  3.3 7.9 %all-to-all-start = ((bf16[4,2,2,4,64,128]{5,4,3,2,1,0:T(8,128)(2,1)}), bf16[4,2,2,4,64,128]{5,4,3,2,1,0:T(8,128)(2,1)S(1)}, u32[]{:S(2)}, u32[]{:S(2)}) async-start(bf16[4,2,2,4,64,128]{5,4,3,2,1,0:T(8,128)(2,1)} %reverse_select_fusion), calls=%async_computation | async-start | bytes 2097152 | tf_op jit(solution)/shard_map/all_to_all | solution.py:151
  11.2 1.2 slice.68
  13.1 1.3 %collective-permute-start = (f32[8,128]{1,0:T(8,128)S(1)}, f32[8,128]{1,0:T(8,128)S(1)}, u32[]{:S(2)}, u32[]{:S(2)}) collective-permute-start(f32[8,128]{1,0:T(8,128)S(1)} %bitcast.77), channel_id=1, source_target_pairs={{64,0},{128,64},{192,128},{256,192},{320,256},{384,320},{448,384},... | collective-permute-start | bytes 12296 | tf_op jit(solution)/shard_map/ppermute | solution.py:157
  14.4 4.0 %collective-permute-start.1 = (f32[8,128]{1,0:T(8,128)S(1)}, f32[8,128]{1,0:T(8,128)S(1)}, u32[]{:S(2)}, u32[]{:S(2)}) collective-permute-start(f32[8,128]{1,0:T(8,128)S(1)} %bitcast.76), channel_id=1, source_target_pairs={{0,64},{64,128},{128,192},{192,256},{256,320},{320,384},{384,448},... | collective-permute-start | bytes 12296 | tf_op jit(solution)/shard_map/ppermute | solution.py:157
  18.4 5.1 %collective-permute-start.3 = (f32[2,1,128]{2,0,1:T(2,128)S(1)}, f32[2,1,128]{2,0,1:T(2,128)S(1)}, u32[]{:S(2)}, u32[]{:S(2)}) collective-permute-start(f32[2,1,128]{2,0,1:T(2,128)S(1)} %get-tuple-element.27), channel_id=1, source_target_pairs={{4,0},{8,4},{12,8},{16,12},{20,16},{24,20},{28,24},{32,28},{36,32}... | collective-permute-start | bytes 3080 | tf_op jit(solution)/shard_map/ppermute | solution.py:161
  23.5 1.9 %collective-permute-start.2 = (f32[2,1,128]{2,0,1:T(2,128)S(1)}, f32[2,1,128]{2,0,1:T(2,128)S(1)}, u32[]{:S(2)}, u32[]{:S(2)}) collective-permute-start(f32[2,1,128]{2,0,1:T(2,128)S(1)} %get-tuple-element.26), channel_id=1, source_target_pairs={{0,4},{4,8},{8,12},{12,16},{16,20},{20,24},{24,28},{28,32},{32,36}... | collective-permute-start | bytes 3080 | tf_op jit(solution)/shard_map/ppermute | solution.py:161
  25.4 0.7 fusion
  26.3 0.0 copy-start.2
  26.3 0.7 copy-done.2
  27.0 0.1 copy.32.table
  27.1 0.1 concatenate.10
  27.2 9.3 %all-to-all-done.a = bf16[4,2,2,4,64,128]{5,4,3,2,1,0:T(8,128)(2,1)S(1)} async-done(((bf16[4,2,2,4,64,128]{5,4,3,2,1,0:T(8,128)(2,1)}), bf16[4,2,2,4,64,128]{5,4,3,2,1,0:T(8,128)(2,1)S(1)}, u32[]{:S(2)}, u32[]{:S(2)}) %all-to-all-start) | async-done | bytes 1048608 | tf_op jit(solution)/shard_map/all_to_all | solution.py:151
  36.6 1.3 %collective-permute-start.4 = (bf16[4,2,2,64,128]{4,3,2,1,0:T(8,128)(2,1)S(1)}, bf16[4,2,2,64,128]{4,3,2,1,0:T(8,128)(2,1)S(1)}, u32[]{:S(2)}, u32[]{:S(2)}) collective-permute-start(bf16[4,2,2,64,128]{4,3,2,1,0:T(8,128)(2,1)S(1)} %get-tuple-element.18), channel_id=1, source_target_pairs={{64,0},{65,1},{66,2},{67,3},{128,64},{129,65},{130,66},{131,67},{1... | collective-permute-start | bytes 786440 | tf_op jit(solution)/shard_map/ppermute | solution.py:221
  37.9 4.0 %collective-permute-start.5 = (bf16[4,2,2,64,128]{4,3,2,1,0:T(8,128)(2,1)S(1)}, bf16[4,2,2,64,128]{4,3,2,1,0:T(8,128)(2,1)S(1)}, u32[]{:S(2)}, u32[]{:S(2)}) collective-permute-start(bf16[4,2,2,64,128]{4,3,2,1,0:T(8,128)(2,1)S(1)} %get-tuple-element.17), channel_id=1, source_target_pairs={{0,64},{1,65},{2,66},{3,67},{64,128},{65,129},{66,130},{67,131},{1... | collective-permute-start | bytes 786440 | tf_op jit(solution)/shard_map/ppermute | solution.py:221
  41.9 1.9 %collective-permute-start.6 = (bf16[4,2,2,64,128]{4,3,2,1,0:T(8,128)(2,1)S(1)}, bf16[4,2,2,64,128]{4,3,2,1,0:T(8,128)(2,1)S(1)}, u32[]{:S(2)}, u32[]{:S(2)}) collective-permute-start(bf16[4,2,2,64,128]{4,3,2,1,0:T(8,128)(2,1)S(1)} %get-tuple-element.16), channel_id=1, source_target_pairs={{1,0},{2,1},{3,2},{7,3},{6,7},{5,6},{4,5},{8,4},{9,8},{10,9},{11,1... | collective-permute-start | bytes 786440 | tf_op jit(solution)/shard_map/ppermute | solution.py:224
  43.8 5.1 %collective-permute-start.7 = (bf16[4,2,2,64,128]{4,3,2,1,0:T(8,128)(2,1)S(1)}, bf16[4,2,2,64,128]{4,3,2,1,0:T(8,128)(2,1)S(1)}, u32[]{:S(2)}, u32[]{:S(2)}) collective-permute-start(bf16[4,2,2,64,128]{4,3,2,1,0:T(8,128)(2,1)S(1)} %get-tuple-element.15), channel_id=1, source_target_pairs={{0,1},{1,2},{2,3},{3,7},{7,6},{6,5},{5,4},{4,8},{8,9},{9,10},{10,1... | collective-permute-start | bytes 786440 | tf_op jit(solution)/shard_map/ppermute | solution.py:224
  49.0 0.0 copy-start
  49.0 0.6 copy-done
  49.6 2.2 %shard_map.55 = (f32[4,128,128]{2,1,0:T(8,128)S(1)}, bf16[4,128,128]{2,1,0:T(8,128)(2,1)S(1)}, bf16[256,2048]{1,0:T(8,128)(2,1)S(1)}) custom-call(s32[1]{0:T(128)} %bitcast.core, f32[8,16]{1,0:T(8,128)S(1)} %copy.32.table, s32[1,128]{1,0:T(1,128)S(1)} %bitcast.62, f32[2,4,128]{2,1,0:T(4,128)S(1)} %pad_maximum_fusion.1.cells, ...), custom_call_target="tpu_custom_call" | custom-call | flops 536870912 | bytes 4194304 | tf_op jit(solution)/shard_map/pallas_call | solution.py:210
  51.9 1.7 %collective-permute-done.7.yl = bf16[4,2,2,64,128]{4,3,2,1,0:T(8,128)(2,1)S(1)} collective-permute-done((bf16[4,2,2,64,128]{4,3,2,1,0:T(8,128)(2,1)S(1)}, bf16[4,2,2,64,128]{4,3,2,1,0:T(8,128)(2,1)S(1)}, u32[]{:S(2)}, u32[]{:S(2)}) %collective-permute-start.7) | collective-permute-done | bytes 262176 | tf_op jit(solution)/shard_map/ppermute | solution.py:224
  53.6 1.8 %shard_map.56 = (f32[4,256,128]{2,1,0:T(8,128)S(1)}, bf16[4,256,128]{2,1,0:T(8,128)(2,1)S(1)}) custom-call(s32[1]{0:T(128)} %bitcast.core, f32[24,128]{1,0:T(8,128)S(1)} %broadcast_multiply_fusion.coef, bf16[256,2048]{1,0:T(8,128)(2,1)S(1)} %get-tuple-element.10.modes, bf16[4,2,2,64,128]{4,3,2,1,0:T(8,128)(2,1)S(1)} %collective-permute-done.4.xr, ...), custom_call_target="tpu_custom_call" | custom-call | flops 805306368 | bytes 6291456 | tf_op jit(solution)/shard_map/pallas_call | solution.py:231
  55.4 2.8 %collective-permute-start.8 = (bf16[4,256,128]{2,1,0:T(8,128)(2,1)S(1)}, bf16[4,256,128]{2,1,0:T(8,128)(2,1)S(1)}, u32[]{:S(2)}, u32[]{:S(2)}) collective-permute-start(bf16[4,256,128]{2,1,0:T(8,128)(2,1)S(1)} %get-tuple-element.14), channel_id=1, source_target_pairs={{0,4},{4,0},{1,5},{5,1},{2,6},{6,2},{3,7},{7,3},{8,12},{12,8},{9,1... | collective-permute-start | bytes 786440 | tf_op jit(solution)/shard_map/ppermute | solution.py:242
  58.2 1.1 collective-permute-done.8
  59.4 0.1 add_convert_fusion
  59.4 34.6 %all_to_all.15 = bf16[256,4,128]{2,1,0:T(4,128)(2,1)S(1)} all-to-all(bf16[256,4,128]{2,1,0:T(4,128)(2,1)S(1)} %bitcast.64), channel_id=1, replica_groups=mesh['gx'=8,'y'=8,'core'=2,'ma'=4] {'ma','gx','y'}, dimensions={0} | all-to-all | bytes 524288 | tf_op jit(solution)/shard_map/all_to_all | solution.py:246
  94.1 0.3 convert_reduce_fusion
  94.4 20.0 %all_to_all.16 = f32[64,4,128]{2,1,0:T(4,128)S(1)} all-to-all(f32[64,4,128]{2,1,0:T(4,128)S(1)} %broadcast_in_dim.16), channel_id=1, replica_groups=mesh['gx'=8,'y'=8,'core'=2,'ma'=4] {'gx','y'}, dimensions={0} | all-to-all | bytes 262144 | tf_op jit(solution)/shard_map/all_to_all | solution.py:249
  114.4 4.7 %collective-permute-start.9 = (f32[4,64,128]{2,1,0:T(8,128)S(1)}, f32[4,64,128]{2,1,0:T(8,128)S(1)}, u32[]{:S(2)}, u32[]{:S(2)}) collective-permute-start(f32[4,64,128]{2,1,0:T(8,128)S(1)} %bitcast.65), channel_id=1, source_target_pairs={{0,4},{4,0},{1,5},{5,1},{2,6},{6,2},{3,7},{7,3},{8,12},{12,8},{9,1... | collective-permute-start | bytes 393224 | tf_op jit(solution)/shard_map/ppermute | solution.py:242
  119.1 1.0 collective-permute-done.9
  120.1 0.7 maximum_bitcast_fusion
  (35 shorter events, 0.3 us)
Async XLA Ops:
  3.3 9.1 %copy-start.1 = (f32[3,2,8,128]{3,2,1,0:T(8,128)S(1)}, f32[3,2,8,128]{3,2,1,0:T(8,128)}, u32[]{:S(2)}) copy-start(f32[3,2,8,128]{3,2,1,0:T(8,128)} %param.6) | copy-start | bytes 73732
  3.3 33.2 %all-to-all-start = ((bf16[4,2,2,4,64,128]{5,4,3,2,1,0:T(8,128)(2,1)}), bf16[4,2,2,4,64,128]{5,4,3,2,1,0:T(8,128)(2,1)S(1)}, u32[]{:S(2)}, u32[]{:S(2)}) async-start(bf16[4,2,2,4,64,128]{5,4,3,2,1,0:T(8,128)(2,1)} %reverse_select_fusion), calls=%async_computation | async-start | bytes 2097152 | tf_op jit(solution)/shard_map/all_to_all | solution.py:151
  13.1 14.0 %collective-permute-start = (f32[8,128]{1,0:T(8,128)S(1)}, f32[8,128]{1,0:T(8,128)S(1)}, u32[]{:S(2)}, u32[]{:S(2)}) collective-permute-start(f32[8,128]{1,0:T(8,128)S(1)} %bitcast.77), channel_id=1, source_target_pairs={{64,0},{128,64},{192,128},{256,192},{320,256},{384,320},{448,384},... | collective-permute-start | bytes 12296 | tf_op jit(solution)/shard_map/ppermute | solution.py:157
  14.4 12.7 %collective-permute-start.1 = (f32[8,128]{1,0:T(8,128)S(1)}, f32[8,128]{1,0:T(8,128)S(1)}, u32[]{:S(2)}, u32[]{:S(2)}) collective-permute-start(f32[8,128]{1,0:T(8,128)S(1)} %bitcast.76), channel_id=1, source_target_pairs={{0,64},{64,128},{128,192},{192,256},{256,320},{320,384},{384,448},... | collective-permute-start | bytes 12296 | tf_op jit(solution)/shard_map/ppermute | solution.py:157
  18.4 8.7 %collective-permute-start.3 = (f32[2,1,128]{2,0,1:T(2,128)S(1)}, f32[2,1,128]{2,0,1:T(2,128)S(1)}, u32[]{:S(2)}, u32[]{:S(2)}) collective-permute-start(f32[2,1,128]{2,0,1:T(2,128)S(1)} %get-tuple-element.27), channel_id=1, source_target_pairs={{4,0},{8,4},{12,8},{16,12},{20,16},{24,20},{28,24},{32,28},{36,32}... | collective-permute-start | bytes 3080 | tf_op jit(solution)/shard_map/ppermute | solution.py:161
  23.5 3.6 %collective-permute-start.2 = (f32[2,1,128]{2,0,1:T(2,128)S(1)}, f32[2,1,128]{2,0,1:T(2,128)S(1)}, u32[]{:S(2)}, u32[]{:S(2)}) collective-permute-start(f32[2,1,128]{2,0,1:T(2,128)S(1)} %get-tuple-element.26), channel_id=1, source_target_pairs={{0,4},{4,8},{8,12},{12,16},{16,20},{20,24},{24,28},{28,32},{32,36}... | collective-permute-start | bytes 3080 | tf_op jit(solution)/shard_map/ppermute | solution.py:161
  26.3 0.7 copy-start.2
  36.6 15.3 %collective-permute-start.4 = (bf16[4,2,2,64,128]{4,3,2,1,0:T(8,128)(2,1)S(1)}, bf16[4,2,2,64,128]{4,3,2,1,0:T(8,128)(2,1)S(1)}, u32[]{:S(2)}, u32[]{:S(2)}) collective-permute-start(bf16[4,2,2,64,128]{4,3,2,1,0:T(8,128)(2,1)S(1)} %get-tuple-element.18), channel_id=1, source_target_pairs={{64,0},{65,1},{66,2},{67,3},{128,64},{129,65},{130,66},{131,67},{1... | collective-permute-start | bytes 786440 | tf_op jit(solution)/shard_map/ppermute | solution.py:221
  37.9 14.0 %collective-permute-start.5 = (bf16[4,2,2,64,128]{4,3,2,1,0:T(8,128)(2,1)S(1)}, bf16[4,2,2,64,128]{4,3,2,1,0:T(8,128)(2,1)S(1)}, u32[]{:S(2)}, u32[]{:S(2)}) collective-permute-start(bf16[4,2,2,64,128]{4,3,2,1,0:T(8,128)(2,1)S(1)} %get-tuple-element.17), channel_id=1, source_target_pairs={{0,64},{1,65},{2,66},{3,67},{64,128},{65,129},{66,130},{67,131},{1... | collective-permute-start | bytes 786440 | tf_op jit(solution)/shard_map/ppermute | solution.py:221
  41.9 10.0 %collective-permute-start.6 = (bf16[4,2,2,64,128]{4,3,2,1,0:T(8,128)(2,1)S(1)}, bf16[4,2,2,64,128]{4,3,2,1,0:T(8,128)(2,1)S(1)}, u32[]{:S(2)}, u32[]{:S(2)}) collective-permute-start(bf16[4,2,2,64,128]{4,3,2,1,0:T(8,128)(2,1)S(1)} %get-tuple-element.16), channel_id=1, source_target_pairs={{1,0},{2,1},{3,2},{7,3},{6,7},{5,6},{4,5},{8,4},{9,8},{10,9},{11,1... | collective-permute-start | bytes 786440 | tf_op jit(solution)/shard_map/ppermute | solution.py:224
  43.8 9.8 %collective-permute-start.7 = (bf16[4,2,2,64,128]{4,3,2,1,0:T(8,128)(2,1)S(1)}, bf16[4,2,2,64,128]{4,3,2,1,0:T(8,128)(2,1)S(1)}, u32[]{:S(2)}, u32[]{:S(2)}) collective-permute-start(bf16[4,2,2,64,128]{4,3,2,1,0:T(8,128)(2,1)S(1)} %get-tuple-element.15), channel_id=1, source_target_pairs={{0,1},{1,2},{2,3},{3,7},{7,6},{6,5},{5,4},{4,8},{8,9},{9,10},{10,1... | collective-permute-start | bytes 786440 | tf_op jit(solution)/shard_map/ppermute | solution.py:224
  49.0 0.7 copy-start
  55.4 3.9 %collective-permute-start.8 = (bf16[4,256,128]{2,1,0:T(8,128)(2,1)S(1)}, bf16[4,256,128]{2,1,0:T(8,128)(2,1)S(1)}, u32[]{:S(2)}, u32[]{:S(2)}) collective-permute-start(bf16[4,256,128]{2,1,0:T(8,128)(2,1)S(1)} %get-tuple-element.14), channel_id=1, source_target_pairs={{0,4},{4,0},{1,5},{5,1},{2,6},{6,2},{3,7},{7,3},{8,12},{12,8},{9,1... | collective-permute-start | bytes 786440 | tf_op jit(solution)/shard_map/ppermute | solution.py:242
  114.4 5.7 %collective-permute-start.9 = (f32[4,64,128]{2,1,0:T(8,128)S(1)}, f32[4,64,128]{2,1,0:T(8,128)S(1)}, u32[]{:S(2)}, u32[]{:S(2)}) collective-permute-start(f32[4,64,128]{2,1,0:T(8,128)S(1)} %bitcast.65), channel_id=1, source_target_pairs={{0,4},{4,0},{1,5},{5,1},{2,6},{6,2},{3,7},{7,3},{8,12},{12,8},{9,1... | collective-permute-start | bytes 393224 | tf_op jit(solution)/shard_map/ppermute | solution.py:242

commit v4 on v3

v4 whole, which is shorter than its diff:
```python
import functools
import math

import jax
import jax.numpy as jnp
from jax import lax
from jax.experimental import pallas as pl
from jax.experimental.pallas import tpu as pltpu
from jax.sharding import Mesh, PartitionSpec as P

LANES = 128
BF16 = jnp.bfloat16
F32 = jnp.float32
CONTRACT_LAST = (((1,), (1,)), ((), ()))


def steps_along_x(shape, step):
    gx_count, y_count, core_count, ma_count = shape
    half = gx_count // 2
    pairs = []
    for gx in range(gx_count):
        to = gx + step
        if 0 <= to < gx_count:
            for ma in range(ma_count):
                to_ma = ma if gx // half == to // half else ma_count - 1 - ma
                pairs.append((gx * ma_count + ma, to * ma_count + to_ma))
    return pairs


def steps_along_y(shape, step):
    gx_count, y_count, core_count, ma_count = shape
    half = gx_count // 2
    gy_count = y_count * core_count

    def number(gx, place):
        gy, k = divmod(place, ma_count)
        ma = ma_count - 1 - k if (gx // half + gy) % 2 else k
        return (gx * gy_count + gy) * ma_count + ma

    places = gy_count * ma_count
    return [
        (number(gx, place), number(gx, place + step))
        for gx in range(gx_count)
        for place in range(places)
        if 0 <= place + step < places
    ]


def pack_kernel(wanted, pieces, *outs):
    half = pieces.shape[3] // 2
    for t in range(4):
        outs[t][...] = pieces[wanted[t], :, :, :half]
        outs[4 + t][...] = pieces[wanted[t], :, :, half:]


def local_kernel(place_of, table, partner, cells, *refs):
    parts, (keep, send, modes, z_image, c_image) = refs[:8], refs[8:]
    fields, block = 2 * parts[0].shape[2], parts[0].shape[3]
    planes = lax.broadcasted_iota(jnp.int32, (LANES, LANES), 0)
    pick = (planes == partner[...]).astype(F32).astype(BF16)
    speed_z, region = cells[0], cells[1]
    coupling = {}
    for f in range(fields):
        for g in range(fields):
            if f != g:
                chosen = jnp.zeros_like(region)
                for number in range(table.shape[0]):
                    chosen = jnp.where(region == float(number), table[number, f * fields + g], chosen)
                coupling[f, g] = chosen
    for col in range(4):
        for t in range(4):
            rows = pl.ds(pl.multiple_of((place_of[1] ^ t) * block, block), block)
            here = [part[col // 2, col % 2, f] for part in (parts[t], parts[4 + t]) for f in range(fields // 2)]
            moved = jnp.dot(jnp.concatenate(here, axis=0), pick, preferred_element_type=F32)
            centre = [cells_f.astype(F32) for cells_f in here]
            for f in range(fields):
                chunk = slice((col * fields + f) * LANES, (col * fields + f + 1) * LANES)
                modes[rows, chunk] = here[f]
                jump = speed_z[col : col + 1] * (moved[f * block : (f + 1) * block] - centre[f])
                z_image[rows, chunk] = jump.astype(BF16)
                running = None
                for g in range(fields):
                    if g != f:
                        term = coupling[f, g][col : col + 1] * centre[g]
                        running = term if running is None else running + term
                c_image[rows, chunk] = running.astype(BF16)
    for q, image in enumerate((z_image, c_image)):
        total = lax.dot_general(image[...], modes[...], CONTRACT_LAST, preferred_element_type=F32)
        place(place_of, keep, send, q, total, block)


def place(place_of, keep, send, q, total, block):
    for j in range(4):
        first = total[j * block : (j + 1) * block, :LANES]
        second = total[j * block : (j + 1) * block, LANES:]
        rows = slice(q * block, (q + 1) * block)
        keep[j, rows, :] = jnp.where(place_of[0] == 0, first, second)
        send[j, rows, :] = jnp.where(place_of[0] == 0, second, first).astype(BF16)


def edge_kernel(place_of, speeds, modes, xr, xl, yr, yl, zc_keep, zc_send, keep, send, x_image, x_edge, x_side, y_image, y_edge, y_side):
    fields, block = 4, modes.shape[0] // 4
    body = 4 * fields * block
    half_speeds = 0.5 * speeds[...]

    def beside_speeds(message):
        rows = message[body:, :].astype(F32)
        return 0.5 * (rows[0:2] + rows[2:4] + rows[4:6])

    def lane_chunk(index):
        return slice(index * LANES, (index + 1) * LANES)

    axes = (
        (0, xr, xl, x_image, x_edge, x_side, lambda line, end: 2 * line + end),
        (4, yr, yl, y_image, y_edge, y_side, lambda line, end: 2 * end + line),
    )
    for base, after, before, image, edge, side, col in axes:
        after_speeds, before_speeds = beside_speeds(after), beside_speeds(before)
        for line in range(2):
            near_speed = half_speeds[base + col(line, 0) : base + col(line, 0) + 1]
            far_speed = half_speeds[base + col(line, 1) : base + col(line, 1) + 1]
            after_speed = after_speeds[line : line + 1]
            before_speed = before_speeds[line : line + 1]
            for j in range(4):
                rows = slice(j * block, (j + 1) * block)
                for f in range(fields):
                    near, far = (lane_chunk(col(line, end) * fields + f) for end in range(2))
                    extra = lane_chunk(line * fields + f)
                    m0 = modes[rows, near].astype(F32)
                    m1 = modes[rows, far].astype(F32)
                    at_near = near_speed * m1
                    at_far = -far_speed * m0
                    start = ((2 * j + line) * 2 + f % 2) * block
                    if f < 2:
                        beside = after[start : start + block, :]
                        at_far = far_speed * beside.astype(F32) + at_far
                        at_side = -after_speed * m1
                    else:
                        beside = before[start : start + block, :]
                        at_near = at_near - near_speed * beside.astype(F32)
                        at_side = before_speed * m0
                    image[rows, near] = at_near.astype(BF16)
                    image[rows, far] = at_far.astype(BF16)
                    edge[rows, extra] = at_side.astype(BF16)
                    side[rows, extra] = beside
    for q, (_, _, _, image, edge, side, _) in enumerate(axes):
        total = lax.dot_general(image[...], modes[...], CONTRACT_LAST, preferred_element_type=F32)
        total += lax.dot_general(edge[...], side[...], CONTRACT_LAST, preferred_element_type=F32)
        place(place_of, keep, send, q, total, block)
    keep[:, 2 * block :, :] = zc_keep[...]
    send[:, 2 * block :, :] = zc_send[...]


def message_kernel(end, place_of, speeds, *refs):
    parts, (x_message, y_message) = refs[:4], refs[4:]
    block = parts[0].shape[3]
    body = 16 * block
    vx, vy = speeds[:4], speeds[4:]
    for t in range(4):
        for line in range(2):
            for f in range(2):
                start = ((place_of[1] ^ t) * 4 + line * 2 + f) * block
                rows = pl.ds(pl.multiple_of(start, block), block)
                x_message[rows, :] = parts[t][line, end, f]
                y_message[rows, :] = parts[t][end, line, f]
    for message, at_edge in (
        (x_message, jnp.concatenate([vx[end : end + 1], vx[2 + end : 3 + end]])),
        (y_message, vy[2 * end : 2 * end + 2]),
    ):
        first = at_edge.astype(BF16).astype(F32)
        rest = at_edge - first
        second = rest.astype(BF16).astype(F32)
        third = rest - second
        message[body:, :] = jnp.concatenate([first, second, third, jnp.zeros((10, LANES), F32)]).astype(BF16)


def on_device(pod_modes, velocity, region, partner, coupling_table):
    block, fields, cells_x, cells_y, planes = pod_modes.shape
    names = ("gx", "y", "core", "ma")
    shape = tuple(lax.axis_size(name) for name in names)
    gx_count, y_count, core_count, ma_count = shape
    gx, y, core, ma = (lax.axis_index(name) for name in names)
    gy_count, gy = y_count * core_count, y * core_count + core
    cell_total = fields * cells_x * gx_count * cells_y * gy_count * planes
    scaling = 1.0 / math.sqrt(cell_total)
    kinds = block * ma_count
    reverse = (gx // (gx_count // 2) + gy) % 2 == 1
    k = jnp.where(reverse, ma_count - 1 - ma, ma)

    homes = jnp.stack([ma ^ t for t in range(ma_count)])
    wanted = jnp.where(reverse, ma_count - 1 - homes, homes).astype(jnp.int32)
    vmem = pl.BlockSpec(memory_space=pltpu.VMEM)
    smem = pl.BlockSpec(memory_space=pltpu.SMEM)
    params = pltpu.CompilerParams(vmem_limit_bytes=40 * 2**20)
    pieces = jnp.transpose(pod_modes, (3, 2, 1, 0, 4)).reshape(ma_count, 2, cells_x, fields, block, planes)
    piece = jax.ShapeDtypeStruct((2, cells_x, fields // 2, block, planes), BF16)
    packed = pl.pallas_call(
        pack_kernel,
        out_shape=(piece,) * (2 * ma_count),
        in_specs=[smem, vmem],
        out_specs=(vmem,) * (2 * ma_count),
        compiler_params=params,
        cost_estimate=pl.CostEstimate(flops=0, bytes_accessed=2 * 2**20, transcendentals=0),
    )(wanted, pieces)

    def collected(parts):
        blocks = {0: parts[0]}
        for t in (2, 3, 1):
            blocks[t] = lax.ppermute(parts[t], "ma", [(i, i ^ t) for i in range(ma_count)])
        return [blocks[t] for t in range(ma_count)]

    low, high = collected(packed[:ma_count]), collected(packed[ma_count:])

    def columns(part):
        return lax.dynamic_slice_in_dim(part, 2 * k, 2, 1).transpose(1, 0, 2).reshape(4, planes)

    vx, vy = columns(velocity[0]), columns(velocity[1])
    cells = jnp.stack([columns(velocity[2]), columns(region.astype(F32))])

    speeds = jnp.concatenate([vx, vy])
    place_of = jnp.stack([core, ma]).astype(jnp.int32)
    width = 4 * fields * planes
    wide = pltpu.VMEM((kinds, width), BF16)
    narrow = pltpu.VMEM((kinds, width // 2), BF16)

    def sums(terms):
        rows = (ma_count, terms * block, LANES)
        return jax.ShapeDtypeStruct(rows, F32), jax.ShapeDtypeStruct(rows, BF16)

    zc_keep, zc_send, modes = pl.pallas_call(
        local_kernel,
        out_shape=(*sums(2), jax.ShapeDtypeStruct((kinds, width), BF16)),
        in_specs=[smem, smem] + [vmem] * 10,
        out_specs=(vmem, vmem, vmem),
        scratch_shapes=[wide, wide],
        compiler_params=params,
        cost_estimate=pl.CostEstimate(flops=2 * 2 * kinds * kinds * width, bytes_accessed=4 * 2**20, transcendentals=0),
    )(place_of, coupling_table.reshape(-1, fields * fields), partner[None], cells, *low, *high)

    def messages(parts, end):
        rows = jax.ShapeDtypeStruct((4 * fields * block + 16, LANES), BF16)
        return pl.pallas_call(
            functools.partial(message_kernel, end),
            out_shape=(rows, rows),
            in_specs=[smem] + [vmem] * 5,
            out_specs=(vmem, vmem),
            compiler_params=params,
            cost_estimate=pl.CostEstimate(flops=0, bytes_accessed=2**20, transcendentals=0),
        )(place_of, speeds, *parts)

    def along_x(part, step):
        return lax.ppermute(part, ("gx", "ma"), steps_along_x(shape, step))

    def along_y(part, step):
        return lax.ppermute(part, names, steps_along_y(shape, step))

    x_message, y_message = messages(low, 0)
    xr, yr = along_x(x_message, -1), along_y(y_message, -1)
    x_message, y_message = messages(high, 1)
    xl, yl = along_x(x_message, 1), along_y(y_message, 1)

    keep, send = pl.pallas_call(
        edge_kernel,
        out_shape=sums(4),
        in_specs=[smem] + [vmem] * 8,
        out_specs=(vmem, vmem),
        scratch_shapes=[wide, narrow, narrow, wide, narrow, narrow],
        compiler_params=params,
        cost_estimate=pl.CostEstimate(flops=2 * 3 * kinds * kinds * width, bytes_accessed=6 * 2**20, transcendentals=0),
    )(place_of, speeds, modes, xr, xl, yr, yl, zc_keep, zc_send)

    def core_swap(part):
        return lax.ppermute(part, "core", [(i, 1 - i) for i in range(core_count)])

    shares = gx_count * y_count
    both = (keep + core_swap(send).astype(F32)).astype(BF16).reshape(ma_count * shares, -1, LANES)
    received = lax.all_to_all(both, ("ma", "gx", "y"), 0, 0)
    share = jnp.sum(received.astype(F32), axis=0) * scaling
    spread = jnp.broadcast_to(share[None], (shares,) + share.shape)
    mine = lax.all_to_all(spread, ("gx", "y"), 0, 0).reshape(4, block, LANES)
    other = core_swap(mine)
    halves = [jnp.where(core == 0, mine, other), jnp.where(core == 0, other, mine)]
    return jnp.concatenate(halves, axis=2).transpose(0, 2, 1)


def solution(mesh):
    gx, gy, ma = (mesh.shape[name] for name in ("gx", "gy", "ma"))
    split = Mesh(mesh.devices.reshape(gx, gy // 2, 2, ma), ("gx", "y", "core", "ma"))
    placed = (
        P("ma", None, "gx", ("y", "core"), None),
        P(None, "gx", ("y", "core"), None),
        P("gx", ("y", "core"), None),
        P(),
        P(),
    )
    return jax.shard_map(
        on_device, mesh=split, in_specs=placed, out_specs=P(None, None, "ma"), check_vma=False
    )
```

time: 121 us -> 121 us (level)
  waiting for transfers between devices: 13.1 us -> 9.89 us
  Pallas kernels: 4.07 us -> 6.74 us
  blocking collectives: 54.6 us -> 57.2 us
  local copies, waits for them, and re-layouts: 4.77 us -> 2.68 us
  starting transfers between devices: 40 us -> 41.4 us
  other arithmetic: 3.21 us -> 1.98 us
    ppermute x4 -> x6, starting transfers between devices: 12.3 us -> 21.8 us  [collected(): lax.ppermute(parts[t], 'ma', [(i, i ^ t) for i in range(ma_count)])]
    all_to_all x1 -> x0, waiting for transfers between devices: 9.29 us -> none  [on_device(): a = lax.all_to_all(pieces, 'ma', 0, 0)]
    all_to_all x1 -> x0, starting transfers between devices: 7.94 us -> none  [on_device(): a = lax.all_to_all(pieces, 'ma', 0, 0)]
    ppermute x4 -> x6, waiting for transfers between devices: 0.01 us -> 5.24 us  [collected(): lax.ppermute(parts[t], 'ma', [(i, i ^ t) for i in range(ma_count)])]
    all_to_all x1, blocking collectives: 34.6 us -> 37.2 us  [on_device(): received = lax.all_to_all(both, ('ma', 'gx', 'y'), 0, 0)]
    unnamed x7 -> x6, local copies, waits for them, and re-layouts: 3.23 us -> 0.66 us
    transpose x4 -> x7, local copies, waits for them, and re-layouts: 0.03 us -> 1.93 us  [the longest x1 1.9 us: on_device(): jnp.transpose(pod_modes, (3, 2, 1, 0, 4))]
    pallas_call x0 -> x3, Pallas kernels: none -> 1.81 us  [the longest x2 1.2 us: messages(): pl.pallas_call(functools.partial(message_kernel, end), out_shape=(rows, r...]
  transfers between devices with their start and end apart: 11 -> 12, of which waited for: 4 -> 5; matrix products, arithmetic and copies ran while one was open for 2% -> 1% of each run, Pallas kernels for 2% -> 3%
where the time goes in v4:
time: 121 us; the launch traced here: 120 us
  blocking collectives  57.2 us (47%)
  starting transfers between devices  41.4 us (34%)
  waiting for transfers between devices  9.89 us (8%)
  Pallas kernels  6.74 us (6%)
  local copies, waits for them, and re-layouts  2.68 us (2%)
  other arithmetic  1.98 us (2%)
    all_to_all x1, blocking collectives, on_device(): received = lax.all_to_all(both, ('ma', 'gx', 'y'), 0, 0)  37.2 us
    ppermute x6, starting transfers between devices, collected(): lax.ppermute(parts[t], 'ma', [(i, i ^ t) for i in range(ma_count)])  21.8 us
    all_to_all x1, blocking collectives, on_device(): mine = lax.all_to_all(spread, ('gx', 'y'), 0, 0).reshape(4, block, LANES)  20 us
    ppermute x2, starting transfers between devices, along_y(): return lax.ppermute(part, names, steps_along_y(shape, step))  6.92 us
    ppermute x2, starting transfers between devices, core_swap(): return lax.ppermute(part, 'core', [(i, 1 - i) for i in range(core_count)])  6.61 us
    ppermute x2, starting transfers between devices, along_x(): return lax.ppermute(part, ('gx', 'ma'), steps_along_x(shape, step))  6 us
    ppermute x6, waiting for transfers between devices, collected(): lax.ppermute(parts[t], 'ma', [(i, i ^ t) for i in range(ma_count)])  5.24 us
    pallas_call x1, Pallas kernels, on_device(): pl.pallas_call(local_kernel, out_shape=(*sums(2), jax.ShapeDtypeStruct((k...  2.55 us
  transfers between devices with their start and end apart: 12, of which 5 were waited for; matrix products, arithmetic and copies ran while one was open for 1% of the time, Pallas kernels for 3%

profile of v4, /device:TPU:1, one launch (start us, length us, event | category | flops | bytes accessed | tf_op | source)
XLA Modules:
  0.0 120.2 jit_solution(8914325111662196381)
XLA Ops:
  0.0 1.9 %copy.13 = bf16[8,2,4,64,128]{4,3,2,1,0:T(8,128)(2,1)S(1)} copy(bf16[8,2,4,64,128]{4,0,1,2,3:T(8,128)(2,1)} %bitcast.36) | data formatting | bytes 2097152 | tf_op jit(solution)/shard_map/transpose | solution.py:195
  1.9 0.1 broadcast_select_fusion.2.wanted
  2.0 0.6 shard_map.55
  2.6 4.8 %collective-permute-start = (bf16[2,2,2,64,128]{4,3,2,1,0:T(8,128)(2,1)S(1)}, bf16[2,2,2,64,128]{4,3,2,1,0:T(8,128)(2,1)S(1)}, u32[]{:S(2)}, u32[]{:S(2)}) collective-permute-start(bf16[2,2,2,64,128]{4,3,2,1,0:T(8,128)(2,1)S(1)} %get-tuple-element.23), channel_id=1, source_target_pairs={{0,1},{1,0},{2,3},{3,2},{4,5},{5,4},{6,7},{7,6},{8,9},{9,8},{10,11... | collective-permute-start | bytes 393224 | tf_op jit(solution)/shard_map/ppermute | solution.py:209
  7.5 5.8 %collective-permute-start.1 = (bf16[2,2,2,64,128]{4,3,2,1,0:T(8,128)(2,1)S(1)}, bf16[2,2,2,64,128]{4,3,2,1,0:T(8,128)(2,1)S(1)}, u32[]{:S(2)}, u32[]{:S(2)}) collective-permute-start(bf16[2,2,2,64,128]{4,3,2,1,0:T(8,128)(2,1)S(1)} %get-tuple-element.24), channel_id=1, source_target_pairs={{0,2},{1,3},{2,0},{3,1},{4,6},{5,7},{6,4},{7,5},{8,10},{9,11},{10,... | collective-permute-start | bytes 393224 | tf_op jit(solution)/shard_map/ppermute | solution.py:209
  13.3 1.9 %collective-permute-start.2 = (bf16[2,2,2,64,128]{4,3,2,1,0:T(8,128)(2,1)S(1)}, bf16[2,2,2,64,128]{4,3,2,1,0:T(8,128)(2,1)S(1)}, u32[]{:S(2)}, u32[]{:S(2)}) collective-permute-start(bf16[2,2,2,64,128]{4,3,2,1,0:T(8,128)(2,1)S(1)} %get-tuple-element.25), channel_id=1, source_target_pairs={{0,3},{1,2},{2,1},{3,0},{4,7},{5,6},{6,5},{7,4},{8,11},{9,10},{10,... | collective-permute-start | bytes 393224 | tf_op jit(solution)/shard_map/ppermute | solution.py:209
  15.2 2.2 %collective-permute-start.3 = (bf16[2,2,2,64,128]{4,3,2,1,0:T(8,128)(2,1)S(1)}, bf16[2,2,2,64,128]{4,3,2,1,0:T(8,128)(2,1)S(1)}, u32[]{:S(2)}, u32[]{:S(2)}) collective-permute-start(bf16[2,2,2,64,128]{4,3,2,1,0:T(8,128)(2,1)S(1)} %get-tuple-element.27), channel_id=1, source_target_pairs={{0,1},{1,0},{2,3},{3,2},{4,5},{5,4},{6,7},{7,6},{8,9},{9,8},{10,11... | collective-permute-start | bytes 393224 | tf_op jit(solution)/shard_map/ppermute | solution.py:209
  17.4 5.2 %collective-permute-start.4 = (bf16[2,2,2,64,128]{4,3,2,1,0:T(8,128)(2,1)S(1)}, bf16[2,2,2,64,128]{4,3,2,1,0:T(8,128)(2,1)S(1)}, u32[]{:S(2)}, u32[]{:S(2)}) collective-permute-start(bf16[2,2,2,64,128]{4,3,2,1,0:T(8,128)(2,1)S(1)} %get-tuple-element.28), channel_id=1, source_target_pairs={{0,2},{1,3},{2,0},{3,1},{4,6},{5,7},{6,4},{7,5},{8,10},{9,11},{10,... | collective-permute-start | bytes 393224 | tf_op jit(solution)/shard_map/ppermute | solution.py:209
  22.6 1.9 %collective-permute-start.5 = (bf16[2,2,2,64,128]{4,3,2,1,0:T(8,128)(2,1)S(1)}, bf16[2,2,2,64,128]{4,3,2,1,0:T(8,128)(2,1)S(1)}, u32[]{:S(2)}, u32[]{:S(2)}) collective-permute-start(bf16[2,2,2,64,128]{4,3,2,1,0:T(8,128)(2,1)S(1)} %get-tuple-element.29), channel_id=1, source_target_pairs={{0,3},{1,2},{2,1},{3,0},{4,7},{5,6},{6,5},{7,4},{8,11},{9,10},{10,... | collective-permute-start | bytes 393224 | tf_op jit(solution)/shard_map/ppermute | solution.py:209
  24.6 0.1 pad_add_fusion.place_of
  24.8 0.6 shard_map.57
  25.4 1.3 %collective-permute-start.6 = (bf16[1040,128]{1,0:T(8,128)(2,1)S(1)}, bf16[1040,128]{1,0:T(8,128)(2,1)S(1)}, u32[]{:S(2)}, u32[]{:S(2)}) collective-permute-start(bf16[1040,128]{1,0:T(8,128)(2,1)S(1)} %get-tuple-element.31), channel_id=1, source_target_pairs={{64,0},{65,1},{66,2},{67,3},{128,64},{129,65},{130,66},{131,67},{1... | collective-permute-start | bytes 798728 | tf_op jit(solution)/shard_map/ppermute | solution.py:252
  26.7 2.2 %collective-permute-done.4.refs_6_.refs_2_ = bf16[2,2,2,64,128]{4,3,2,1,0:T(8,128)(2,1)S(1)} collective-permute-done((bf16[2,2,2,64,128]{4,3,2,1,0:T(8,128)(2,1)S(1)}, bf16[2,2,2,64,128]{4,3,2,1,0:T(8,128)(2,1)S(1)}, u32[]{:S(2)}, u32[]{:S(2)}) %collective-permute-start.4) | collective-permute-done | bytes 131104 | tf_op jit(solution)/shard_map/ppermute | solution.py:209
  28.9 3.0 %collective-permute-done.5.refs_7_.refs_3_ = bf16[2,2,2,64,128]{4,3,2,1,0:T(8,128)(2,1)S(1)} collective-permute-done((bf16[2,2,2,64,128]{4,3,2,1,0:T(8,128)(2,1)S(1)}, bf16[2,2,2,64,128]{4,3,2,1,0:T(8,128)(2,1)S(1)}, u32[]{:S(2)}, u32[]{:S(2)}) %collective-permute-start.5) | collective-permute-done | bytes 131104 | tf_op jit(solution)/shard_map/ppermute | solution.py:209
  31.9 0.6 shard_map.58
  32.5 4.7 %collective-permute-start.7 = (bf16[1040,128]{1,0:T(8,128)(2,1)S(1)}, bf16[1040,128]{1,0:T(8,128)(2,1)S(1)}, u32[]{:S(2)}, u32[]{:S(2)}) collective-permute-start(bf16[1040,128]{1,0:T(8,128)(2,1)S(1)} %get-tuple-element.32), channel_id=1, source_target_pairs={{0,64},{1,65},{2,66},{3,67},{64,128},{65,129},{66,130},{67,131},{1... | collective-permute-start | bytes 798728 | tf_op jit(solution)/shard_map/ppermute | solution.py:252
  37.2 5.0 %collective-permute-start.8 = (bf16[1040,128]{1,0:T(8,128)(2,1)S(1)}, bf16[1040,128]{1,0:T(8,128)(2,1)S(1)}, u32[]{:S(2)}, u32[]{:S(2)}) collective-permute-start(bf16[1040,128]{1,0:T(8,128)(2,1)S(1)} %get-tuple-element.33), channel_id=1, source_target_pairs={{1,0},{2,1},{3,2},{7,3},{6,7},{5,6},{4,5},{8,4},{9,8},{10,9},{11,1... | collective-permute-start | bytes 798728 | tf_op jit(solution)/shard_map/ppermute | solution.py:255
  42.2 1.9 %collective-permute-start.9 = (bf16[1040,128]{1,0:T(8,128)(2,1)S(1)}, bf16[1040,128]{1,0:T(8,128)(2,1)S(1)}, u32[]{:S(2)}, u32[]{:S(2)}) collective-permute-start(bf16[1040,128]{1,0:T(8,128)(2,1)S(1)} %get-tuple-element.34), channel_id=1, source_target_pairs={{0,1},{1,2},{2,3},{3,7},{7,6},{6,5},{5,4},{4,8},{8,9},{9,10},{10,1... | collective-permute-start | bytes 798728 | tf_op jit(solution)/shard_map/ppermute | solution.py:255
  44.2 0.7 fusion
  44.9 0.6 copy-done
  45.5 2.5 %shard_map.56 = (f32[4,128,128]{2,1,0:T(8,128)S(1)}, bf16[4,128,128]{2,1,0:T(8,128)(2,1)S(1)}, bf16[256,2048]{1,0:T(8,128)(2,1)S(1)}) custom-call(s32[2]{0:T(128)S(1)} %pad_add_fusion.place_of, f32[8,16]{1,0:T(8,128)S(1)} %copy.14.table, s32[1,128]{1,0:T(1,128)S(1)} %bitcast.35, f32[2,4,128]{2,1,0:T(4,128)S(1)} %pad_maximum_fusion.1.cells, ...), custom_call_target="tpu_custom_call" | custom-call | flops 536870912 | bytes 4194304 | tf_op jit(solution)/shard_map/pallas_call | solution.py:230
  48.1 2.2 %collective-permute-done.9.yl = bf16[1040,128]{1,0:T(8,128)(2,1)S(1)} collective-permute-done((bf16[1040,128]{1,0:T(8,128)(2,1)S(1)}, bf16[1040,128]{1,0:T(8,128)(2,1)S(1)}, u32[]{:S(2)}, u32[]{:S(2)}) %collective-permute-start.9) | collective-permute-done | bytes 266272 | tf_op jit(solution)/shard_map/ppermute | solution.py:255
  50.3 2.4 %shard_map.59 = (f32[4,256,128]{2,1,0:T(8,128)S(1)}, bf16[4,256,128]{2,1,0:T(8,128)(2,1)S(1)}) custom-call(s32[2]{0:T(128)S(1)} %pad_add_fusion.place_of, f32[8,128]{1,0:T(8,128)S(1)} %pad_maximum_fusion.speeds, bf16[256,2048]{1,0:T(8,128)(2,1)S(1)} %get-tuple-element.30.modes, bf16[1040,128]{1,0:T(8,128)(2,1)S(1)} %collective-permute-done.6.xr, ...), custom_call_target="tpu_custom_call" | custom-call | flops 805306368 | bytes 6291456 | tf_op jit(solution)/shard_map/pallas_call | solution.py:262
  52.7 1.9 %collective-permute-start.10 = (bf16[4,256,128]{2,1,0:T(8,128)(2,1)S(1)}, bf16[4,256,128]{2,1,0:T(8,128)(2,1)S(1)}, u32[]{:S(2)}, u32[]{:S(2)}) collective-permute-start(bf16[4,256,128]{2,1,0:T(8,128)(2,1)S(1)} %get-tuple-element.38), channel_id=1, source_target_pairs={{0,4},{4,0},{1,5},{5,1},{2,6},{6,2},{3,7},{7,3},{8,12},{12,8},{9,1... | collective-permute-start | bytes 786440 | tf_op jit(solution)/shard_map/ppermute | solution.py:273
  54.6 1.5 %collective-permute-done.10 = bf16[4,256,128]{2,1,0:T(8,128)(2,1)S(1)} collective-permute-done((bf16[4,256,128]{2,1,0:T(8,128)(2,1)S(1)}, bf16[4,256,128]{2,1,0:T(8,128)(2,1)S(1)}, u32[]{:S(2)}, u32[]{:S(2)}) %collective-permute-start.10) | collective-permute-done | bytes 262176 | tf_op jit(solution)/shard_map/ppermute | solution.py:273
  56.1 0.1 add_convert_fusion
  56.2 37.2 %all_to_all.10 = bf16[256,4,128]{2,1,0:T(4,128)(2,1)S(1)} all-to-all(bf16[256,4,128]{2,1,0:T(4,128)(2,1)S(1)} %bitcast.37), channel_id=1, replica_groups=mesh['gx'=8,'y'=8,'core'=2,'ma'=4] {'ma','gx','y'}, dimensions={0} | all-to-all | bytes 524288 | tf_op jit(solution)/shard_map/all_to_all | solution.py:277
  93.4 0.3 convert_reduce_fusion
  93.7 20.0 %all_to_all.11 = f32[64,4,128]{2,1,0:T(4,128)S(1)} all-to-all(f32[64,4,128]{2,1,0:T(4,128)S(1)} %broadcast_in_dim.10), channel_id=1, replica_groups=mesh['gx'=8,'y'=8,'core'=2,'ma'=4] {'gx','y'}, dimensions={0} | all-to-all | bytes 262144 | tf_op jit(solution)/shard_map/all_to_all | solution.py:280
  113.7 4.7 %collective-permute-start.11 = (f32[4,64,128]{2,1,0:T(8,128)S(1)}, f32[4,64,128]{2,1,0:T(8,128)S(1)}, u32[]{:S(2)}, u32[]{:S(2)}) collective-permute-start(f32[4,64,128]{2,1,0:T(8,128)S(1)} %bitcast.38), channel_id=1, source_target_pairs={{0,4},{4,0},{1,5},{5,1},{2,6},{6,2},{3,7},{7,3},{8,12},{12,8},{9,1... | collective-permute-start | bytes 393224 | tf_op jit(solution)/shard_map/ppermute | solution.py:273
  118.5 1.0 collective-permute-done.11
  119.4 0.7 maximum_bitcast_fusion
  (25 shorter events, 0.2 us)
Async XLA Ops:
  2.0 20.6 %copy-start.1 = (f32[3,2,8,128]{3,2,1,0:T(8,128)S(1)}, f32[3,2,8,128]{3,2,1,0:T(8,128)}, u32[]{:S(2)}) copy-start(f32[3,2,8,128]{3,2,1,0:T(8,128)} %param.6) | copy-start | bytes 73732
  2.6 20.0 %collective-permute-start = (bf16[2,2,2,64,128]{4,3,2,1,0:T(8,128)(2,1)S(1)}, bf16[2,2,2,64,128]{4,3,2,1,0:T(8,128)(2,1)S(1)}, u32[]{:S(2)}, u32[]{:S(2)}) collective-permute-start(bf16[2,2,2,64,128]{4,3,2,1,0:T(8,128)(2,1)S(1)} %get-tuple-element.23), channel_id=1, source_target_pairs={{0,1},{1,0},{2,3},{3,2},{4,5},{5,4},{6,7},{7,6},{8,9},{9,8},{10,11... | collective-permute-start | bytes 393224 | tf_op jit(solution)/shard_map/ppermute | solution.py:209
  7.5 17.3 %collective-permute-start.1 = (bf16[2,2,2,64,128]{4,3,2,1,0:T(8,128)(2,1)S(1)}, bf16[2,2,2,64,128]{4,3,2,1,0:T(8,128)(2,1)S(1)}, u32[]{:S(2)}, u32[]{:S(2)}) collective-permute-start(bf16[2,2,2,64,128]{4,3,2,1,0:T(8,128)(2,1)S(1)} %get-tuple-element.24), channel_id=1, source_target_pairs={{0,2},{1,3},{2,0},{3,1},{4,6},{5,7},{6,4},{7,5},{8,10},{9,11},{10,... | collective-permute-start | bytes 393224 | tf_op jit(solution)/shard_map/ppermute | solution.py:209
  13.3 11.5 %collective-permute-start.2 = (bf16[2,2,2,64,128]{4,3,2,1,0:T(8,128)(2,1)S(1)}, bf16[2,2,2,64,128]{4,3,2,1,0:T(8,128)(2,1)S(1)}, u32[]{:S(2)}, u32[]{:S(2)}) collective-permute-start(bf16[2,2,2,64,128]{4,3,2,1,0:T(8,128)(2,1)S(1)} %get-tuple-element.25), channel_id=1, source_target_pairs={{0,3},{1,2},{2,1},{3,0},{4,7},{5,6},{6,5},{7,4},{8,11},{9,10},{10,... | collective-permute-start | bytes 393224 | tf_op jit(solution)/shard_map/ppermute | solution.py:209
  15.2 11.5 %collective-permute-start.3 = (bf16[2,2,2,64,128]{4,3,2,1,0:T(8,128)(2,1)S(1)}, bf16[2,2,2,64,128]{4,3,2,1,0:T(8,128)(2,1)S(1)}, u32[]{:S(2)}, u32[]{:S(2)}) collective-permute-start(bf16[2,2,2,64,128]{4,3,2,1,0:T(8,128)(2,1)S(1)} %get-tuple-element.27), channel_id=1, source_target_pairs={{0,1},{1,0},{2,3},{3,2},{4,5},{5,4},{6,7},{7,6},{8,9},{9,8},{10,11... | collective-permute-start | bytes 393224 | tf_op jit(solution)/shard_map/ppermute | solution.py:209
  17.4 11.5 %collective-permute-start.4 = (bf16[2,2,2,64,128]{4,3,2,1,0:T(8,128)(2,1)S(1)}, bf16[2,2,2,64,128]{4,3,2,1,0:T(8,128)(2,1)S(1)}, u32[]{:S(2)}, u32[]{:S(2)}) collective-permute-start(bf16[2,2,2,64,128]{4,3,2,1,0:T(8,128)(2,1)S(1)} %get-tuple-element.28), channel_id=1, source_target_pairs={{0,2},{1,3},{2,0},{3,1},{4,6},{5,7},{6,4},{7,5},{8,10},{9,11},{10,... | collective-permute-start | bytes 393224 | tf_op jit(solution)/shard_map/ppermute | solution.py:209
  22.6 2.0 %copy-start.2 = (f32[8,4,4]{0,2,1:T(4,128)S(1)}, f32[8,4,4]{0,2,1:T(4,128)}, u32[]{:S(2)}) copy-start(f32[8,4,4]{0,2,1:T(4,128)} %param.9) | copy-start | bytes 1540
  22.6 9.3 %collective-permute-start.5 = (bf16[2,2,2,64,128]{4,3,2,1,0:T(8,128)(2,1)S(1)}, bf16[2,2,2,64,128]{4,3,2,1,0:T(8,128)(2,1)S(1)}, u32[]{:S(2)}, u32[]{:S(2)}) collective-permute-start(bf16[2,2,2,64,128]{4,3,2,1,0:T(8,128)(2,1)S(1)} %get-tuple-element.29), channel_id=1, source_target_pairs={{0,3},{1,2},{2,1},{3,0},{4,7},{5,6},{6,5},{7,4},{8,11},{9,10},{10,... | collective-permute-start | bytes 393224 | tf_op jit(solution)/shard_map/ppermute | solution.py:209
  25.4 22.7 %collective-permute-start.6 = (bf16[1040,128]{1,0:T(8,128)(2,1)S(1)}, bf16[1040,128]{1,0:T(8,128)(2,1)S(1)}, u32[]{:S(2)}, u32[]{:S(2)}) collective-permute-start(bf16[1040,128]{1,0:T(8,128)(2,1)S(1)} %get-tuple-element.31), channel_id=1, source_target_pairs={{64,0},{65,1},{66,2},{67,3},{128,64},{129,65},{130,66},{131,67},{1... | collective-permute-start | bytes 798728 | tf_op jit(solution)/shard_map/ppermute | solution.py:252
  32.5 15.6 %collective-permute-start.7 = (bf16[1040,128]{1,0:T(8,128)(2,1)S(1)}, bf16[1040,128]{1,0:T(8,128)(2,1)S(1)}, u32[]{:S(2)}, u32[]{:S(2)}) collective-permute-start(bf16[1040,128]{1,0:T(8,128)(2,1)S(1)} %get-tuple-element.32), channel_id=1, source_target_pairs={{0,64},{1,65},{2,66},{3,67},{64,128},{65,129},{66,130},{67,131},{1... | collective-permute-start | bytes 798728 | tf_op jit(solution)/shard_map/ppermute | solution.py:252
  37.2 10.9 %collective-permute-start.8 = (bf16[1040,128]{1,0:T(8,128)(2,1)S(1)}, bf16[1040,128]{1,0:T(8,128)(2,1)S(1)}, u32[]{:S(2)}, u32[]{:S(2)}) collective-permute-start(bf16[1040,128]{1,0:T(8,128)(2,1)S(1)} %get-tuple-element.33), channel_id=1, source_target_pairs={{1,0},{2,1},{3,2},{7,3},{6,7},{5,6},{4,5},{8,4},{9,8},{10,9},{11,1... | collective-permute-start | bytes 798728 | tf_op jit(solution)/shard_map/ppermute | solution.py:255
  42.2 8.1 %collective-permute-start.9 = (bf16[1040,128]{1,0:T(8,128)(2,1)S(1)}, bf16[1040,128]{1,0:T(8,128)(2,1)S(1)}, u32[]{:S(2)}, u32[]{:S(2)}) collective-permute-start(bf16[1040,128]{1,0:T(8,128)(2,1)S(1)} %get-tuple-element.34), channel_id=1, source_target_pairs={{0,1},{1,2},{2,3},{3,7},{7,6},{6,5},{5,4},{4,8},{8,9},{9,10},{10,1... | collective-permute-start | bytes 798728 | tf_op jit(solution)/shard_map/ppermute | solution.py:255
  44.9 0.7 copy-start
  52.7 3.4 %collective-permute-start.10 = (bf16[4,256,128]{2,1,0:T(8,128)(2,1)S(1)}, bf16[4,256,128]{2,1,0:T(8,128)(2,1)S(1)}, u32[]{:S(2)}, u32[]{:S(2)}) collective-permute-start(bf16[4,256,128]{2,1,0:T(8,128)(2,1)S(1)} %get-tuple-element.38), channel_id=1, source_target_pairs={{0,4},{4,0},{1,5},{5,1},{2,6},{6,2},{3,7},{7,3},{8,12},{12,8},{9,1... | collective-permute-start | bytes 786440 | tf_op jit(solution)/shard_map/ppermute | solution.py:273
  113.7 5.7 %collective-permute-start.11 = (f32[4,64,128]{2,1,0:T(8,128)S(1)}, f32[4,64,128]{2,1,0:T(8,128)S(1)}, u32[]{:S(2)}, u32[]{:S(2)}) collective-permute-start(f32[4,64,128]{2,1,0:T(8,128)S(1)} %bitcast.38), channel_id=1, source_target_pairs={{0,4},{4,0},{1,5},{5,1},{2,6},{6,2},{3,7},{7,3},{8,12},{12,8},{9,1... | collective-permute-start | bytes 393224 | tf_op jit(solution)/shard_map/ppermute | solution.py:273

commit v5 on v4

--- a/solution.py
+++ b/solution.py
@@ -1,4 +1,3 @@
-import functools
 import math
 
 import jax
@@ -47,15 +46,16 @@
 
 
 def pack_kernel(wanted, pieces, *outs):
-    half = pieces.shape[3] // 2
     for t in range(4):
-        outs[t][...] = pieces[wanted[t], :, :, :half]
-        outs[4 + t][...] = pieces[wanted[t], :, :, half:]
+        outs[t][0] = pieces[wanted[t], 0, 1]
+        outs[t][1] = pieces[wanted[t], 1, 0]
+        outs[4][t, 0] = pieces[wanted[4 + t], 0, 0]
+        outs[4][t, 1] = pieces[wanted[4 + t], 1, 1]
 
 
 def local_kernel(place_of, table, partner, cells, *refs):
-    parts, (keep, send, modes, z_image, c_image) = refs[:8], refs[8:]
-    fields, block = 2 * parts[0].shape[2], parts[0].shape[3]
+    early, late, (keep, send, modes, z_image, c_image) = refs[:4], refs[4], refs[5:]
+    fields, block = late.shape[2], late.shape[3]
     planes = lax.broadcasted_iota(jnp.int32, (LANES, LANES), 0)
     pick = (planes == partner[...]).astype(F32).astype(BF16)
     speed_z, region = cells[0], cells[1]
@@ -69,8 +69,12 @@
                 coupling[f, g] = chosen
     for col in range(4):
         for t in range(4):
-            rows = pl.ds(pl.multiple_of((place_of[1] ^ t) * block, block), block)
-            here = [part[col // 2, col % 2, f] for part in (parts[t], parts[4 + t]) for f in range(fields // 2)]
+            if col in (0, 3):
+                rows = slice(t * block, (t + 1) * block)
+                here = [late[t, col // 2, f] for f in range(fields)]
+            else:
+                rows = pl.ds(pl.multiple_of((place_of[1] ^ t) * block, block), block)
+                here = [early[t][col - 1, f] for f in range(fields)]
             moved = jnp.dot(jnp.concatenate(here, axis=0), pick, preferred_element_type=F32)
             centre = [cells_f.astype(F32) for cells_f in here]
             for f in range(fields):
@@ -103,9 +107,9 @@
     body = 4 * fields * block
     half_speeds = 0.5 * speeds[...]
 
-    def beside_speeds(message):
-        rows = message[body:, :].astype(F32)
-        return 0.5 * (rows[0:2] + rows[2:4] + rows[4:6])
+    def beside_speed(message, axis):
+        rows = message[body:, :].astype(F32)[3 * axis : 3 * axis + 3]
+        return 0.5 * (rows[0:1] + rows[1:2] + rows[2:3])
 
     def lane_chunk(index):
         return slice(index * LANES, (index + 1) * LANES)
@@ -114,13 +118,11 @@
         (0, xr, xl, x_image, x_edge, x_side, lambda line, end: 2 * line + end),
         (4, yr, yl, y_image, y_edge, y_side, lambda line, end: 2 * end + line),
     )
-    for base, after, before, image, edge, side, col in axes:
-        after_speeds, before_speeds = beside_speeds(after), beside_speeds(before)
-        for line in range(2):
+    for axis, (base, after, before, image, edge, side, col) in enumerate(axes):
+        for line, message in enumerate((before, after)):
             near_speed = half_speeds[base + col(line, 0) : base + col(line, 0) + 1]
             far_speed = half_speeds[base + col(line, 1) : base + col(line, 1) + 1]
-            after_speed = after_speeds[line : line + 1]
-            before_speed = before_speeds[line : line + 1]
+            their_speed = beside_speed(message, axis)
             for j in range(4):
                 rows = slice(j * block, (j + 1) * block)
                 for f in range(fields):
@@ -128,17 +130,16 @@
                     extra = lane_chunk(line * fields + f)
                     m0 = modes[rows, near].astype(F32)
                     m1 = modes[rows, far].astype(F32)
+                    start = (j * fields + f) * block
+                    beside = message[start : start + block, :]
                     at_near = near_speed * m1
                     at_far = -far_speed * m0
-                    start = ((2 * j + line) * 2 + f % 2) * block
-                    if f < 2:
-                        beside = after[start : start + block, :]
+                    if line == 1:
                         at_far = far_speed * beside.astype(F32) + at_far
-                        at_side = -after_speed * m1
+                        at_side = -their_speed * m1
                     else:
-                        beside = before[start : start + block, :]
                         at_near = at_near - near_speed * beside.astype(F32)
-                        at_side = before_speed * m0
+                        at_side = their_speed * m0
                     image[rows, near] = at_near.astype(BF16)
                     image[rows, far] = at_far.astype(BF16)
                     edge[rows, extra] = at_side.astype(BF16)
@@ -151,27 +152,23 @@
     send[:, 2 * block :, :] = zc_send[...]
 
 
-def message_kernel(end, place_of, speeds, *refs):
-    parts, (x_message, y_message) = refs[:4], refs[4:]
-    block = parts[0].shape[3]
-    body = 16 * block
-    vx, vy = speeds[:4], speeds[4:]
-    for t in range(4):
-        for line in range(2):
-            for f in range(2):
-                start = ((place_of[1] ^ t) * 4 + line * 2 + f) * block
-                rows = pl.ds(pl.multiple_of(start, block), block)
-                x_message[rows, :] = parts[t][line, end, f]
-                y_message[rows, :] = parts[t][end, line, f]
-    for message, at_edge in (
-        (x_message, jnp.concatenate([vx[end : end + 1], vx[2 + end : 3 + end]])),
-        (y_message, vy[2 * end : 2 * end + 2]),
-    ):
-        first = at_edge.astype(BF16).astype(F32)
-        rest = at_edge - first
-        second = rest.astype(BF16).astype(F32)
-        third = rest - second
-        message[body:, :] = jnp.concatenate([first, second, third, jnp.zeros((10, LANES), F32)]).astype(BF16)
+def message_kernel(place_of, speeds, *refs):
+    parts, messages = refs[:4], refs[4:]
+    fields, block = parts[0].shape[1], parts[0].shape[2]
+    body = 4 * fields * block
+    for number, message in enumerate(messages):
+        for t in range(4):
+            for f in range(fields):
+                start = ((place_of[1] ^ t) * fields + f) * block
+                message[pl.ds(pl.multiple_of(start, block), block), :] = parts[t][number, f]
+        rows = []
+        for axis in range(2):
+            rest = speeds[4 * axis + 1 + number : 4 * axis + 2 + number, :]
+            for _ in range(3):
+                rows.append(rest.astype(BF16).astype(F32))
+                rest = rest - rows[-1]
+        rows.append(jnp.zeros((10, LANES), F32))
+        message[body:, :] = jnp.concatenate(rows).astype(BF16)
 
 
 def on_device(pod_modes, velocity, region, partner, coupling_table):
@@ -187,29 +184,24 @@
     reverse = (gx // (gx_count // 2) + gy) % 2 == 1
     k = jnp.where(reverse, ma_count - 1 - ma, ma)
 
-    homes = jnp.stack([ma ^ t for t in range(ma_count)])
+    homes = jnp.stack([ma ^ t for t in range(ma_count)] + [jnp.asarray(m) for m in range(ma_count)])
     wanted = jnp.where(reverse, ma_count - 1 - homes, homes).astype(jnp.int32)
     vmem = pl.BlockSpec(memory_space=pltpu.VMEM)
     smem = pl.BlockSpec(memory_space=pltpu.SMEM)
     params = pltpu.CompilerParams(vmem_limit_bytes=40 * 2**20)
     pieces = jnp.transpose(pod_modes, (3, 2, 1, 0, 4)).reshape(ma_count, 2, cells_x, fields, block, planes)
-    piece = jax.ShapeDtypeStruct((2, cells_x, fields // 2, block, planes), BF16)
-    packed = pl.pallas_call(
+    piece = (2, fields, block, planes)
+    *early, late = pl.pallas_call(
         pack_kernel,
-        out_shape=(piece,) * (2 * ma_count),
+        out_shape=(jax.ShapeDtypeStruct(piece, BF16),) * ma_count + (jax.ShapeDtypeStruct((ma_count, *piece), BF16),),
         in_specs=[smem, vmem],
-        out_specs=(vmem,) * (2 * ma_count),
+        out_specs=(vmem,) * (ma_count + 1),
         compiler_params=params,
         cost_estimate=pl.CostEstimate(flops=0, bytes_accessed=2 * 2**20, transcendentals=0),
     )(wanted, pieces)
-
-    def collected(parts):
-        blocks = {0: parts[0]}
-        for t in (2, 3, 1):
-            blocks[t] = lax.ppermute(parts[t], "ma", [(i, i ^ t) for i in range(ma_count)])
-        return [blocks[t] for t in range(ma_count)]
-
-    low, high = collected(packed[:ma_count]), collected(packed[ma_count:])
+    for t in (2, 3, 1):
+        early[t] = lax.ppermute(early[t], "ma", [(i, i ^ t) for i in range(ma_count)])
+    late = lax.all_to_all(late, "ma", 0, 0)
 
     def columns(part):
         return lax.dynamic_slice_in_dim(part, 2 * k, 2, 1).transpose(1, 0, 2).reshape(4, planes)
@@ -230,23 +222,22 @@
     zc_keep, zc_send, modes = pl.pallas_call(
         local_kernel,
         out_shape=(*sums(2), jax.ShapeDtypeStruct((kinds, width), BF16)),
-        in_specs=[smem, smem] + [vmem] * 10,
+        in_specs=[smem, smem] + [vmem] * 7,
         out_specs=(vmem, vmem, vmem),
         scratch_shapes=[wide, wide],
         compiler_params=params,
         cost_estimate=pl.CostEstimate(flops=2 * 2 * kinds * kinds * width, bytes_accessed=4 * 2**20, transcendentals=0),
-    )(place_of, coupling_table.reshape(-1, fields * fields), partner[None], cells, *low, *high)
-
-    def messages(parts, end):
-        rows = jax.ShapeDtypeStruct((4 * fields * block + 16, LANES), BF16)
-        return pl.pallas_call(
-            functools.partial(message_kernel, end),
-            out_shape=(rows, rows),
-            in_specs=[smem] + [vmem] * 5,
-            out_specs=(vmem, vmem),
-            compiler_params=params,
-            cost_estimate=pl.CostEstimate(flops=0, bytes_accessed=2**20, transcendentals=0),
-        )(place_of, speeds, *parts)
+    )(place_of, coupling_table.reshape(-1, fields * fields), partner[None], cells, *early, late)
+
+    rows = jax.ShapeDtypeStruct((4 * fields * block + 16, LANES), BF16)
+    first, second = pl.pallas_call(
+        message_kernel,
+        out_shape=(rows, rows),
+        in_specs=[smem] + [vmem] * 5,
+        out_specs=(vmem, vmem),
+        compiler_params=params,
+        cost_estimate=pl.CostEstimate(flops=0, bytes_accessed=2**20, transcendentals=0),
+    )(place_of, speeds, *early)
 
     def along_x(part, step):
         return lax.ppermute(part, ("gx", "ma"), steps_along_x(shape, step))
@@ -254,10 +245,8 @@
     def along_y(part, step):
         return lax.ppermute(part, names, steps_along_y(shape, step))
 
-    x_message, y_message = messages(low, 0)
-    xr, yr = along_x(x_message, -1), along_y(y_message, -1)
-    x_message, y_message = messages(high, 1)
-    xl, yl = along_x(x_message, 1), along_y(y_message, 1)
+    xr, xl = along_x(second, -1), along_x(first, 1)
+    yr, yl = along_y(first, -1), along_y(second, 1)
 
     keep, send = pl.pallas_call(
         edge_kernel,
@@ -276,11 +265,9 @@
     both = (keep + core_swap(send).astype(F32)).astype(BF16).reshape(ma_count * shares, -1, LANES)
     received = lax.all_to_all(both, ("ma", "gx", "y"), 0, 0)
     share = jnp.sum(received.astype(F32), axis=0) * scaling
-    spread = jnp.broadcast_to(share[None], (shares,) + share.shape)
-    mine = lax.all_to_all(spread, ("gx", "y"), 0, 0).reshape(4, block, LANES)
-    other = core_swap(mine)
-    halves = [jnp.where(core == 0, mine, other), jnp.where(core == 0, other, mine)]
-    return jnp.concatenate(halves, axis=2).transpose(0, 2, 1)
+    spread = jnp.broadcast_to(share[None], (shares * core_count,) + share.shape)
+    whole = lax.all_to_all(spread, ("core", "gx", "y"), 0, 0)
+    return whole.reshape(core_count, 4, block, LANES).transpose(1, 0, 3, 2).reshape(4, kinds, block)
 
 
 def solution(mesh):

time: 121 us -> 121 us (level)
  blocking collectives: 57.2 us -> 67.5 us
  starting transfers between devices: 41.4 us -> 34.8 us
  waiting for transfers between devices: 9.89 us -> 5.82 us
  local copies, waits for them, and re-layouts: 2.68 us -> 4.11 us
    ppermute x6 -> x3, starting transfers between devices: 21.8 us -> 12.5 us  [on_device(): lax.ppermute(early[t], 'ma', [(i, i ^ t) for i in range(ma_count)])]
    all_to_all x1, blocking collectives: 20 us -> 26.8 us  [on_device(): whole = lax.all_to_all(spread, ('core', 'gx', 'y'), 0, 0)]
    all_to_all x0 -> x1, starting transfers between devices: none -> 4.53 us  [on_device(): late = lax.all_to_all(late, 'ma', 0, 0)]
    ppermute x6 -> x3, waiting for transfers between devices: 5.24 us -> 1.36 us  [on_device(): lax.ppermute(early[t], 'ma', [(i, i ^ t) for i in range(ma_count)])]
    all_to_all x1, blocking collectives: 37.2 us -> 40.7 us  [on_device(): received = lax.all_to_all(both, ('ma', 'gx', 'y'), 0, 0)]
    ppermute x2, starting transfers between devices: 6.92 us -> 9.68 us  [along_y(): return lax.ppermute(part, names, steps_along_y(shape, step))]
    ppermute x2, starting transfers between devices: 6 us -> 3.37 us  [along_x(): return lax.ppermute(part, ('gx', 'ma'), steps_along_x(shape, step))]
    ppermute x2 -> x1, starting transfers between devices: 6.61 us -> 4.67 us  [core_swap(): return lax.ppermute(part, 'core', [(i, 1 - i) for i in range(core_count)])]
  transfers between devices with their start and end apart: 12 -> 9, of which waited for: 5 -> 4; matrix products, arithmetic and copies ran while one was open for 1% -> 1% of each run, Pallas kernels for 3% -> 3%
where the time goes in v5:
time: 121 us; the launch traced here: 120 us
  blocking collectives  67.5 us (56%)
  starting transfers between devices  34.8 us (29%)
  Pallas kernels  6.52 us (5%)
  waiting for transfers between devices  5.82 us (5%)
  local copies, waits for them, and re-layouts  4.11 us (3%)
    all_to_all x1, blocking collectives, on_device(): received = lax.all_to_all(both, ('ma', 'gx', 'y'), 0, 0)  40.7 us
    all_to_all x1, blocking collectives, on_device(): whole = lax.all_to_all(spread, ('core', 'gx', 'y'), 0, 0)  26.8 us
    ppermute x3, starting transfers between devices, on_device(): lax.ppermute(early[t], 'ma', [(i, i ^ t) for i in range(ma_count)])  12.5 us
    ppermute x2, starting transfers between devices, along_y(): return lax.ppermute(part, names, steps_along_y(shape, step))  9.68 us
    ppermute x1, starting transfers between devices, core_swap(): return lax.ppermute(part, 'core', [(i, 1 - i) for i in range(core_count)])  4.67 us
    all_to_all x1, starting transfers between devices, on_device(): late = lax.all_to_all(late, 'ma', 0, 0)  4.53 us
    ppermute x2, starting transfers between devices, along_x(): return lax.ppermute(part, ('gx', 'ma'), steps_along_x(shape, step))  3.37 us
    ppermute x2, waiting for transfers between devices, along_y(): return lax.ppermute(part, names, steps_along_y(shape, step))  2.87 us
  transfers between devices with their start and end apart: 9, of which 4 were waited for; matrix products, arithmetic and copies ran while one was open for 1% of the time, Pallas kernels for 3%

profile of v5, /device:TPU:1, one launch (start us, length us, event | category | flops | bytes accessed | tf_op | source)
XLA Modules:
  0.0 120.1 jit_solution(14002350818026233801)
XLA Ops:
  0.0 1.9 %copy.19 = bf16[8,2,4,64,128]{4,3,2,1,0:T(8,128)(2,1)S(1)} copy(bf16[8,2,4,64,128]{4,0,1,2,3:T(8,128)(2,1)} %bitcast.37) | data formatting | bytes 2097152 | tf_op jit(solution)/shard_map/transpose | solution.py:192
  1.9 0.1 stack.32
  2.0 1.4 %shard_map.55 = (bf16[2,4,64,128]{3,2,1,0:T(8,128)(2,1)S(1)}, bf16[2,4,64,128]{3,2,1,0:T(8,128)(2,1)S(1)}, bf16[2,4,64,128]{3,2,1,0:T(8,128)(2,1)S(1)}, bf16[2,4...) custom-call(s32[8]{0:T(128)S(1)} %broadcast_select_fusion.wanted, bf16[4,2,2,4,64,128]{5,4,3,2,1,0:T(8,128)(2,1)S(1)} %bitcast.35), custom_call_target="tpu_custom_call" | custom-call | bytes 2097152 | tf_op jit(solution)/shard_map/pallas_call | solution.py:194
  3.4 4.8 %collective-permute-start = (bf16[2,4,64,128]{3,2,1,0:T(8,128)(2,1)S(1)}, bf16[2,4,64,128]{3,2,1,0:T(8,128)(2,1)S(1)}, u32[]{:S(2)}, u32[]{:S(2)}) collective-permute-start(bf16[2,4,64,128]{3,2,1,0:T(8,128)(2,1)S(1)} %get-tuple-element.18), channel_id=1, source_target_pairs={{0,1},{1,0},{2,3},{3,2},{4,5},{5,4},{6,7},{7,6},{8,9},{9,8},{10,11... | collective-permute-start | bytes 393224 | tf_op jit(solution)/shard_map/ppermute | solution.py:203
  8.2 5.8 %collective-permute-start.1 = (bf16[2,4,64,128]{3,2,1,0:T(8,128)(2,1)S(1)}, bf16[2,4,64,128]{3,2,1,0:T(8,128)(2,1)S(1)}, u32[]{:S(2)}, u32[]{:S(2)}) collective-permute-start(bf16[2,4,64,128]{3,2,1,0:T(8,128)(2,1)S(1)} %get-tuple-element.19), channel_id=1, source_target_pairs={{0,2},{1,3},{2,0},{3,1},{4,6},{5,7},{6,4},{7,5},{8,10},{9,11},{10,... | collective-permute-start | bytes 393224 | tf_op jit(solution)/shard_map/ppermute | solution.py:203
  14.1 1.9 %collective-permute-start.2 = (bf16[2,4,64,128]{3,2,1,0:T(8,128)(2,1)S(1)}, bf16[2,4,64,128]{3,2,1,0:T(8,128)(2,1)S(1)}, u32[]{:S(2)}, u32[]{:S(2)}) collective-permute-start(bf16[2,4,64,128]{3,2,1,0:T(8,128)(2,1)S(1)} %get-tuple-element.20), channel_id=1, source_target_pairs={{0,3},{1,2},{2,1},{3,0},{4,7},{5,6},{6,5},{7,4},{8,11},{9,10},{10,... | collective-permute-start | bytes 393224 | tf_op jit(solution)/shard_map/ppermute | solution.py:203
  16.0 0.0 copy-start.1
  16.0 4.5 %all-to-all-start = ((bf16[4,2,4,64,128]{4,3,2,1,0:T(8,128)(2,1)}), bf16[4,2,4,64,128]{4,3,2,1,0:T(8,128)(2,1)S(1)}, u32[]{:S(2)}, u32[]{:S(2)}) async-start(bf16[4,2,4,64,128]{4,3,2,1,0:T(8,128)(2,1)} %get-tuple-element.21), calls=%async_computation | async-start | bytes 1048576 | tf_op jit(solution)/shard_map/all_to_all | solution.py:204
  20.6 0.0 copy-start.2
  20.6 0.1 pad_add_fusion.place_of
  20.7 0.6 copy-done.2
  21.3 0.1 copy.20.table
  21.4 0.0 collective-permute-done.refs_1_
  21.4 1.4 %collective-permute-done.2.refs_3_ = bf16[2,4,64,128]{3,2,1,0:T(8,128)(2,1)S(1)} collective-permute-done((bf16[2,4,64,128]{3,2,1,0:T(8,128)(2,1)S(1)}, bf16[2,4,64,128]{3,2,1,0:T(8,128)(2,1)S(1)}, u32[]{:S(2)}, u32[]{:S(2)}) %collective-permute-start.2) | collective-permute-done | bytes 131104 | tf_op jit(solution)/shard_map/ppermute | solution.py:203
  22.7 0.6 shard_map.57
  23.3 2.1 %collective-permute-start.4 = (bf16[1040,128]{1,0:T(8,128)(2,1)S(1)}, bf16[1040,128]{1,0:T(8,128)(2,1)S(1)}, u32[]{:S(2)}, u32[]{:S(2)}) collective-permute-start(bf16[1040,128]{1,0:T(8,128)(2,1)S(1)} %get-tuple-element.24), channel_id=1, source_target_pairs={{0,64},{1,65},{2,66},{3,67},{64,128},{65,129},{66,130},{67,131},{1... | collective-permute-start | bytes 798728 | tf_op jit(solution)/shard_map/ppermute | solution.py:243
  25.4 7.8 %collective-permute-start.5 = (bf16[1040,128]{1,0:T(8,128)(2,1)S(1)}, bf16[1040,128]{1,0:T(8,128)(2,1)S(1)}, u32[]{:S(2)}, u32[]{:S(2)}) collective-permute-start(bf16[1040,128]{1,0:T(8,128)(2,1)S(1)} %get-tuple-element.24), channel_id=1, source_target_pairs={{1,0},{2,1},{3,2},{7,3},{6,7},{5,6},{4,5},{8,4},{9,8},{10,9},{11,1... | collective-permute-start | bytes 798728 | tf_op jit(solution)/shard_map/ppermute | solution.py:246
  33.2 1.3 %collective-permute-start.3 = (bf16[1040,128]{1,0:T(8,128)(2,1)S(1)}, bf16[1040,128]{1,0:T(8,128)(2,1)S(1)}, u32[]{:S(2)}, u32[]{:S(2)}) collective-permute-start(bf16[1040,128]{1,0:T(8,128)(2,1)S(1)} %get-tuple-element.23), channel_id=1, source_target_pairs={{64,0},{65,1},{66,2},{67,3},{128,64},{129,65},{130,66},{131,67},{1... | collective-permute-start | bytes 798728 | tf_op jit(solution)/shard_map/ppermute | solution.py:243
  34.5 1.9 %collective-permute-start.6 = (bf16[1040,128]{1,0:T(8,128)(2,1)S(1)}, bf16[1040,128]{1,0:T(8,128)(2,1)S(1)}, u32[]{:S(2)}, u32[]{:S(2)}) collective-permute-start(bf16[1040,128]{1,0:T(8,128)(2,1)S(1)} %get-tuple-element.23), channel_id=1, source_target_pairs={{0,1},{1,2},{2,3},{3,7},{7,6},{6,5},{5,4},{4,8},{8,9},{9,10},{10,1... | collective-permute-start | bytes 798728 | tf_op jit(solution)/shard_map/ppermute | solution.py:246
  36.4 0.7 fusion
  37.1 0.6 copy-done
  37.8 2.4 %shard_map.56 = (f32[4,128,128]{2,1,0:T(8,128)S(1)}, bf16[4,128,128]{2,1,0:T(8,128)(2,1)S(1)}, bf16[256,2048]{1,0:T(8,128)(2,1)S(1)}) custom-call(s32[2]{0:T(128)S(1)} %pad_add_fusion.place_of, f32[8,16]{1,0:T(8,128)S(1)} %copy.20.table, s32[1,128]{1,0:T(1,128)S(1)} %bitcast.36, f32[2,4,128]{2,1,0:T(4,128)S(1)} %pad_maximum_fusion.1.cells, ...), custom_call_target="tpu_custom_call" | custom-call | flops 536870912 | bytes 4194304 | tf_op jit(solution)/shard_map/pallas_call | solution.py:222
  40.2 0.4 collective-permute-done.3.xr
  40.7 2.9 %collective-permute-done.6.yl = bf16[1040,128]{1,0:T(8,128)(2,1)S(1)} collective-permute-done((bf16[1040,128]{1,0:T(8,128)(2,1)S(1)}, bf16[1040,128]{1,0:T(8,128)(2,1)S(1)}, u32[]{:S(2)}, u32[]{:S(2)}) %collective-permute-start.6) | collective-permute-done | bytes 266272 | tf_op jit(solution)/shard_map/ppermute | solution.py:246
  43.5 2.1 %shard_map.58 = (f32[4,256,128]{2,1,0:T(8,128)S(1)}, bf16[4,256,128]{2,1,0:T(8,128)(2,1)S(1)}) custom-call(s32[2]{0:T(128)S(1)} %pad_add_fusion.place_of, f32[8,128]{1,0:T(8,128)S(1)} %pad_maximum_fusion.speeds, bf16[256,2048]{1,0:T(8,128)(2,1)S(1)} %get-tuple-element.22.modes, bf16[1040,128]{1,0:T(8,128)(2,1)S(1)} %collective-permute-done.3.xr, ...), custom_call_target="tpu_custom_call" | custom-call | flops 805306368 | bytes 6291456 | tf_op jit(solution)/shard_map/pallas_call | solution.py:251
  45.6 4.7 %collective-permute-start.7 = (bf16[4,256,128]{2,1,0:T(8,128)(2,1)S(1)}, bf16[4,256,128]{2,1,0:T(8,128)(2,1)S(1)}, u32[]{:S(2)}, u32[]{:S(2)}) collective-permute-start(bf16[4,256,128]{2,1,0:T(8,128)(2,1)S(1)} %get-tuple-element.28), channel_id=1, source_target_pairs={{0,4},{4,0},{1,5},{5,1},{2,6},{6,2},{3,7},{7,3},{8,12},{12,8},{9,1... | collective-permute-start | bytes 786440 | tf_op jit(solution)/shard_map/ppermute | solution.py:262
  50.3 1.1 collective-permute-done.7
  51.5 0.1 add_convert_fusion
  51.5 40.7 %all_to_all.15 = bf16[256,4,128]{2,1,0:T(4,128)(2,1)S(1)} all-to-all(bf16[256,4,128]{2,1,0:T(4,128)(2,1)S(1)} %bitcast.39), channel_id=1, replica_groups=mesh['gx'=8,'y'=8,'core'=2,'ma'=4] {'ma','gx','y'}, dimensions={0} | all-to-all | bytes 524288 | tf_op jit(solution)/shard_map/all_to_all | solution.py:266
  92.2 0.3 convert_reduce_fusion
  92.6 26.8 %all_to_all.16 = f32[128,4,128]{2,1,0:T(4,128)S(1)} all-to-all(f32[128,4,128]{2,1,0:T(4,128)S(1)} %broadcast_in_dim.10), channel_id=1, replica_groups=mesh['gx'=8,'y'=8,'core'=2,'ma'=4] {'core','gx','y'}, dimensions={0} | all-to-all | bytes 524288 | tf_op jit(solution)/shard_map/all_to_all | solution.py:269
  119.4 0.7 copy.24
  (18 shorter events, 0.1 us)
Async XLA Ops:
  3.4 17.9 %collective-permute-start = (bf16[2,4,64,128]{3,2,1,0:T(8,128)(2,1)S(1)}, bf16[2,4,64,128]{3,2,1,0:T(8,128)(2,1)S(1)}, u32[]{:S(2)}, u32[]{:S(2)}) collective-permute-start(bf16[2,4,64,128]{3,2,1,0:T(8,128)(2,1)S(1)} %get-tuple-element.18), channel_id=1, source_target_pairs={{0,1},{1,0},{2,3},{3,2},{4,5},{5,4},{6,7},{7,6},{8,9},{9,8},{10,11... | collective-permute-start | bytes 393224 | tf_op jit(solution)/shard_map/ppermute | solution.py:203
  8.2 13.1 %collective-permute-start.1 = (bf16[2,4,64,128]{3,2,1,0:T(8,128)(2,1)S(1)}, bf16[2,4,64,128]{3,2,1,0:T(8,128)(2,1)S(1)}, u32[]{:S(2)}, u32[]{:S(2)}) collective-permute-start(bf16[2,4,64,128]{3,2,1,0:T(8,128)(2,1)S(1)} %get-tuple-element.19), channel_id=1, source_target_pairs={{0,2},{1,3},{2,0},{3,1},{4,6},{5,7},{6,4},{7,5},{8,10},{9,11},{10,... | collective-permute-start | bytes 393224 | tf_op jit(solution)/shard_map/ppermute | solution.py:203
  14.1 8.7 %collective-permute-start.2 = (bf16[2,4,64,128]{3,2,1,0:T(8,128)(2,1)S(1)}, bf16[2,4,64,128]{3,2,1,0:T(8,128)(2,1)S(1)}, u32[]{:S(2)}, u32[]{:S(2)}) collective-permute-start(bf16[2,4,64,128]{3,2,1,0:T(8,128)(2,1)S(1)} %get-tuple-element.20), channel_id=1, source_target_pairs={{0,3},{1,2},{2,1},{3,0},{4,7},{5,6},{6,5},{7,4},{8,11},{9,10},{10,... | collective-permute-start | bytes 393224 | tf_op jit(solution)/shard_map/ppermute | solution.py:203
  16.0 4.5 %copy-start.1 = (f32[3,2,8,128]{3,2,1,0:T(8,128)S(1)}, f32[3,2,8,128]{3,2,1,0:T(8,128)}, u32[]{:S(2)}) copy-start(f32[3,2,8,128]{3,2,1,0:T(8,128)} %param.6) | copy-start | bytes 73732
  16.0 21.1 %all-to-all-start = ((bf16[4,2,4,64,128]{4,3,2,1,0:T(8,128)(2,1)}), bf16[4,2,4,64,128]{4,3,2,1,0:T(8,128)(2,1)S(1)}, u32[]{:S(2)}, u32[]{:S(2)}) async-start(bf16[4,2,4,64,128]{4,3,2,1,0:T(8,128)(2,1)} %get-tuple-element.21), calls=%async_computation | async-start | bytes 1048576 | tf_op jit(solution)/shard_map/all_to_all | solution.py:204
  20.6 0.7 copy-start.2
  23.3 17.3 %collective-permute-start.4 = (bf16[1040,128]{1,0:T(8,128)(2,1)S(1)}, bf16[1040,128]{1,0:T(8,128)(2,1)S(1)}, u32[]{:S(2)}, u32[]{:S(2)}) collective-permute-start(bf16[1040,128]{1,0:T(8,128)(2,1)S(1)} %get-tuple-element.24), channel_id=1, source_target_pairs={{0,64},{1,65},{2,66},{3,67},{64,128},{65,129},{66,130},{67,131},{1... | collective-permute-start | bytes 798728 | tf_op jit(solution)/shard_map/ppermute | solution.py:243
  25.4 15.3 %collective-permute-start.5 = (bf16[1040,128]{1,0:T(8,128)(2,1)S(1)}, bf16[1040,128]{1,0:T(8,128)(2,1)S(1)}, u32[]{:S(2)}, u32[]{:S(2)}) collective-permute-start(bf16[1040,128]{1,0:T(8,128)(2,1)S(1)} %get-tuple-element.24), channel_id=1, source_target_pairs={{1,0},{2,1},{3,2},{7,3},{6,7},{5,6},{4,5},{8,4},{9,8},{10,9},{11,1... | collective-permute-start | bytes 798728 | tf_op jit(solution)/shard_map/ppermute | solution.py:246
  33.2 7.5 %collective-permute-start.3 = (bf16[1040,128]{1,0:T(8,128)(2,1)S(1)}, bf16[1040,128]{1,0:T(8,128)(2,1)S(1)}, u32[]{:S(2)}, u32[]{:S(2)}) collective-permute-start(bf16[1040,128]{1,0:T(8,128)(2,1)S(1)} %get-tuple-element.23), channel_id=1, source_target_pairs={{64,0},{65,1},{66,2},{67,3},{128,64},{129,65},{130,66},{131,67},{1... | collective-permute-start | bytes 798728 | tf_op jit(solution)/shard_map/ppermute | solution.py:243
  34.5 9.1 %collective-permute-start.6 = (bf16[1040,128]{1,0:T(8,128)(2,1)S(1)}, bf16[1040,128]{1,0:T(8,128)(2,1)S(1)}, u32[]{:S(2)}, u32[]{:S(2)}) collective-permute-start(bf16[1040,128]{1,0:T(8,128)(2,1)S(1)} %get-tuple-element.23), channel_id=1, source_target_pairs={{0,1},{1,2},{2,3},{3,7},{7,6},{6,5},{5,4},{4,8},{8,9},{9,10},{10,1... | collective-permute-start | bytes 798728 | tf_op jit(solution)/shard_map/ppermute | solution.py:246
  37.1 0.7 copy-start
  45.6 5.8 %collective-permute-start.7 = (bf16[4,256,128]{2,1,0:T(8,128)(2,1)S(1)}, bf16[4,256,128]{2,1,0:T(8,128)(2,1)S(1)}, u32[]{:S(2)}, u32[]{:S(2)}) collective-permute-start(bf16[4,256,128]{2,1,0:T(8,128)(2,1)S(1)} %get-tuple-element.28), channel_id=1, source_target_pairs={{0,4},{4,0},{1,5},{5,1},{2,6},{6,2},{3,7},{7,3},{8,12},{12,8},{9,1... | collective-permute-start | bytes 786440 | tf_op jit(solution)/shard_map/ppermute | solution.py:262

commit v6 on v5

--- a/solution.py
+++ b/solution.py
@@ -47,15 +47,12 @@
 
 def pack_kernel(wanted, pieces, *outs):
     for t in range(4):
-        outs[t][0] = pieces[wanted[t], 0, 1]
-        outs[t][1] = pieces[wanted[t], 1, 0]
-        outs[4][t, 0] = pieces[wanted[4 + t], 0, 0]
-        outs[4][t, 1] = pieces[wanted[4 + t], 1, 1]
+        outs[t][...] = pieces[wanted[t]]
 
 
 def local_kernel(place_of, table, partner, cells, *refs):
-    early, late, (keep, send, modes, z_image, c_image) = refs[:4], refs[4], refs[5:]
-    fields, block = late.shape[2], late.shape[3]
+    parts, (keep, send, modes, z_image, c_image) = refs[:4], refs[4:]
+    fields, block = parts[0].shape[2], parts[0].shape[3]
     planes = lax.broadcasted_iota(jnp.int32, (LANES, LANES), 0)
     pick = (planes == partner[...]).astype(F32).astype(BF16)
     speed_z, region = cells[0], cells[1]
@@ -69,12 +66,8 @@
                 coupling[f, g] = chosen
     for col in range(4):
         for t in range(4):
-            if col in (0, 3):
-                rows = slice(t * block, (t + 1) * block)
-                here = [late[t, col // 2, f] for f in range(fields)]
-            else:
-                rows = pl.ds(pl.multiple_of((place_of[1] ^ t) * block, block), block)
-                here = [early[t][col - 1, f] for f in range(fields)]
+            rows = pl.ds(pl.multiple_of((place_of[1] ^ t) * block, block), block)
+            here = [parts[t][col // 2, col % 2, f] for f in range(fields)]
             moved = jnp.dot(jnp.concatenate(here, axis=0), pick, preferred_element_type=F32)
             centre = [cells_f.astype(F32) for cells_f in here]
             for f in range(fields):
@@ -154,13 +147,13 @@
 
 def message_kernel(place_of, speeds, *refs):
     parts, messages = refs[:4], refs[4:]
-    fields, block = parts[0].shape[1], parts[0].shape[2]
+    fields, block = parts[0].shape[2], parts[0].shape[3]
     body = 4 * fields * block
     for number, message in enumerate(messages):
         for t in range(4):
             for f in range(fields):
                 start = ((place_of[1] ^ t) * fields + f) * block
-                message[pl.ds(pl.multiple_of(start, block), block), :] = parts[t][number, f]
+                message[pl.ds(pl.multiple_of(start, block), block), :] = parts[t][number, 1 - number, f]
         rows = []
         for axis in range(2):
             rest = speeds[4 * axis + 1 + number : 4 * axis + 2 + number, :]
@@ -184,24 +177,24 @@
     reverse = (gx // (gx_count // 2) + gy) % 2 == 1
     k = jnp.where(reverse, ma_count - 1 - ma, ma)
 
-    homes = jnp.stack([ma ^ t for t in range(ma_count)] + [jnp.asarray(m) for m in range(ma_count)])
+    homes = jnp.stack([ma ^ t for t in range(ma_count)])
     wanted = jnp.where(reverse, ma_count - 1 - homes, homes).astype(jnp.int32)
     vmem = pl.BlockSpec(memory_space=pltpu.VMEM)
     smem = pl.BlockSpec(memory_space=pltpu.SMEM)
     params = pltpu.CompilerParams(vmem_limit_bytes=40 * 2**20)
     pieces = jnp.transpose(pod_modes, (3, 2, 1, 0, 4)).reshape(ma_count, 2, cells_x, fields, block, planes)
-    piece = (2, fields, block, planes)
-    *early, late = pl.pallas_call(
+    piece = jax.ShapeDtypeStruct((2, cells_x, fields, block, planes), BF16)
+    parts = pl.pallas_call(
         pack_kernel,
-        out_shape=(jax.ShapeDtypeStruct(piece, BF16),) * ma_count + (jax.ShapeDtypeStruct((ma_count, *piece), BF16),),
+        out_shape=(piece,) * ma_count,
         in_specs=[smem, vmem],
-        out_specs=(vmem,) * (ma_count + 1),
+        out_specs=(vmem,) * ma_count,
         compiler_params=params,
         cost_estimate=pl.CostEstimate(flops=0, bytes_accessed=2 * 2**20, transcendentals=0),
     )(wanted, pieces)
+    parts = list(parts)
     for t in (2, 3, 1):
-        early[t] = lax.ppermute(early[t], "ma", [(i, i ^ t) for i in range(ma_count)])
-    late = lax.all_to_all(late, "ma", 0, 0)
+        parts[t] = lax.ppermute(parts[t], "ma", [(i, i ^ t) for i in range(ma_count)])
 
     def columns(part):
         return lax.dynamic_slice_in_dim(part, 2 * k, 2, 1).transpose(1, 0, 2).reshape(4, planes)
@@ -222,12 +215,12 @@
     zc_keep, zc_send, modes = pl.pallas_call(
         local_kernel,
         out_shape=(*sums(2), jax.ShapeDtypeStruct((kinds, width), BF16)),
-        in_specs=[smem, smem] + [vmem] * 7,
+        in_specs=[smem, smem] + [vmem] * 6,
         out_specs=(vmem, vmem, vmem),
         scratch_shapes=[wide, wide],
         compiler_params=params,
         cost_estimate=pl.CostEstimate(flops=2 * 2 * kinds * kinds * width, bytes_accessed=4 * 2**20, transcendentals=0),
-    )(place_of, coupling_table.reshape(-1, fields * fields), partner[None], cells, *early, late)
+    )(place_of, coupling_table.reshape(-1, fields * fields), partner[None], cells, *parts)
 
     rows = jax.ShapeDtypeStruct((4 * fields * block + 16, LANES), BF16)
     first, second = pl.pallas_call(
@@ -237,7 +230,7 @@
         out_specs=(vmem, vmem),
         compiler_params=params,
         cost_estimate=pl.CostEstimate(flops=0, bytes_accessed=2**20, transcendentals=0),
-    )(place_of, speeds, *early)
+    )(place_of, speeds, *parts)
 
     def along_x(part, step):
         return lax.ppermute(part, ("gx", "ma"), steps_along_x(shape, step))

time: 121 us -> 125 us (1.033)
  waiting for transfers between devices: 5.82 us -> 14.7 us
  starting transfers between devices: 34.8 us -> 31.3 us
    ppermute x3, waiting for transfers between devices: 1.36 us -> 12.1 us  [on_device(): lax.ppermute(parts[t], 'ma', [(i, i ^ t) for i in range(ma_count)])]
    all_to_all x1 -> x0, starting transfers between devices: 4.53 us -> none  [on_device(): late = lax.all_to_all(late, 'ma', 0, 0)]
    ppermute x2, starting transfers between devices: 3.37 us -> 6.41 us  [along_x(): return lax.ppermute(part, ('gx', 'ma'), steps_along_x(shape, step))]
    ppermute x1, starting transfers between devices: 4.67 us -> 2.59 us  [core_swap(): return lax.ppermute(part, 'core', [(i, 1 - i) for i in range(core_count)])]
    ppermute x2, waiting for transfers between devices: 2.87 us -> 1.45 us  [along_y(): return lax.ppermute(part, names, steps_along_y(shape, step))]
  transfers between devices with their start and end apart: 9 -> 8, of which waited for: 4 -> 4; matrix products, arithmetic and copies ran while one was open for 1% -> 1% of each run, Pallas kernels for 3% -> 2%
where the time goes in v6:
time: 125 us
  blocking collectives  67.5 us (54%)
  starting transfers between devices  31.3 us (25%)
  waiting for transfers between devices  14.7 us (12%)
  Pallas kernels  5.85 us (5%)
  local copies, waits for them, and re-layouts  4.07 us (3%)
    all_to_all x1, blocking collectives, on_device(): received = lax.all_to_all(both, ('ma', 'gx', 'y'), 0, 0)  40.7 us
    all_to_all x1, blocking collectives, on_device(): whole = lax.all_to_all(spread, ('core', 'gx', 'y'), 0, 0)  26.8 us
    ppermute x3, starting transfers between devices, on_device(): lax.ppermute(parts[t], 'ma', [(i, i ^ t) for i in range(ma_count)])  12.6 us
    ppermute x3, waiting for transfers between devices, on_device(): lax.ppermute(parts[t], 'ma', [(i, i ^ t) for i in range(ma_count)])  12.1 us
    ppermute x2, starting transfers between devices, along_y(): return lax.ppermute(part, names, steps_along_y(shape, step))  9.73 us
    ppermute x2, starting transfers between devices, along_x(): return lax.ppermute(part, ('gx', 'ma'), steps_along_x(shape, step))  6.41 us
    ppermute x1, starting transfers between devices, core_swap(): return lax.ppermute(part, 'core', [(i, 1 - i) for i in range(core_count)])  2.59 us
    pallas_call x1, Pallas kernels, on_device(): pl.pallas_call(local_kernel, out_shape=(*sums(2), jax.ShapeDtypeStruct((k...  2.55 us
  transfers between devices with their start and end apart: 8, of which 4 were waited for; matrix products, arithmetic and copies ran while one was open for 1% of the time, Pallas kernels for 2%

profile of v6, /device:TPU:1, one launch (start us, length us, event | category | flops | bytes accessed | tf_op | source)
XLA Modules:
  0.0 124.9 jit_solution(9848063328108624835)
XLA Ops:
  0.0 1.9 %copy.19 = bf16[8,2,4,64,128]{4,3,2,1,0:T(8,128)(2,1)S(1)} copy(bf16[8,2,4,64,128]{4,0,1,2,3:T(8,128)(2,1)} %bitcast.37) | data formatting | bytes 2097152 | tf_op jit(solution)/shard_map/transpose | solution.py:185
  1.9 0.1 broadcast_select_fusion.wanted
  2.0 0.6 shard_map.55
  2.6 4.8 %collective-permute-start = (bf16[2,2,4,64,128]{4,3,2,1,0:T(8,128)(2,1)S(1)}, bf16[2,2,4,64,128]{4,3,2,1,0:T(8,128)(2,1)S(1)}, u32[]{:S(2)}, u32[]{:S(2)}) collective-permute-start(bf16[2,2,4,64,128]{4,3,2,1,0:T(8,128)(2,1)S(1)} %get-tuple-element.17), channel_id=1, source_target_pairs={{0,1},{1,0},{2,3},{3,2},{4,5},{5,4},{6,7},{7,6},{8,9},{9,8},{10,11... | collective-permute-start | bytes 786440 | tf_op jit(solution)/shard_map/ppermute | solution.py:197
  7.5 5.8 %collective-permute-start.1 = (bf16[2,2,4,64,128]{4,3,2,1,0:T(8,128)(2,1)S(1)}, bf16[2,2,4,64,128]{4,3,2,1,0:T(8,128)(2,1)S(1)}, u32[]{:S(2)}, u32[]{:S(2)}) collective-permute-start(bf16[2,2,4,64,128]{4,3,2,1,0:T(8,128)(2,1)S(1)} %get-tuple-element.18), channel_id=1, source_target_pairs={{0,2},{1,3},{2,0},{3,1},{4,6},{5,7},{6,4},{7,5},{8,10},{9,11},{10,... | collective-permute-start | bytes 786440 | tf_op jit(solution)/shard_map/ppermute | solution.py:197
  13.3 1.9 %collective-permute-start.2 = (bf16[2,2,4,64,128]{4,3,2,1,0:T(8,128)(2,1)S(1)}, bf16[2,2,4,64,128]{4,3,2,1,0:T(8,128)(2,1)S(1)}, u32[]{:S(2)}, u32[]{:S(2)}) collective-permute-start(bf16[2,2,4,64,128]{4,3,2,1,0:T(8,128)(2,1)S(1)} %get-tuple-element.19), channel_id=1, source_target_pairs={{0,3},{1,2},{2,1},{3,0},{4,7},{5,6},{6,5},{7,4},{8,11},{9,10},{10,... | collective-permute-start | bytes 786440 | tf_op jit(solution)/shard_map/ppermute | solution.py:197
  15.2 0.0 copy-start.2
  15.3 0.6 copy-done.2
  15.9 0.1 copy.20.table
  16.0 0.1 pad_add_fusion.place_of
  16.1 0.0 collective-permute-done.refs_1_
  16.1 3.4 %collective-permute-done.1.refs_2_ = bf16[2,2,4,64,128]{4,3,2,1,0:T(8,128)(2,1)S(1)} collective-permute-done((bf16[2,2,4,64,128]{4,3,2,1,0:T(8,128)(2,1)S(1)}, bf16[2,2,4,64,128]{4,3,2,1,0:T(8,128)(2,1)S(1)}, u32[]{:S(2)}, u32[]{:S(2)}) %collective-permute-start.1) | collective-permute-done | bytes 262176 | tf_op jit(solution)/shard_map/ppermute | solution.py:197
  19.5 8.7 %collective-permute-done.2.refs_3_ = bf16[2,2,4,64,128]{4,3,2,1,0:T(8,128)(2,1)S(1)} collective-permute-done((bf16[2,2,4,64,128]{4,3,2,1,0:T(8,128)(2,1)S(1)}, bf16[2,2,4,64,128]{4,3,2,1,0:T(8,128)(2,1)S(1)}, u32[]{:S(2)}, u32[]{:S(2)}) %collective-permute-start.2) | collective-permute-done | bytes 262176 | tf_op jit(solution)/shard_map/ppermute | solution.py:197
  28.2 0.6 shard_map.57
  28.8 5.1 %collective-permute-start.4 = (bf16[1040,128]{1,0:T(8,128)(2,1)S(1)}, bf16[1040,128]{1,0:T(8,128)(2,1)S(1)}, u32[]{:S(2)}, u32[]{:S(2)}) collective-permute-start(bf16[1040,128]{1,0:T(8,128)(2,1)S(1)} %get-tuple-element.22), channel_id=1, source_target_pairs={{0,64},{1,65},{2,66},{3,67},{64,128},{65,129},{66,130},{67,131},{1... | collective-permute-start | bytes 798728 | tf_op jit(solution)/shard_map/ppermute | solution.py:236
  33.9 7.8 %collective-permute-start.5 = (bf16[1040,128]{1,0:T(8,128)(2,1)S(1)}, bf16[1040,128]{1,0:T(8,128)(2,1)S(1)}, u32[]{:S(2)}, u32[]{:S(2)}) collective-permute-start(bf16[1040,128]{1,0:T(8,128)(2,1)S(1)} %get-tuple-element.22), channel_id=1, source_target_pairs={{1,0},{2,1},{3,2},{7,3},{6,7},{5,6},{4,5},{8,4},{9,8},{10,9},{11,1... | collective-permute-start | bytes 798728 | tf_op jit(solution)/shard_map/ppermute | solution.py:239
  41.7 1.3 %collective-permute-start.3 = (bf16[1040,128]{1,0:T(8,128)(2,1)S(1)}, bf16[1040,128]{1,0:T(8,128)(2,1)S(1)}, u32[]{:S(2)}, u32[]{:S(2)}) collective-permute-start(bf16[1040,128]{1,0:T(8,128)(2,1)S(1)} %get-tuple-element.21), channel_id=1, source_target_pairs={{64,0},{65,1},{66,2},{67,3},{128,64},{129,65},{130,66},{131,67},{1... | collective-permute-start | bytes 798728 | tf_op jit(solution)/shard_map/ppermute | solution.py:236
  43.0 1.9 %collective-permute-start.6 = (bf16[1040,128]{1,0:T(8,128)(2,1)S(1)}, bf16[1040,128]{1,0:T(8,128)(2,1)S(1)}, u32[]{:S(2)}, u32[]{:S(2)}) collective-permute-start(bf16[1040,128]{1,0:T(8,128)(2,1)S(1)} %get-tuple-element.21), channel_id=1, source_target_pairs={{0,1},{1,2},{2,3},{3,7},{7,6},{6,5},{5,4},{4,8},{8,9},{9,10},{10,1... | collective-permute-start | bytes 798728 | tf_op jit(solution)/shard_map/ppermute | solution.py:239
  45.0 0.7 fusion
  45.7 0.6 copy-done
  46.4 2.6 %shard_map.56 = (f32[4,128,128]{2,1,0:T(8,128)S(1)}, bf16[4,128,128]{2,1,0:T(8,128)(2,1)S(1)}, bf16[256,2048]{1,0:T(8,128)(2,1)S(1)}) custom-call(s32[2]{0:T(128)S(1)} %pad_add_fusion.place_of, f32[8,16]{1,0:T(8,128)S(1)} %copy.20.table, s32[1,128]{1,0:T(1,128)S(1)} %bitcast.36, f32[2,4,128]{2,1,0:T(4,128)S(1)} %pad_maximum_fusion.1.cells, ...), custom_call_target="tpu_custom_call" | custom-call | flops 536870912 | bytes 4194304 | tf_op jit(solution)/shard_map/pallas_call | solution.py:215
  48.9 0.0 collective-permute-done.4.xl
  48.9 0.0 collective-permute-done.5.yr
  48.9 1.5 %collective-permute-done.6.yl = bf16[1040,128]{1,0:T(8,128)(2,1)S(1)} collective-permute-done((bf16[1040,128]{1,0:T(8,128)(2,1)S(1)}, bf16[1040,128]{1,0:T(8,128)(2,1)S(1)}, u32[]{:S(2)}, u32[]{:S(2)}) %collective-permute-start.6) | collective-permute-done | bytes 266272 | tf_op jit(solution)/shard_map/ppermute | solution.py:239
  50.4 2.1 %shard_map.58 = (f32[4,256,128]{2,1,0:T(8,128)S(1)}, bf16[4,256,128]{2,1,0:T(8,128)(2,1)S(1)}) custom-call(s32[2]{0:T(128)S(1)} %pad_add_fusion.place_of, f32[8,128]{1,0:T(8,128)S(1)} %pad_maximum_fusion.speeds, bf16[256,2048]{1,0:T(8,128)(2,1)S(1)} %get-tuple-element.20.modes, bf16[1040,128]{1,0:T(8,128)(2,1)S(1)} %collective-permute-done.3.xr, ...), custom_call_target="tpu_custom_call" | custom-call | flops 805306368 | bytes 6291456 | tf_op jit(solution)/shard_map/pallas_call | solution.py:244
  52.5 2.6 %collective-permute-start.7 = (bf16[4,256,128]{2,1,0:T(8,128)(2,1)S(1)}, bf16[4,256,128]{2,1,0:T(8,128)(2,1)S(1)}, u32[]{:S(2)}, u32[]{:S(2)}) collective-permute-start(bf16[4,256,128]{2,1,0:T(8,128)(2,1)S(1)} %get-tuple-element.26), channel_id=1, source_target_pairs={{0,4},{4,0},{1,5},{5,1},{2,6},{6,2},{3,7},{7,3},{8,12},{12,8},{9,1... | collective-permute-start | bytes 786440 | tf_op jit(solution)/shard_map/ppermute | solution.py:255
  55.1 1.1 collective-permute-done.7
  56.2 0.1 add_convert_fusion
  56.3 40.7 %all_to_all.10 = bf16[256,4,128]{2,1,0:T(4,128)(2,1)S(1)} all-to-all(bf16[256,4,128]{2,1,0:T(4,128)(2,1)S(1)} %bitcast.39), channel_id=1, replica_groups=mesh['gx'=8,'y'=8,'core'=2,'ma'=4] {'ma','gx','y'}, dimensions={0} | all-to-all | bytes 524288 | tf_op jit(solution)/shard_map/all_to_all | solution.py:259
  97.0 0.3 convert_reduce_fusion
  97.4 26.8 %all_to_all.11 = f32[128,4,128]{2,1,0:T(4,128)S(1)} all-to-all(f32[128,4,128]{2,1,0:T(4,128)S(1)} %broadcast_in_dim.10), channel_id=1, replica_groups=mesh['gx'=8,'y'=8,'core'=2,'ma'=4] {'core','gx','y'}, dimensions={0} | all-to-all | bytes 524288 | tf_op jit(solution)/shard_map/all_to_all | solution.py:262
  124.2 0.7 copy.24
  (15 shorter events, 0.1 us)
Async XLA Ops:
  2.0 13.2 %copy-start.1 = (f32[3,2,8,128]{3,2,1,0:T(8,128)S(1)}, f32[3,2,8,128]{3,2,1,0:T(8,128)}, u32[]{:S(2)}) copy-start(f32[3,2,8,128]{3,2,1,0:T(8,128)} %param.6) | copy-start | bytes 73732
  2.6 13.5 %collective-permute-start = (bf16[2,2,4,64,128]{4,3,2,1,0:T(8,128)(2,1)S(1)}, bf16[2,2,4,64,128]{4,3,2,1,0:T(8,128)(2,1)S(1)}, u32[]{:S(2)}, u32[]{:S(2)}) collective-permute-start(bf16[2,2,4,64,128]{4,3,2,1,0:T(8,128)(2,1)S(1)} %get-tuple-element.17), channel_id=1, source_target_pairs={{0,1},{1,0},{2,3},{3,2},{4,5},{5,4},{6,7},{7,6},{8,9},{9,8},{10,11... | collective-permute-start | bytes 786440 | tf_op jit(solution)/shard_map/ppermute | solution.py:197
  7.5 12.0 %collective-permute-start.1 = (bf16[2,2,4,64,128]{4,3,2,1,0:T(8,128)(2,1)S(1)}, bf16[2,2,4,64,128]{4,3,2,1,0:T(8,128)(2,1)S(1)}, u32[]{:S(2)}, u32[]{:S(2)}) collective-permute-start(bf16[2,2,4,64,128]{4,3,2,1,0:T(8,128)(2,1)S(1)} %get-tuple-element.18), channel_id=1, source_target_pairs={{0,2},{1,3},{2,0},{3,1},{4,6},{5,7},{6,4},{7,5},{8,10},{9,11},{10,... | collective-permute-start | bytes 786440 | tf_op jit(solution)/shard_map/ppermute | solution.py:197
  13.3 15.0 %collective-permute-start.2 = (bf16[2,2,4,64,128]{4,3,2,1,0:T(8,128)(2,1)S(1)}, bf16[2,2,4,64,128]{4,3,2,1,0:T(8,128)(2,1)S(1)}, u32[]{:S(2)}, u32[]{:S(2)}) collective-permute-start(bf16[2,2,4,64,128]{4,3,2,1,0:T(8,128)(2,1)S(1)} %get-tuple-element.19), channel_id=1, source_target_pairs={{0,3},{1,2},{2,1},{3,0},{4,7},{5,6},{6,5},{7,4},{8,11},{9,10},{10,... | collective-permute-start | bytes 786440 | tf_op jit(solution)/shard_map/ppermute | solution.py:197
  15.2 0.7 copy-start.2
  28.8 20.1 %collective-permute-start.4 = (bf16[1040,128]{1,0:T(8,128)(2,1)S(1)}, bf16[1040,128]{1,0:T(8,128)(2,1)S(1)}, u32[]{:S(2)}, u32[]{:S(2)}) collective-permute-start(bf16[1040,128]{1,0:T(8,128)(2,1)S(1)} %get-tuple-element.22), channel_id=1, source_target_pairs={{0,64},{1,65},{2,66},{3,67},{64,128},{65,129},{66,130},{67,131},{1... | collective-permute-start | bytes 798728 | tf_op jit(solution)/shard_map/ppermute | solution.py:236
  33.9 15.0 %collective-permute-start.5 = (bf16[1040,128]{1,0:T(8,128)(2,1)S(1)}, bf16[1040,128]{1,0:T(8,128)(2,1)S(1)}, u32[]{:S(2)}, u32[]{:S(2)}) collective-permute-start(bf16[1040,128]{1,0:T(8,128)(2,1)S(1)} %get-tuple-element.22), channel_id=1, source_target_pairs={{1,0},{2,1},{3,2},{7,3},{6,7},{5,6},{4,5},{8,4},{9,8},{10,9},{11,1... | collective-permute-start | bytes 798728 | tf_op jit(solution)/shard_map/ppermute | solution.py:239
  41.7 7.2 %collective-permute-start.3 = (bf16[1040,128]{1,0:T(8,128)(2,1)S(1)}, bf16[1040,128]{1,0:T(8,128)(2,1)S(1)}, u32[]{:S(2)}, u32[]{:S(2)}) collective-permute-start(bf16[1040,128]{1,0:T(8,128)(2,1)S(1)} %get-tuple-element.21), channel_id=1, source_target_pairs={{64,0},{65,1},{66,2},{67,3},{128,64},{129,65},{130,66},{131,67},{1... | collective-permute-start | bytes 798728 | tf_op jit(solution)/shard_map/ppermute | solution.py:236
  43.0 7.3 %collective-permute-start.6 = (bf16[1040,128]{1,0:T(8,128)(2,1)S(1)}, bf16[1040,128]{1,0:T(8,128)(2,1)S(1)}, u32[]{:S(2)}, u32[]{:S(2)}) collective-permute-start(bf16[1040,128]{1,0:T(8,128)(2,1)S(1)} %get-tuple-element.21), channel_id=1, source_target_pairs={{0,1},{1,2},{2,3},{3,7},{7,6},{6,5},{5,4},{4,8},{8,9},{9,10},{10,1... | collective-permute-start | bytes 798728 | tf_op jit(solution)/shard_map/ppermute | solution.py:239
  45.7 0.7 copy-start
  52.5 3.7 %collective-permute-start.7 = (bf16[4,256,128]{2,1,0:T(8,128)(2,1)S(1)}, bf16[4,256,128]{2,1,0:T(8,128)(2,1)S(1)}, u32[]{:S(2)}, u32[]{:S(2)}) collective-permute-start(bf16[4,256,128]{2,1,0:T(8,128)(2,1)S(1)} %get-tuple-element.26), channel_id=1, source_target_pairs={{0,4},{4,0},{1,5},{5,1},{2,6},{6,2},{3,7},{7,3},{8,12},{12,8},{9,1... | collective-permute-start | bytes 786440 | tf_op jit(solution)/shard_map/ppermute | solution.py:255

commit v7 on v6

--- a/solution.py
+++ b/solution.py
@@ -45,14 +45,8 @@
     ]
 
 
-def pack_kernel(wanted, pieces, *outs):
-    for t in range(4):
-        outs[t][...] = pieces[wanted[t]]
-
-
-def local_kernel(place_of, table, partner, cells, *refs):
-    parts, (keep, send, modes, z_image, c_image) = refs[:4], refs[4:]
-    fields, block = parts[0].shape[2], parts[0].shape[3]
+def local_kernel(core, table, partner, cells, a, keep, send, modes, z_image, c_image):
+    fields, block = a.shape[3], a.shape[4]
     planes = lax.broadcasted_iota(jnp.int32, (LANES, LANES), 0)
     pick = (planes == partner[...]).astype(F32).astype(BF16)
     speed_z, region = cells[0], cells[1]
@@ -65,9 +59,9 @@
                     chosen = jnp.where(region == float(number), table[number, f * fields + g], chosen)
                 coupling[f, g] = chosen
     for col in range(4):
-        for t in range(4):
-            rows = pl.ds(pl.multiple_of((place_of[1] ^ t) * block, block), block)
-            here = [parts[t][col // 2, col % 2, f] for f in range(fields)]
+        for j in range(4):
+            rows = slice(j * block, (j + 1) * block)
+            here = [a[j, col // 2, col % 2, f] for f in range(fields)]
             moved = jnp.dot(jnp.concatenate(here, axis=0), pick, preferred_element_type=F32)
             centre = [cells_f.astype(F32) for cells_f in here]
             for f in range(fields):
@@ -83,19 +77,19 @@
                 c_image[rows, chunk] = running.astype(BF16)
     for q, image in enumerate((z_image, c_image)):
         total = lax.dot_general(image[...], modes[...], CONTRACT_LAST, preferred_element_type=F32)
-        place(place_of, keep, send, q, total, block)
-
-
-def place(place_of, keep, send, q, total, block):
+        place(core, keep, send, q, total, block)
+
+
+def place(core, keep, send, q, total, block):
     for j in range(4):
         first = total[j * block : (j + 1) * block, :LANES]
         second = total[j * block : (j + 1) * block, LANES:]
         rows = slice(q * block, (q + 1) * block)
-        keep[j, rows, :] = jnp.where(place_of[0] == 0, first, second)
-        send[j, rows, :] = jnp.where(place_of[0] == 0, second, first).astype(BF16)
-
-
-def edge_kernel(place_of, speeds, modes, xr, xl, yr, yl, zc_keep, zc_send, keep, send, x_image, x_edge, x_side, y_image, y_edge, y_side):
+        keep[j, rows, :] = jnp.where(core[0] == 0, first, second)
+        send[j, rows, :] = jnp.where(core[0] == 0, second, first).astype(BF16)
+
+
+def edge_kernel(core, speeds, modes, xr, xl, yr, yl, zc_keep, zc_send, keep, send, x_image, x_edge, x_side, y_image, y_edge, y_side):
     fields, block = 4, modes.shape[0] // 4
     body = 4 * fields * block
     half_speeds = 0.5 * speeds[...]
@@ -140,20 +134,19 @@
     for q, (_, _, _, image, edge, side, _) in enumerate(axes):
         total = lax.dot_general(image[...], modes[...], CONTRACT_LAST, preferred_element_type=F32)
         total += lax.dot_general(edge[...], side[...], CONTRACT_LAST, preferred_element_type=F32)
-        place(place_of, keep, send, q, total, block)
+        place(core, keep, send, q, total, block)
     keep[:, 2 * block :, :] = zc_keep[...]
     send[:, 2 * block :, :] = zc_send[...]
 
 
-def message_kernel(place_of, speeds, *refs):
-    parts, messages = refs[:4], refs[4:]
-    fields, block = parts[0].shape[2], parts[0].shape[3]
+def message_kernel(speeds, a, *messages):
+    fields, block = a.shape[3], a.shape[4]
     body = 4 * fields * block
     for number, message in enumerate(messages):
-        for t in range(4):
+        for j in range(4):
             for f in range(fields):
-                start = ((place_of[1] ^ t) * fields + f) * block
-                message[pl.ds(pl.multiple_of(start, block), block), :] = parts[t][number, 1 - number, f]
+                start = (j * fields + f) * block
+                message[start : start + block, :] = a[j, number, 1 - number, f]
         rows = []
         for axis in range(2):
             rest = speeds[4 * axis + 1 + number : 4 * axis + 2 + number, :]
@@ -177,24 +170,11 @@
     reverse = (gx // (gx_count // 2) + gy) % 2 == 1
     k = jnp.where(reverse, ma_count - 1 - ma, ma)
 
-    homes = jnp.stack([ma ^ t for t in range(ma_count)])
-    wanted = jnp.where(reverse, ma_count - 1 - homes, homes).astype(jnp.int32)
     vmem = pl.BlockSpec(memory_space=pltpu.VMEM)
     smem = pl.BlockSpec(memory_space=pltpu.SMEM)
     params = pltpu.CompilerParams(vmem_limit_bytes=40 * 2**20)
     pieces = jnp.transpose(pod_modes, (3, 2, 1, 0, 4)).reshape(ma_count, 2, cells_x, fields, block, planes)
-    piece = jax.ShapeDtypeStruct((2, cells_x, fields, block, planes), BF16)
-    parts = pl.pallas_call(
-        pack_kernel,
-        out_shape=(piece,) * ma_count,
-        in_specs=[smem, vmem],
-        out_specs=(vmem,) * ma_count,
-        compiler_params=params,
-        cost_estimate=pl.CostEstimate(flops=0, bytes_accessed=2 * 2**20, transcendentals=0),
-    )(wanted, pieces)
-    parts = list(parts)
-    for t in (2, 3, 1):
-        parts[t] = lax.ppermute(parts[t], "ma", [(i, i ^ t) for i in range(ma_count)])
+    a = lax.all_to_all(jnp.where(reverse, pieces[::-1], pieces), "ma", 0, 0)
 
     def columns(part):
         return lax.dynamic_slice_in_dim(part, 2 * k, 2, 1).transpose(1, 0, 2).reshape(4, planes)
@@ -203,7 +183,7 @@
     cells = jnp.stack([columns(velocity[2]), columns(region.astype(F32))])
 
     speeds = jnp.concatenate([vx, vy])
-    place_of = jnp.stack([core, ma]).astype(jnp.int32)
+    core_here = core.astype(jnp.int32)[None]
     width = 4 * fields * planes
     wide = pltpu.VMEM((kinds, width), BF16)
     narrow = pltpu.VMEM((kinds, width // 2), BF16)
@@ -215,22 +195,22 @@
     zc_keep, zc_send, modes = pl.pallas_call(
         local_kernel,
         out_shape=(*sums(2), jax.ShapeDtypeStruct((kinds, width), BF16)),
-        in_specs=[smem, smem] + [vmem] * 6,
+        in_specs=[smem, smem] + [vmem] * 3,
         out_specs=(vmem, vmem, vmem),
         scratch_shapes=[wide, wide],
         compiler_params=params,
         cost_estimate=pl.CostEstimate(flops=2 * 2 * kinds * kinds * width, bytes_accessed=4 * 2**20, transcendentals=0),
-    )(place_of, coupling_table.reshape(-1, fields * fields), partner[None], cells, *parts)
+    )(core_here, coupling_table.reshape(-1, fields * fields), partner[None], cells, a)
 
     rows = jax.ShapeDtypeStruct((4 * fields * block + 16, LANES), BF16)
     first, second = pl.pallas_call(
         message_kernel,
         out_shape=(rows, rows),
-        in_specs=[smem] + [vmem] * 5,
+        in_specs=[vmem] * 2,
         out_specs=(vmem, vmem),
         compiler_params=params,
         cost_estimate=pl.CostEstimate(flops=0, bytes_accessed=2**20, transcendentals=0),
-    )(place_of, speeds, *parts)
+    )(speeds, a)
 
     def along_x(part, step):
         return lax.ppermute(part, ("gx", "ma"), steps_along_x(shape, step))
@@ -238,8 +218,8 @@
     def along_y(part, step):
         return lax.ppermute(part, names, steps_along_y(shape, step))
 
+    yr, yl = along_y(first, -1), along_y(second, 1)
     xr, xl = along_x(second, -1), along_x(first, 1)
-    yr, yl = along_y(first, -1), along_y(second, 1)
 
     keep, send = pl.pallas_call(
         edge_kernel,
@@ -249,7 +229,7 @@
         scratch_shapes=[wide, narrow, narrow, wide, narrow, narrow],
         compiler_params=params,
         cost_estimate=pl.CostEstimate(flops=2 * 3 * kinds * kinds * width, bytes_accessed=6 * 2**20, transcendentals=0),
-    )(place_of, speeds, modes, xr, xl, yr, yl, zc_keep, zc_send)
+    )(core_here, speeds, modes, xr, xl, yr, yl, zc_keep, zc_send)
 
     def core_swap(part):
         return lax.ppermute(part, "core", [(i, 1 - i) for i in range(core_count)])

time: 125 us -> 128 us (1.024)
  waiting for transfers between devices: 14.7 us -> 26.7 us
  starting transfers between devices: 31.3 us -> 21.6 us
  Pallas kernels: 5.85 us -> 3.84 us
  blocking collectives: 67.5 us -> 69 us
    all_to_all x0 -> x1, waiting for transfers between devices: none -> 25.1 us  [on_device(): a = lax.all_to_all(jnp.where(reverse, pieces[::-1], pieces), 'ma', 0, 0)]
    ppermute x3 -> x0, starting transfers between devices: 12.6 us -> none  [on_device(): lax.ppermute(parts[t], 'ma', [(i, i ^ t) for i in range(ma_count)])]
    ppermute x3 -> x0, waiting for transfers between devices: 12.1 us -> none  [on_device(): lax.ppermute(parts[t], 'ma', [(i, i ^ t) for i in range(ma_count)])]
    all_to_all x0 -> x1, starting transfers between devices: none -> 7.94 us  [on_device(): a = lax.all_to_all(jnp.where(reverse, pieces[::-1], pieces), 'ma', 0, 0)]
    ppermute x2, starting transfers between devices: 9.73 us -> 6.74 us  [along_y(): return lax.ppermute(part, names, steps_along_y(shape, step))]
    ppermute x2, starting transfers between devices: 6.41 us -> 4.43 us  [along_x(): return lax.ppermute(part, ('gx', 'ma'), steps_along_x(shape, step))]
    all_to_all x1, blocking collectives: 40.7 us -> 42.2 us  [on_device(): received = lax.all_to_all(both, ('ma', 'gx', 'y'), 0, 0)]
  transfers between devices with their start and end apart: 8 -> 6, of which waited for: 4 -> 3; matrix products, arithmetic and copies ran while one was open for 1% -> 1% of each run, Pallas kernels for 2% -> 2%
where the time goes in v7:
time: 128 us; the launch traced here: 127 us
  blocking collectives  69 us (54%)
  waiting for transfers between devices  26.7 us (21%)
  starting transfers between devices  21.6 us (17%)
  Pallas kernels  3.84 us (3%)
  local copies, waits for them, and re-layouts  3.43 us (3%)
  other arithmetic  2.38 us (2%)
    all_to_all x1, blocking collectives, on_device(): received = lax.all_to_all(both, ('ma', 'gx', 'y'), 0, 0)  42.2 us
    all_to_all x1, blocking collectives, on_device(): whole = lax.all_to_all(spread, ('core', 'gx', 'y'), 0, 0)  26.8 us
    all_to_all x1, waiting for transfers between devices, on_device(): a = lax.all_to_all(jnp.where(reverse, pieces[::-1], pieces), 'ma', 0, 0)  25.1 us
    all_to_all x1, starting transfers between devices, on_device(): a = lax.all_to_all(jnp.where(reverse, pieces[::-1], pieces), 'ma', 0, 0)  7.94 us
    ppermute x2, starting transfers between devices, along_y(): return lax.ppermute(part, names, steps_along_y(shape, step))  6.74 us
    ppermute x2, starting transfers between devices, along_x(): return lax.ppermute(part, ('gx', 'ma'), steps_along_x(shape, step))  4.43 us
  transfers between devices with their start and end apart: 6, of which 3 were waited for; matrix products, arithmetic and copies ran while one was open for 1% of the time, Pallas kernels for 2%

profile of v7, /device:TPU:1, one launch (start us, length us, event | category | flops | bytes accessed | tf_op | source)
XLA Modules:
  0.0 127.1 jit_solution(14529099234403099208)
XLA Ops:
  0.0 1.9 %copy.19 = bf16[8,2,4,64,128]{4,3,2,1,0:T(8,128)(2,1)S(1)} copy(bf16[8,2,4,64,128]{4,0,1,2,3:T(8,128)(2,1)} %bitcast.33) | data formatting | bytes 2097152 | tf_op jit(solution)/shard_map/transpose | solution.py:176
  1.9 1.3 %reverse_select_fusion = bf16[4,2,2,4,64,128]{5,4,3,2,1,0:T(8,128)(2,1)} fusion(bf16[4,2,2,4,64,128]{5,4,3,2,1,0:T(8,128)(2,1)S(1)} %bitcast.32, pred[]{:T(512)S(6)} %eq.5), kind=kLoop, calls=%fused_computation | loop fusion | flops 524288 | bytes 2097153 | tf_op jit(solution)/shard_map/jit(_where)/select_n | solution.py:177
  3.2 0.0 copy-start.1
  3.2 7.9 %all-to-all-start = ((bf16[4,2,2,4,64,128]{5,4,3,2,1,0:T(8,128)(2,1)}), bf16[4,2,2,4,64,128]{5,4,3,2,1,0:T(8,128)(2,1)S(1)}, u32[]{:S(2)}, u32[]{:S(2)}) async-start(bf16[4,2,2,4,64,128]{5,4,3,2,1,0:T(8,128)(2,1)} %reverse_select_fusion), calls=%async_computation | async-start | bytes 2097152 | tf_op jit(solution)/shard_map/all_to_all | solution.py:177
  11.2 0.0 copy-done.1
  11.3 25.1 %all-to-all-done.a = bf16[4,2,2,4,64,128]{5,4,3,2,1,0:T(8,128)(2,1)S(1)} async-done(((bf16[4,2,2,4,64,128]{5,4,3,2,1,0:T(8,128)(2,1)}), bf16[4,2,2,4,64,128]{5,4,3,2,1,0:T(8,128)(2,1)S(1)}, u32[]{:S(2)}, u32[]{:S(2)}) %all-to-all-start) | async-done | bytes 1048608 | tf_op jit(solution)/shard_map/all_to_all | solution.py:177
  36.4 0.0 copy-start.2
  36.4 3.1 %collective-permute-start.1 = (bf16[1040,128]{1,0:T(8,128)(2,1)S(1)}, bf16[1040,128]{1,0:T(8,128)(2,1)S(1)}, u32[]{:S(2)}, u32[]{:S(2)}) collective-permute-start(bf16[1040,128]{1,0:T(8,128)(2,1)S(1)} %get-tuple-element.14), channel_id=1, source_target_pairs={{0,64},{1,65},{2,66},{3,67},{64,128},{65,129},{66,130},{67,131},{1... | collective-permute-start | bytes 798728 | tf_op jit(solution)/shard_map/ppermute | solution.py:216
  39.6 1.9 %collective-permute-start.2 = (bf16[1040,128]{1,0:T(8,128)(2,1)S(1)}, bf16[1040,128]{1,0:T(8,128)(2,1)S(1)}, u32[]{:S(2)}, u32[]{:S(2)}) collective-permute-start(bf16[1040,128]{1,0:T(8,128)(2,1)S(1)} %get-tuple-element.14), channel_id=1, source_target_pairs={{1,0},{2,1},{3,2},{7,3},{6,7},{5,6},{4,5},{8,4},{9,8},{10,9},{11,1... | collective-permute-start | bytes 798728 | tf_op jit(solution)/shard_map/ppermute | solution.py:219
  41.5 1.3 %collective-permute-start = (bf16[1040,128]{1,0:T(8,128)(2,1)S(1)}, bf16[1040,128]{1,0:T(8,128)(2,1)S(1)}, u32[]{:S(2)}, u32[]{:S(2)}) collective-permute-start(bf16[1040,128]{1,0:T(8,128)(2,1)S(1)} %get-tuple-element.13), channel_id=1, source_target_pairs={{64,0},{65,1},{66,2},{67,3},{128,64},{129,65},{130,66},{131,67},{1... | collective-permute-start | bytes 798728 | tf_op jit(solution)/shard_map/ppermute | solution.py:216
  42.8 4.8 %collective-permute-start.3 = (bf16[1040,128]{1,0:T(8,128)(2,1)S(1)}, bf16[1040,128]{1,0:T(8,128)(2,1)S(1)}, u32[]{:S(2)}, u32[]{:S(2)}) collective-permute-start(bf16[1040,128]{1,0:T(8,128)(2,1)S(1)} %get-tuple-element.13), channel_id=1, source_target_pairs={{0,1},{1,2},{2,3},{3,7},{7,6},{6,5},{5,4},{4,8},{8,9},{9,10},{10,1... | collective-permute-start | bytes 798728 | tf_op jit(solution)/shard_map/ppermute | solution.py:219
  47.6 0.7 fusion
  48.4 0.0 copy-done.2
  48.4 0.1 copy.20.table
  48.4 0.0 copy-start
  48.4 0.7 copy-done
  49.1 2.2 %shard_map.55 = (f32[4,128,128]{2,1,0:T(8,128)S(1)}, bf16[4,128,128]{2,1,0:T(8,128)(2,1)S(1)}, bf16[256,2048]{1,0:T(8,128)(2,1)S(1)}) custom-call(s32[1]{0:T(128)} %bitcast.core, f32[8,16]{1,0:T(8,128)S(1)} %copy.20.table, s32[1,128]{1,0:T(1,128)S(1)} %bitcast.31, f32[2,4,128]{2,1,0:T(4,128)S(1)} %pad_maximum_fusion.1.cells, ...), custom_call_target="tpu_custom_call" | custom-call | flops 536870912 | bytes 4194304 | tf_op jit(solution)/shard_map/pallas_call | solution.py:195
  51.3 0.0 collective-permute-done.xr
  51.3 0.0 collective-permute-done.1.xl
  51.4 0.0 collective-permute-done.2.yr
  51.4 0.5 collective-permute-done.3.yl
  51.8 1.6 %shard_map.57 = (f32[4,256,128]{2,1,0:T(8,128)S(1)}, bf16[4,256,128]{2,1,0:T(8,128)(2,1)S(1)}) custom-call(s32[1]{0:T(128)} %bitcast.core, f32[8,128]{1,0:T(8,128)S(1)} %pad_maximum_fusion.speeds, bf16[256,2048]{1,0:T(8,128)(2,1)S(1)} %get-tuple-element.12.modes, bf16[1040,128]{1,0:T(8,128)(2,1)S(1)} %collective-permute-done.xr, ...), custom_call_target="tpu_custom_call" | custom-call | flops 805306368 | bytes 6291456 | tf_op jit(solution)/shard_map/pallas_call | solution.py:224
  53.4 2.5 %collective-permute-start.4 = (bf16[4,256,128]{2,1,0:T(8,128)(2,1)S(1)}, bf16[4,256,128]{2,1,0:T(8,128)(2,1)S(1)}, u32[]{:S(2)}, u32[]{:S(2)}) collective-permute-start(bf16[4,256,128]{2,1,0:T(8,128)(2,1)S(1)} %get-tuple-element.18), channel_id=1, source_target_pairs={{0,4},{4,0},{1,5},{5,1},{2,6},{6,2},{3,7},{7,3},{8,12},{12,8},{9,1... | collective-permute-start | bytes 786440 | tf_op jit(solution)/shard_map/ppermute | solution.py:235
  55.9 1.1 collective-permute-done.4
  57.0 0.1 add_convert_fusion
  57.1 42.2 %all_to_all.15 = bf16[256,4,128]{2,1,0:T(4,128)(2,1)S(1)} all-to-all(bf16[256,4,128]{2,1,0:T(4,128)(2,1)S(1)} %bitcast.35), channel_id=1, replica_groups=mesh['gx'=8,'y'=8,'core'=2,'ma'=4] {'ma','gx','y'}, dimensions={0} | all-to-all | bytes 524288 | tf_op jit(solution)/shard_map/all_to_all | solution.py:239
  99.3 0.3 convert_reduce_fusion
  99.6 26.8 %all_to_all.16 = f32[128,4,128]{2,1,0:T(4,128)S(1)} all-to-all(f32[128,4,128]{2,1,0:T(4,128)S(1)} %broadcast_in_dim.14), channel_id=1, replica_groups=mesh['gx'=8,'y'=8,'core'=2,'ma'=4] {'core','gx','y'}, dimensions={0} | all-to-all | bytes 524288 | tf_op jit(solution)/shard_map/all_to_all | solution.py:242
  126.4 0.7 copy.24
  (12 shorter events, 0.1 us)
Async XLA Ops:
  3.2 7.9 %copy-start.1 = (f32[3,2,8,128]{3,2,1,0:T(8,128)S(1)}, f32[3,2,8,128]{3,2,1,0:T(8,128)}, u32[]{:S(2)}) copy-start(f32[3,2,8,128]{3,2,1,0:T(8,128)} %param.6) | copy-start | bytes 73732
  3.2 33.2 %all-to-all-start = ((bf16[4,2,2,4,64,128]{5,4,3,2,1,0:T(8,128)(2,1)}), bf16[4,2,2,4,64,128]{5,4,3,2,1,0:T(8,128)(2,1)S(1)}, u32[]{:S(2)}, u32[]{:S(2)}) async-start(bf16[4,2,2,4,64,128]{5,4,3,2,1,0:T(8,128)(2,1)} %reverse_select_fusion), calls=%async_computation | async-start | bytes 2097152 | tf_op jit(solution)/shard_map/all_to_all | solution.py:177
  36.4 11.9 %copy-start.2 = (f32[8,4,4]{0,2,1:T(4,128)S(1)}, f32[8,4,4]{0,2,1:T(4,128)}, u32[]{:S(2)}) copy-start(f32[8,4,4]{0,2,1:T(4,128)} %param.9) | copy-start | bytes 1540
  36.4 14.9 %collective-permute-start.1 = (bf16[1040,128]{1,0:T(8,128)(2,1)S(1)}, bf16[1040,128]{1,0:T(8,128)(2,1)S(1)}, u32[]{:S(2)}, u32[]{:S(2)}) collective-permute-start(bf16[1040,128]{1,0:T(8,128)(2,1)S(1)} %get-tuple-element.14), channel_id=1, source_target_pairs={{0,64},{1,65},{2,66},{3,67},{64,128},{65,129},{66,130},{67,131},{1... | collective-permute-start | bytes 798728 | tf_op jit(solution)/shard_map/ppermute | solution.py:216
  39.6 11.8 %collective-permute-start.2 = (bf16[1040,128]{1,0:T(8,128)(2,1)S(1)}, bf16[1040,128]{1,0:T(8,128)(2,1)S(1)}, u32[]{:S(2)}, u32[]{:S(2)}) collective-permute-start(bf16[1040,128]{1,0:T(8,128)(2,1)S(1)} %get-tuple-element.14), channel_id=1, source_target_pairs={{1,0},{2,1},{3,2},{7,3},{6,7},{5,6},{4,5},{8,4},{9,8},{10,9},{11,1... | collective-permute-start | bytes 798728 | tf_op jit(solution)/shard_map/ppermute | solution.py:219
  41.5 9.8 %collective-permute-start = (bf16[1040,128]{1,0:T(8,128)(2,1)S(1)}, bf16[1040,128]{1,0:T(8,128)(2,1)S(1)}, u32[]{:S(2)}, u32[]{:S(2)}) collective-permute-start(bf16[1040,128]{1,0:T(8,128)(2,1)S(1)} %get-tuple-element.13), channel_id=1, source_target_pairs={{64,0},{65,1},{66,2},{67,3},{128,64},{129,65},{130,66},{131,67},{1... | collective-permute-start | bytes 798728 | tf_op jit(solution)/shard_map/ppermute | solution.py:216
  42.8 9.0 %collective-permute-start.3 = (bf16[1040,128]{1,0:T(8,128)(2,1)S(1)}, bf16[1040,128]{1,0:T(8,128)(2,1)S(1)}, u32[]{:S(2)}, u32[]{:S(2)}) collective-permute-start(bf16[1040,128]{1,0:T(8,128)(2,1)S(1)} %get-tuple-element.13), channel_id=1, source_target_pairs={{0,1},{1,2},{2,3},{3,7},{7,6},{6,5},{5,4},{4,8},{8,9},{9,10},{10,1... | collective-permute-start | bytes 798728 | tf_op jit(solution)/shard_map/ppermute | solution.py:219
  48.4 0.7 copy-start
  53.4 3.6 %collective-permute-start.4 = (bf16[4,256,128]{2,1,0:T(8,128)(2,1)S(1)}, bf16[4,256,128]{2,1,0:T(8,128)(2,1)S(1)}, u32[]{:S(2)}, u32[]{:S(2)}) collective-permute-start(bf16[4,256,128]{2,1,0:T(8,128)(2,1)S(1)} %get-tuple-element.18), channel_id=1, source_target_pairs={{0,4},{4,0},{1,5},{5,1},{2,6},{6,2},{3,7},{7,3},{8,12},{12,8},{9,1... | collective-permute-start | bytes 786440 | tf_op jit(solution)/shard_map/ppermute | solution.py:235

commit v8 on v6

--- a/solution.py
+++ b/solution.py
@@ -47,12 +47,14 @@
 
 def pack_kernel(wanted, pieces, *outs):
     for t in range(4):
-        outs[t][...] = pieces[wanted[t]]
+        for number, (row, xi) in enumerate(((0, 1), (1, 0))):
+            outs[t][number] = pieces[wanted[t], row, xi]
+            outs[4 + t][number] = pieces[wanted[t], row, 1 - xi]
 
 
 def local_kernel(place_of, table, partner, cells, *refs):
-    parts, (keep, send, modes, z_image, c_image) = refs[:4], refs[4:]
-    fields, block = parts[0].shape[2], parts[0].shape[3]
+    early, late, (keep, send, modes, z_image, c_image) = refs[:4], refs[4:8], refs[8:]
+    fields, block = early[0].shape[1], early[0].shape[2]
     planes = lax.broadcasted_iota(jnp.int32, (LANES, LANES), 0)
     pick = (planes == partner[...]).astype(F32).astype(BF16)
     speed_z, region = cells[0], cells[1]
@@ -67,7 +69,8 @@
     for col in range(4):
         for t in range(4):
             rows = pl.ds(pl.multiple_of((place_of[1] ^ t) * block, block), block)
-            here = [parts[t][col // 2, col % 2, f] for f in range(fields)]
+            cell = (early if col in (1, 2) else late)[t]
+            here = [cell[col // 2, f] for f in range(fields)]
             moved = jnp.dot(jnp.concatenate(here, axis=0), pick, preferred_element_type=F32)
             centre = [cells_f.astype(F32) for cells_f in here]
             for f in range(fields):
@@ -147,13 +150,13 @@
 
 def message_kernel(place_of, speeds, *refs):
     parts, messages = refs[:4], refs[4:]
-    fields, block = parts[0].shape[2], parts[0].shape[3]
+    fields, block = parts[0].shape[1], parts[0].shape[2]
     body = 4 * fields * block
     for number, message in enumerate(messages):
         for t in range(4):
             for f in range(fields):
                 start = ((place_of[1] ^ t) * fields + f) * block
-                message[pl.ds(pl.multiple_of(start, block), block), :] = parts[t][number, 1 - number, f]
+                message[pl.ds(pl.multiple_of(start, block), block), :] = parts[t][number, f]
         rows = []
         for axis in range(2):
             rest = speeds[4 * axis + 1 + number : 4 * axis + 2 + number, :]
@@ -183,18 +186,23 @@
     smem = pl.BlockSpec(memory_space=pltpu.SMEM)
     params = pltpu.CompilerParams(vmem_limit_bytes=40 * 2**20)
     pieces = jnp.transpose(pod_modes, (3, 2, 1, 0, 4)).reshape(ma_count, 2, cells_x, fields, block, planes)
-    piece = jax.ShapeDtypeStruct((2, cells_x, fields, block, planes), BF16)
-    parts = pl.pallas_call(
+    piece = jax.ShapeDtypeStruct((2, fields, block, planes), BF16)
+    packed = pl.pallas_call(
         pack_kernel,
-        out_shape=(piece,) * ma_count,
+        out_shape=(piece,) * (2 * ma_count),
         in_specs=[smem, vmem],
-        out_specs=(vmem,) * ma_count,
+        out_specs=(vmem,) * (2 * ma_count),
         compiler_params=params,
         cost_estimate=pl.CostEstimate(flops=0, bytes_accessed=2 * 2**20, transcendentals=0),
     )(wanted, pieces)
-    parts = list(parts)
-    for t in (2, 3, 1):
-        parts[t] = lax.ppermute(parts[t], "ma", [(i, i ^ t) for i in range(ma_count)])
+
+    def collected(parts):
+        blocks = {0: parts[0]}
+        for t in (2, 3, 1):
+            blocks[t] = lax.ppermute(parts[t], "ma", [(i, i ^ t) for i in range(ma_count)])
+        return [blocks[t] for t in range(ma_count)]
+
+    early, late = collected(packed[:ma_count]), collected(packed[ma_count:])
 
     def columns(part):
         return lax.dynamic_slice_in_dim(part, 2 * k, 2, 1).transpose(1, 0, 2).reshape(4, planes)
@@ -215,12 +223,12 @@
     zc_keep, zc_send, modes = pl.pallas_call(
         local_kernel,
         out_shape=(*sums(2), jax.ShapeDtypeStruct((kinds, width), BF16)),
-        in_specs=[smem, smem] + [vmem] * 6,
+        in_specs=[smem, smem] + [vmem] * 10,
         out_specs=(vmem, vmem, vmem),
         scratch_shapes=[wide, wide],
         compiler_params=params,
         cost_estimate=pl.CostEstimate(flops=2 * 2 * kinds * kinds * width, bytes_accessed=4 * 2**20, transcendentals=0),
-    )(place_of, coupling_table.reshape(-1, fields * fields), partner[None], cells, *parts)
+    )(place_of, coupling_table.reshape(-1, fields * fields), partner[None], cells, *early, *late)
 
     rows = jax.ShapeDtypeStruct((4 * fields * block + 16, LANES), BF16)
     first, second = pl.pallas_call(
@@ -230,7 +238,7 @@
         out_specs=(vmem, vmem),
         compiler_params=params,
         cost_estimate=pl.CostEstimate(flops=0, bytes_accessed=2**20, transcendentals=0),
-    )(place_of, speeds, *parts)
+    )(place_of, speeds, *early)
 
     def along_x(part, step):
         return lax.ppermute(part, ("gx", "ma"), steps_along_x(shape, step))

time: 125 us -> 120 us (0.960)
  waiting for transfers between devices: 14.7 us -> 1.17 us
  starting transfers between devices: 31.3 us -> 40.3 us
    ppermute x3 -> x6, waiting for transfers between devices: 12.1 us -> 0.02 us  [collected(): lax.ppermute(parts[t], 'ma', [(i, i ^ t) for i in range(ma_count)])]
    ppermute x3 -> x6, starting transfers between devices: 12.6 us -> 21.8 us  [collected(): lax.ppermute(parts[t], 'ma', [(i, i ^ t) for i in range(ma_count)])]
    ppermute x1, starting transfers between devices: 2.59 us -> 5.69 us  [core_swap(): return lax.ppermute(part, 'core', [(i, 1 - i) for i in range(core_count)])]
    ppermute x2, starting transfers between devices: 6.41 us -> 4.42 us  [along_x(): return lax.ppermute(part, ('gx', 'ma'), steps_along_x(shape, step))]
    ppermute x2, waiting for transfers between devices: 1.45 us -> 0.01 us  [along_y(): return lax.ppermute(part, names, steps_along_y(shape, step))]
    ppermute x2, starting transfers between devices: 9.73 us -> 8.35 us  [along_y(): return lax.ppermute(part, names, steps_along_y(shape, step))]
  transfers between devices with their start and end apart: 8 -> 11, of which waited for: 4 -> 1; matrix products, arithmetic and copies ran while one was open for 1% -> 1% of each run, Pallas kernels for 2% -> 3%
where the time goes in v8:
time: 120 us; the launch traced here: 119 us
  blocking collectives  67.1 us (56%)
  starting transfers between devices  40.3 us (34%)
  Pallas kernels  5.84 us (5%)
  local copies, waits for them, and re-layouts  3.42 us (3%)
  other arithmetic  1.23 us (1%)
    all_to_all x1, blocking collectives, on_device(): received = lax.all_to_all(both, ('ma', 'gx', 'y'), 0, 0)  40.3 us
    all_to_all x1, blocking collectives, on_device(): whole = lax.all_to_all(spread, ('core', 'gx', 'y'), 0, 0)  26.8 us
    ppermute x6, starting transfers between devices, collected(): lax.ppermute(parts[t], 'ma', [(i, i ^ t) for i in range(ma_count)])  21.8 us
    ppermute x2, starting transfers between devices, along_y(): return lax.ppermute(part, names, steps_along_y(shape, step))  8.35 us
    ppermute x1, starting transfers between devices, core_swap(): return lax.ppermute(part, 'core', [(i, 1 - i) for i in range(core_count)])  5.69 us
    ppermute x2, starting transfers between devices, along_x(): return lax.ppermute(part, ('gx', 'ma'), steps_along_x(shape, step))  4.42 us
    pallas_call x1, Pallas kernels, on_device(): pl.pallas_call(local_kernel, out_shape=(*sums(2), jax.ShapeDtypeStruct((k...  2.55 us
  transfers between devices with their start and end apart: 11, of which 1 were waited for; matrix products, arithmetic and copies ran while one was open for 1% of the time, Pallas kernels for 3%

profile of v8, /device:TPU:1, one launch (start us, length us, event | category | flops | bytes accessed | tf_op | source)
XLA Modules:
  0.0 119.3 jit_solution(11261021490136199201)
XLA Ops:
  0.0 1.9 %copy.19 = bf16[8,2,4,64,128]{4,3,2,1,0:T(8,128)(2,1)S(1)} copy(bf16[8,2,4,64,128]{4,0,1,2,3:T(8,128)(2,1)} %bitcast.37) | data formatting | bytes 2097152 | tf_op jit(solution)/shard_map/transpose | solution.py:188
  1.9 0.1 broadcast_select_fusion.wanted
  2.0 0.6 shard_map.55
  2.6 4.8 %collective-permute-start = (bf16[2,4,64,128]{3,2,1,0:T(8,128)(2,1)S(1)}, bf16[2,4,64,128]{3,2,1,0:T(8,128)(2,1)S(1)}, u32[]{:S(2)}, u32[]{:S(2)}) collective-permute-start(bf16[2,4,64,128]{3,2,1,0:T(8,128)(2,1)S(1)} %get-tuple-element.21), channel_id=1, source_target_pairs={{0,1},{1,0},{2,3},{3,2},{4,5},{5,4},{6,7},{7,6},{8,9},{9,8},{10,11... | collective-permute-start | bytes 393224 | tf_op jit(solution)/shard_map/ppermute | solution.py:202
  7.5 5.8 %collective-permute-start.1 = (bf16[2,4,64,128]{3,2,1,0:T(8,128)(2,1)S(1)}, bf16[2,4,64,128]{3,2,1,0:T(8,128)(2,1)S(1)}, u32[]{:S(2)}, u32[]{:S(2)}) collective-permute-start(bf16[2,4,64,128]{3,2,1,0:T(8,128)(2,1)S(1)} %get-tuple-element.22), channel_id=1, source_target_pairs={{0,2},{1,3},{2,0},{3,1},{4,6},{5,7},{6,4},{7,5},{8,10},{9,11},{10,... | collective-permute-start | bytes 393224 | tf_op jit(solution)/shard_map/ppermute | solution.py:202
  13.3 1.9 %collective-permute-start.2 = (bf16[2,4,64,128]{3,2,1,0:T(8,128)(2,1)S(1)}, bf16[2,4,64,128]{3,2,1,0:T(8,128)(2,1)S(1)}, u32[]{:S(2)}, u32[]{:S(2)}) collective-permute-start(bf16[2,4,64,128]{3,2,1,0:T(8,128)(2,1)S(1)} %get-tuple-element.23), channel_id=1, source_target_pairs={{0,3},{1,2},{2,1},{3,0},{4,7},{5,6},{6,5},{7,4},{8,11},{9,10},{10,... | collective-permute-start | bytes 393224 | tf_op jit(solution)/shard_map/ppermute | solution.py:202
  15.2 2.2 %collective-permute-start.3 = (bf16[2,4,64,128]{3,2,1,0:T(8,128)(2,1)S(1)}, bf16[2,4,64,128]{3,2,1,0:T(8,128)(2,1)S(1)}, u32[]{:S(2)}, u32[]{:S(2)}) collective-permute-start(bf16[2,4,64,128]{3,2,1,0:T(8,128)(2,1)S(1)} %get-tuple-element.25), channel_id=1, source_target_pairs={{0,1},{1,0},{2,3},{3,2},{4,5},{5,4},{6,7},{7,6},{8,9},{9,8},{10,11... | collective-permute-start | bytes 393224 | tf_op jit(solution)/shard_map/ppermute | solution.py:202
  17.4 5.2 %collective-permute-start.4 = (bf16[2,4,64,128]{3,2,1,0:T(8,128)(2,1)S(1)}, bf16[2,4,64,128]{3,2,1,0:T(8,128)(2,1)S(1)}, u32[]{:S(2)}, u32[]{:S(2)}) collective-permute-start(bf16[2,4,64,128]{3,2,1,0:T(8,128)(2,1)S(1)} %get-tuple-element.26), channel_id=1, source_target_pairs={{0,2},{1,3},{2,0},{3,1},{4,6},{5,7},{6,4},{7,5},{8,10},{9,11},{10,... | collective-permute-start | bytes 393224 | tf_op jit(solution)/shard_map/ppermute | solution.py:202
  22.6 0.1 pad_add_fusion.place_of
  22.7 1.9 %collective-permute-start.5 = (bf16[2,4,64,128]{3,2,1,0:T(8,128)(2,1)S(1)}, bf16[2,4,64,128]{3,2,1,0:T(8,128)(2,1)S(1)}, u32[]{:S(2)}, u32[]{:S(2)}) collective-permute-start(bf16[2,4,64,128]{3,2,1,0:T(8,128)(2,1)S(1)} %get-tuple-element.27), channel_id=1, source_target_pairs={{0,3},{1,2},{2,1},{3,0},{4,7},{5,6},{6,5},{7,4},{8,11},{9,10},{10,... | collective-permute-start | bytes 393224 | tf_op jit(solution)/shard_map/ppermute | solution.py:202
  24.7 0.0 collective-permute-done.1.refs_2_
  24.7 0.6 shard_map.57
  25.3 0.0 copy-start.2
  25.3 3.1 %collective-permute-start.7 = (bf16[1040,128]{1,0:T(8,128)(2,1)S(1)}, bf16[1040,128]{1,0:T(8,128)(2,1)S(1)}, u32[]{:S(2)}, u32[]{:S(2)}) collective-permute-start(bf16[1040,128]{1,0:T(8,128)(2,1)S(1)} %get-tuple-element.30), channel_id=1, source_target_pairs={{0,64},{1,65},{2,66},{3,67},{64,128},{65,129},{66,130},{67,131},{1... | collective-permute-start | bytes 798728 | tf_op jit(solution)/shard_map/ppermute | solution.py:244
  28.4 3.2 %collective-permute-start.8 = (bf16[1040,128]{1,0:T(8,128)(2,1)S(1)}, bf16[1040,128]{1,0:T(8,128)(2,1)S(1)}, u32[]{:S(2)}, u32[]{:S(2)}) collective-permute-start(bf16[1040,128]{1,0:T(8,128)(2,1)S(1)} %get-tuple-element.30), channel_id=1, source_target_pairs={{1,0},{2,1},{3,2},{7,3},{6,7},{5,6},{4,5},{8,4},{9,8},{10,9},{11,1... | collective-permute-start | bytes 798728 | tf_op jit(solution)/shard_map/ppermute | solution.py:247
  31.6 0.0 collective-permute-done.3.refs_5_
  31.6 1.3 %collective-permute-start.6 = (bf16[1040,128]{1,0:T(8,128)(2,1)S(1)}, bf16[1040,128]{1,0:T(8,128)(2,1)S(1)}, u32[]{:S(2)}, u32[]{:S(2)}) collective-permute-start(bf16[1040,128]{1,0:T(8,128)(2,1)S(1)} %get-tuple-element.29), channel_id=1, source_target_pairs={{64,0},{65,1},{66,2},{67,3},{128,64},{129,65},{130,66},{131,67},{1... | collective-permute-start | bytes 798728 | tf_op jit(solution)/shard_map/ppermute | solution.py:244
  32.9 5.2 %collective-permute-start.9 = (bf16[1040,128]{1,0:T(8,128)(2,1)S(1)}, bf16[1040,128]{1,0:T(8,128)(2,1)S(1)}, u32[]{:S(2)}, u32[]{:S(2)}) collective-permute-start(bf16[1040,128]{1,0:T(8,128)(2,1)S(1)} %get-tuple-element.29), channel_id=1, source_target_pairs={{0,1},{1,2},{2,3},{3,7},{7,6},{6,5},{5,4},{4,8},{8,9},{9,10},{10,1... | collective-permute-start | bytes 798728 | tf_op jit(solution)/shard_map/ppermute | solution.py:247
  38.1 0.7 fusion
  38.8 0.1 copy.20.table
  38.9 0.0 collective-permute-done.5.refs_7_
  38.9 0.0 copy-start
  38.9 0.6 copy-done
  39.6 2.6 %shard_map.56 = (f32[4,128,128]{2,1,0:T(8,128)S(1)}, bf16[4,128,128]{2,1,0:T(8,128)(2,1)S(1)}, bf16[256,2048]{1,0:T(8,128)(2,1)S(1)}) custom-call(s32[2]{0:T(128)S(1)} %pad_add_fusion.place_of, f32[8,16]{1,0:T(8,128)S(1)} %copy.20.table, s32[1,128]{1,0:T(1,128)S(1)} %bitcast.36, f32[2,4,128]{2,1,0:T(4,128)S(1)} %pad_maximum_fusion.1.cells, ...), custom_call_target="tpu_custom_call" | custom-call | flops 536870912 | bytes 4194304 | tf_op jit(solution)/shard_map/pallas_call | solution.py:223
  42.2 2.1 %shard_map.58 = (f32[4,256,128]{2,1,0:T(8,128)S(1)}, bf16[4,256,128]{2,1,0:T(8,128)(2,1)S(1)}) custom-call(s32[2]{0:T(128)S(1)} %pad_add_fusion.place_of, f32[8,128]{1,0:T(8,128)S(1)} %pad_maximum_fusion.speeds, bf16[256,2048]{1,0:T(8,128)(2,1)S(1)} %get-tuple-element.28.modes, bf16[1040,128]{1,0:T(8,128)(2,1)S(1)} %collective-permute-done.6.xr, ...), custom_call_target="tpu_custom_call" | custom-call | flops 805306368 | bytes 6291456 | tf_op jit(solution)/shard_map/pallas_call | solution.py:252
  44.3 5.7 %collective-permute-start.10 = (bf16[4,256,128]{2,1,0:T(8,128)(2,1)S(1)}, bf16[4,256,128]{2,1,0:T(8,128)(2,1)S(1)}, u32[]{:S(2)}, u32[]{:S(2)}) collective-permute-start(bf16[4,256,128]{2,1,0:T(8,128)(2,1)S(1)} %get-tuple-element.34), channel_id=1, source_target_pairs={{0,4},{4,0},{1,5},{5,1},{2,6},{6,2},{3,7},{7,3},{8,12},{12,8},{9,1... | collective-permute-start | bytes 786440 | tf_op jit(solution)/shard_map/ppermute | solution.py:263
  50.0 1.1 collective-permute-done.10
  51.1 0.1 add_convert_fusion
  51.2 40.3 %all_to_all.10 = bf16[256,4,128]{2,1,0:T(4,128)(2,1)S(1)} all-to-all(bf16[256,4,128]{2,1,0:T(4,128)(2,1)S(1)} %bitcast.39), channel_id=1, replica_groups=mesh['gx'=8,'y'=8,'core'=2,'ma'=4] {'ma','gx','y'}, dimensions={0} | all-to-all | bytes 524288 | tf_op jit(solution)/shard_map/all_to_all | solution.py:267
  91.5 0.3 convert_reduce_fusion
  91.8 26.8 %all_to_all.11 = f32[128,4,128]{2,1,0:T(4,128)S(1)} all-to-all(f32[128,4,128]{2,1,0:T(4,128)S(1)} %broadcast_in_dim.10), channel_id=1, replica_groups=mesh['gx'=8,'y'=8,'core'=2,'ma'=4] {'core','gx','y'}, dimensions={0} | all-to-all | bytes 524288 | tf_op jit(solution)/shard_map/all_to_all | solution.py:270
  118.6 0.7 copy.24
  (21 shorter events, 0.1 us)
Async XLA Ops:
  2.0 20.6 %copy-start.1 = (f32[3,2,8,128]{3,2,1,0:T(8,128)S(1)}, f32[3,2,8,128]{3,2,1,0:T(8,128)}, u32[]{:S(2)}) copy-start(f32[3,2,8,128]{3,2,1,0:T(8,128)} %param.6) | copy-start | bytes 73732
  2.6 20.1 %collective-permute-start = (bf16[2,4,64,128]{3,2,1,0:T(8,128)(2,1)S(1)}, bf16[2,4,64,128]{3,2,1,0:T(8,128)(2,1)S(1)}, u32[]{:S(2)}, u32[]{:S(2)}) collective-permute-start(bf16[2,4,64,128]{3,2,1,0:T(8,128)(2,1)S(1)} %get-tuple-element.21), channel_id=1, source_target_pairs={{0,1},{1,0},{2,3},{3,2},{4,5},{5,4},{6,7},{7,6},{8,9},{9,8},{10,11... | collective-permute-start | bytes 393224 | tf_op jit(solution)/shard_map/ppermute | solution.py:202
  7.5 17.2 %collective-permute-start.1 = (bf16[2,4,64,128]{3,2,1,0:T(8,128)(2,1)S(1)}, bf16[2,4,64,128]{3,2,1,0:T(8,128)(2,1)S(1)}, u32[]{:S(2)}, u32[]{:S(2)}) collective-permute-start(bf16[2,4,64,128]{3,2,1,0:T(8,128)(2,1)S(1)} %get-tuple-element.22), channel_id=1, source_target_pairs={{0,2},{1,3},{2,0},{3,1},{4,6},{5,7},{6,4},{7,5},{8,10},{9,11},{10,... | collective-permute-start | bytes 393224 | tf_op jit(solution)/shard_map/ppermute | solution.py:202
  13.3 11.4 %collective-permute-start.2 = (bf16[2,4,64,128]{3,2,1,0:T(8,128)(2,1)S(1)}, bf16[2,4,64,128]{3,2,1,0:T(8,128)(2,1)S(1)}, u32[]{:S(2)}, u32[]{:S(2)}) collective-permute-start(bf16[2,4,64,128]{3,2,1,0:T(8,128)(2,1)S(1)} %get-tuple-element.23), channel_id=1, source_target_pairs={{0,3},{1,2},{2,1},{3,0},{4,7},{5,6},{6,5},{7,4},{8,11},{9,10},{10,... | collective-permute-start | bytes 393224 | tf_op jit(solution)/shard_map/ppermute | solution.py:202
  15.2 16.4 %collective-permute-start.3 = (bf16[2,4,64,128]{3,2,1,0:T(8,128)(2,1)S(1)}, bf16[2,4,64,128]{3,2,1,0:T(8,128)(2,1)S(1)}, u32[]{:S(2)}, u32[]{:S(2)}) collective-permute-start(bf16[2,4,64,128]{3,2,1,0:T(8,128)(2,1)S(1)} %get-tuple-element.25), channel_id=1, source_target_pairs={{0,1},{1,0},{2,3},{3,2},{4,5},{5,4},{6,7},{7,6},{8,9},{9,8},{10,11... | collective-permute-start | bytes 393224 | tf_op jit(solution)/shard_map/ppermute | solution.py:202
  17.4 15.5 %collective-permute-start.4 = (bf16[2,4,64,128]{3,2,1,0:T(8,128)(2,1)S(1)}, bf16[2,4,64,128]{3,2,1,0:T(8,128)(2,1)S(1)}, u32[]{:S(2)}, u32[]{:S(2)}) collective-permute-start(bf16[2,4,64,128]{3,2,1,0:T(8,128)(2,1)S(1)} %get-tuple-element.26), channel_id=1, source_target_pairs={{0,2},{1,3},{2,0},{3,1},{4,6},{5,7},{6,4},{7,5},{8,10},{9,11},{10,... | collective-permute-start | bytes 393224 | tf_op jit(solution)/shard_map/ppermute | solution.py:202
  22.7 16.2 %collective-permute-start.5 = (bf16[2,4,64,128]{3,2,1,0:T(8,128)(2,1)S(1)}, bf16[2,4,64,128]{3,2,1,0:T(8,128)(2,1)S(1)}, u32[]{:S(2)}, u32[]{:S(2)}) collective-permute-start(bf16[2,4,64,128]{3,2,1,0:T(8,128)(2,1)S(1)} %get-tuple-element.27), channel_id=1, source_target_pairs={{0,3},{1,2},{2,1},{3,0},{4,7},{5,6},{6,5},{7,4},{8,11},{9,10},{10,... | collective-permute-start | bytes 393224 | tf_op jit(solution)/shard_map/ppermute | solution.py:202
  25.3 13.6 %copy-start.2 = (f32[8,4,4]{0,2,1:T(4,128)S(1)}, f32[8,4,4]{0,2,1:T(4,128)}, u32[]{:S(2)}) copy-start(f32[8,4,4]{0,2,1:T(4,128)} %param.9) | copy-start | bytes 1540
  25.3 16.9 %collective-permute-start.7 = (bf16[1040,128]{1,0:T(8,128)(2,1)S(1)}, bf16[1040,128]{1,0:T(8,128)(2,1)S(1)}, u32[]{:S(2)}, u32[]{:S(2)}) collective-permute-start(bf16[1040,128]{1,0:T(8,128)(2,1)S(1)} %get-tuple-element.30), channel_id=1, source_target_pairs={{0,64},{1,65},{2,66},{3,67},{64,128},{65,129},{66,130},{67,131},{1... | collective-permute-start | bytes 798728 | tf_op jit(solution)/shard_map/ppermute | solution.py:244
  28.4 13.7 %collective-permute-start.8 = (bf16[1040,128]{1,0:T(8,128)(2,1)S(1)}, bf16[1040,128]{1,0:T(8,128)(2,1)S(1)}, u32[]{:S(2)}, u32[]{:S(2)}) collective-permute-start(bf16[1040,128]{1,0:T(8,128)(2,1)S(1)} %get-tuple-element.30), channel_id=1, source_target_pairs={{1,0},{2,1},{3,2},{7,3},{6,7},{5,6},{4,5},{8,4},{9,8},{10,9},{11,1... | collective-permute-start | bytes 798728 | tf_op jit(solution)/shard_map/ppermute | solution.py:247
  31.6 10.5 %collective-permute-start.6 = (bf16[1040,128]{1,0:T(8,128)(2,1)S(1)}, bf16[1040,128]{1,0:T(8,128)(2,1)S(1)}, u32[]{:S(2)}, u32[]{:S(2)}) collective-permute-start(bf16[1040,128]{1,0:T(8,128)(2,1)S(1)} %get-tuple-element.29), channel_id=1, source_target_pairs={{64,0},{65,1},{66,2},{67,3},{128,64},{129,65},{130,66},{131,67},{1... | collective-permute-start | bytes 798728 | tf_op jit(solution)/shard_map/ppermute | solution.py:244
  32.9 9.2 %collective-permute-start.9 = (bf16[1040,128]{1,0:T(8,128)(2,1)S(1)}, bf16[1040,128]{1,0:T(8,128)(2,1)S(1)}, u32[]{:S(2)}, u32[]{:S(2)}) collective-permute-start(bf16[1040,128]{1,0:T(8,128)(2,1)S(1)} %get-tuple-element.29), channel_id=1, source_target_pairs={{0,1},{1,2},{2,3},{3,7},{7,6},{6,5},{5,4},{4,8},{8,9},{9,10},{10,1... | collective-permute-start | bytes 798728 | tf_op jit(solution)/shard_map/ppermute | solution.py:247
  38.9 0.7 copy-start
  44.3 6.8 %collective-permute-start.10 = (bf16[4,256,128]{2,1,0:T(8,128)(2,1)S(1)}, bf16[4,256,128]{2,1,0:T(8,128)(2,1)S(1)}, u32[]{:S(2)}, u32[]{:S(2)}) collective-permute-start(bf16[4,256,128]{2,1,0:T(8,128)(2,1)S(1)} %get-tuple-element.34), channel_id=1, source_target_pairs={{0,4},{4,0},{1,5},{5,1},{2,6},{6,2},{3,7},{7,3},{8,12},{12,8},{9,1... | collective-permute-start | bytes 786440 | tf_op jit(solution)/shard_map/ppermute | solution.py:263

commit v9 on v8

--- a/solution.py
+++ b/solution.py
@@ -52,12 +52,12 @@
             outs[4 + t][number] = pieces[wanted[t], row, 1 - xi]
 
 
-def local_kernel(place_of, table, partner, cells, *refs):
+def local_kernel(place_of, table, cells, *refs):
     early, late, (keep, send, modes, z_image, c_image) = refs[:4], refs[4:8], refs[8:]
     fields, block = early[0].shape[1], early[0].shape[2]
-    planes = lax.broadcasted_iota(jnp.int32, (LANES, LANES), 0)
-    pick = (planes == partner[...]).astype(F32).astype(BF16)
-    speed_z, region = cells[0], cells[1]
+    planes = lax.broadcasted_iota(jnp.int32, (LANES, LANES), 0).astype(F32)
+    speed_z, region, partner = cells[:4, :], cells[4:8, :], cells[8:9, :]
+    pick = (planes == partner).astype(F32).astype(BF16)
     coupling = {}
     for f in range(fields):
         for g in range(fields):
@@ -148,7 +148,7 @@
     send[:, 2 * block :, :] = zc_send[...]
 
 
-def message_kernel(place_of, speeds, *refs):
+def message_kernel(place_of, speeds, cells, *refs):
     parts, messages = refs[:4], refs[4:]
     fields, block = parts[0].shape[1], parts[0].shape[2]
     body = 4 * fields * block
@@ -208,7 +208,8 @@
         return lax.dynamic_slice_in_dim(part, 2 * k, 2, 1).transpose(1, 0, 2).reshape(4, planes)
 
     vx, vy = columns(velocity[0]), columns(velocity[1])
-    cells = jnp.stack([columns(velocity[2]), columns(region.astype(F32))])
+    partners = jnp.broadcast_to(partner.astype(F32)[None], (8, planes))
+    cells = jnp.concatenate([columns(velocity[2]), columns(region.astype(F32)), partners])
 
     speeds = jnp.concatenate([vx, vy])
     place_of = jnp.stack([core, ma]).astype(jnp.int32)
@@ -223,22 +224,22 @@
     zc_keep, zc_send, modes = pl.pallas_call(
         local_kernel,
         out_shape=(*sums(2), jax.ShapeDtypeStruct((kinds, width), BF16)),
-        in_specs=[smem, smem] + [vmem] * 10,
+        in_specs=[smem, smem] + [vmem] * 9,
         out_specs=(vmem, vmem, vmem),
         scratch_shapes=[wide, wide],
         compiler_params=params,
         cost_estimate=pl.CostEstimate(flops=2 * 2 * kinds * kinds * width, bytes_accessed=4 * 2**20, transcendentals=0),
-    )(place_of, coupling_table.reshape(-1, fields * fields), partner[None], cells, *early, *late)
+    )(place_of, coupling_table.reshape(-1, fields * fields), cells, *early, *late)
 
     rows = jax.ShapeDtypeStruct((4 * fields * block + 16, LANES), BF16)
     first, second = pl.pallas_call(
         message_kernel,
         out_shape=(rows, rows),
-        in_specs=[smem] + [vmem] * 5,
+        in_specs=[smem] + [vmem] * 6,
         out_specs=(vmem, vmem),
         compiler_params=params,
         cost_estimate=pl.CostEstimate(flops=0, bytes_accessed=2**20, transcendentals=0),
-    )(place_of, speeds, *early)
+    )(place_of, speeds, cells, *early)
 
     def along_x(part, step):
         return lax.ppermute(part, ("gx", "ma"), steps_along_x(shape, step))
@@ -266,9 +267,9 @@
     both = (keep + core_swap(send).astype(F32)).astype(BF16).reshape(ma_count * shares, -1, LANES)
     received = lax.all_to_all(both, ("ma", "gx", "y"), 0, 0)
     share = jnp.sum(received.astype(F32), axis=0) * scaling
-    spread = jnp.broadcast_to(share[None], (shares * core_count,) + share.shape)
+    spread = jnp.broadcast_to(share.astype(BF16)[None], (shares * core_count,) + share.shape)
     whole = lax.all_to_all(spread, ("core", "gx", "y"), 0, 0)
-    return whole.reshape(core_count, 4, block, LANES).transpose(1, 0, 3, 2).reshape(4, kinds, block)
+    return whole.reshape(core_count, 4, block, LANES).transpose(1, 0, 3, 2).reshape(4, kinds, block).astype(F32)
 
 
 def solution(mesh):

time: 120 us -> 117 us (0.975)
  blocking collectives: 67.1 us -> 55.1 us
  waiting for transfers between devices: 1.17 us -> 9.82 us
    all_to_all x1, blocking collectives: 40.3 us -> 31.1 us  [on_device(): received = lax.all_to_all(both, ('ma', 'gx', 'y'), 0, 0)]
    ppermute x6, waiting for transfers between devices: 0.02 us -> 8.67 us  [collected(): lax.ppermute(parts[t], 'ma', [(i, i ^ t) for i in range(ma_count)])]
    all_to_all x1, blocking collectives: 26.8 us -> 24 us  [on_device(): whole = lax.all_to_all(spread, ('core', 'gx', 'y'), 0, 0)]
    ppermute x6, starting transfers between devices: 21.8 us -> 23.6 us  [collected(): lax.ppermute(parts[t], 'ma', [(i, i ^ t) for i in range(ma_count)])]
    ppermute x1, starting transfers between devices: 5.69 us -> 4.23 us  [core_swap(): return lax.ppermute(part, 'core', [(i, 1 - i) for i in range(core_count)])]
  transfers between devices with their start and end apart: 11 -> 11, of which waited for: 1 -> 2; matrix products, arithmetic and copies ran while one was open for 1% -> 1% of each run, Pallas kernels for 3% -> 3%
where the time goes in v9:
time: 117 us; the launch traced here: 116 us
  blocking collectives  55.1 us (47%)
  starting transfers between devices  40.7 us (35%)
  waiting for transfers between devices  9.82 us (8%)
  Pallas kernels  5.85 us (5%)
  local copies, waits for them, and re-layouts  2.7 us (2%)
  other arithmetic  1.95 us (2%)
    all_to_all x1, blocking collectives, on_device(): received = lax.all_to_all(both, ('ma', 'gx', 'y'), 0, 0)  31.1 us
    all_to_all x1, blocking collectives, on_device(): whole = lax.all_to_all(spread, ('core', 'gx', 'y'), 0, 0)  24 us
    ppermute x6, starting transfers between devices, collected(): lax.ppermute(parts[t], 'ma', [(i, i ^ t) for i in range(ma_count)])  23.6 us
    ppermute x6, waiting for transfers between devices, collected(): lax.ppermute(parts[t], 'ma', [(i, i ^ t) for i in range(ma_count)])  8.67 us
    ppermute x2, starting transfers between devices, along_y(): return lax.ppermute(part, names, steps_along_y(shape, step))  7.65 us
    ppermute x2, starting transfers between devices, along_x(): return lax.ppermute(part, ('gx', 'ma'), steps_along_x(shape, step))  5.29 us
    ppermute x1, starting transfers between devices, core_swap(): return lax.ppermute(part, 'core', [(i, 1 - i) for i in range(core_count)])  4.23 us
    pallas_call x1, Pallas kernels, on_device(): pl.pallas_call(local_kernel, out_shape=(*sums(2), jax.ShapeDtypeStruct((k...  2.56 us
  transfers between devices with their start and end apart: 11, of which 2 were waited for; matrix products, arithmetic and copies ran while one was open for 1% of the time, Pallas kernels for 3%

profile of v9, /device:TPU:1, one launch (start us, length us, event | category | flops | bytes accessed | tf_op | source)
XLA Modules:
  0.0 116.4 jit_solution(2440198190355500216)
XLA Ops:
  0.0 1.9 %copy.19 = bf16[8,2,4,64,128]{4,3,2,1,0:T(8,128)(2,1)S(1)} copy(bf16[8,2,4,64,128]{4,0,1,2,3:T(8,128)(2,1)} %bitcast.36) | data formatting | bytes 2097152 | tf_op jit(solution)/shard_map/transpose | solution.py:188
  1.9 0.1 broadcast_select_fusion.wanted
  2.0 0.6 shard_map.55
  2.6 4.8 %collective-permute-start = (bf16[2,4,64,128]{3,2,1,0:T(8,128)(2,1)S(1)}, bf16[2,4,64,128]{3,2,1,0:T(8,128)(2,1)S(1)}, u32[]{:S(2)}, u32[]{:S(2)}) collective-permute-start(bf16[2,4,64,128]{3,2,1,0:T(8,128)(2,1)S(1)} %get-tuple-element.21), channel_id=1, source_target_pairs={{0,1},{1,0},{2,3},{3,2},{4,5},{5,4},{6,7},{7,6},{8,9},{9,8},{10,11... | collective-permute-start | bytes 393224 | tf_op jit(solution)/shard_map/ppermute | solution.py:202
  7.5 5.8 %collective-permute-start.1 = (bf16[2,4,64,128]{3,2,1,0:T(8,128)(2,1)S(1)}, bf16[2,4,64,128]{3,2,1,0:T(8,128)(2,1)S(1)}, u32[]{:S(2)}, u32[]{:S(2)}) collective-permute-start(bf16[2,4,64,128]{3,2,1,0:T(8,128)(2,1)S(1)} %get-tuple-element.22), channel_id=1, source_target_pairs={{0,2},{1,3},{2,0},{3,1},{4,6},{5,7},{6,4},{7,5},{8,10},{9,11},{10,... | collective-permute-start | bytes 393224 | tf_op jit(solution)/shard_map/ppermute | solution.py:202
  13.3 1.9 %collective-permute-start.2 = (bf16[2,4,64,128]{3,2,1,0:T(8,128)(2,1)S(1)}, bf16[2,4,64,128]{3,2,1,0:T(8,128)(2,1)S(1)}, u32[]{:S(2)}, u32[]{:S(2)}) collective-permute-start(bf16[2,4,64,128]{3,2,1,0:T(8,128)(2,1)S(1)} %get-tuple-element.23), channel_id=1, source_target_pairs={{0,3},{1,2},{2,1},{3,0},{4,7},{5,6},{6,5},{7,4},{8,11},{9,10},{10,... | collective-permute-start | bytes 393224 | tf_op jit(solution)/shard_map/ppermute | solution.py:202
  15.2 2.2 %collective-permute-start.3 = (bf16[2,4,64,128]{3,2,1,0:T(8,128)(2,1)S(1)}, bf16[2,4,64,128]{3,2,1,0:T(8,128)(2,1)S(1)}, u32[]{:S(2)}, u32[]{:S(2)}) collective-permute-start(bf16[2,4,64,128]{3,2,1,0:T(8,128)(2,1)S(1)} %get-tuple-element.25), channel_id=1, source_target_pairs={{0,1},{1,0},{2,3},{3,2},{4,5},{5,4},{6,7},{7,6},{8,9},{9,8},{10,11... | collective-permute-start | bytes 393224 | tf_op jit(solution)/shard_map/ppermute | solution.py:202
  17.4 5.2 %collective-permute-start.4 = (bf16[2,4,64,128]{3,2,1,0:T(8,128)(2,1)S(1)}, bf16[2,4,64,128]{3,2,1,0:T(8,128)(2,1)S(1)}, u32[]{:S(2)}, u32[]{:S(2)}) collective-permute-start(bf16[2,4,64,128]{3,2,1,0:T(8,128)(2,1)S(1)} %get-tuple-element.26), channel_id=1, source_target_pairs={{0,2},{1,3},{2,0},{3,1},{4,6},{5,7},{6,4},{7,5},{8,10},{9,11},{10,... | collective-permute-start | bytes 393224 | tf_op jit(solution)/shard_map/ppermute | solution.py:202
  22.6 0.0 copy-start.2
  22.7 0.6 copy-done.2
  23.3 0.7 fusion
  24.0 0.1 pad_add_fusion.place_of
  24.1 0.0 collective-permute-done.1.refs_2_
  24.1 0.0 collective-permute-done.2.refs_3_
  24.1 0.0 copy-start.1
  24.1 0.6 shard_map.57
  24.7 1.3 %collective-permute-start.6 = (bf16[1040,128]{1,0:T(8,128)(2,1)S(1)}, bf16[1040,128]{1,0:T(8,128)(2,1)S(1)}, u32[]{:S(2)}, u32[]{:S(2)}) collective-permute-start(bf16[1040,128]{1,0:T(8,128)(2,1)S(1)} %get-tuple-element.29), channel_id=1, source_target_pairs={{64,0},{65,1},{66,2},{67,3},{128,64},{129,65},{130,66},{131,67},{1... | collective-permute-start | bytes 798728 | tf_op jit(solution)/shard_map/ppermute | solution.py:245
  26.0 4.0 %collective-permute-start.7 = (bf16[1040,128]{1,0:T(8,128)(2,1)S(1)}, bf16[1040,128]{1,0:T(8,128)(2,1)S(1)}, u32[]{:S(2)}, u32[]{:S(2)}) collective-permute-start(bf16[1040,128]{1,0:T(8,128)(2,1)S(1)} %get-tuple-element.30), channel_id=1, source_target_pairs={{0,64},{1,65},{2,66},{3,67},{64,128},{65,129},{66,130},{67,131},{1... | collective-permute-start | bytes 798728 | tf_op jit(solution)/shard_map/ppermute | solution.py:245
  30.0 3.5 %collective-permute-start.8 = (bf16[1040,128]{1,0:T(8,128)(2,1)S(1)}, bf16[1040,128]{1,0:T(8,128)(2,1)S(1)}, u32[]{:S(2)}, u32[]{:S(2)}) collective-permute-start(bf16[1040,128]{1,0:T(8,128)(2,1)S(1)} %get-tuple-element.30), channel_id=1, source_target_pairs={{1,0},{2,1},{3,2},{7,3},{6,7},{5,6},{4,5},{8,4},{9,8},{10,9},{11,1... | collective-permute-start | bytes 798728 | tf_op jit(solution)/shard_map/ppermute | solution.py:248
  33.5 4.2 %collective-permute-start.9 = (bf16[1040,128]{1,0:T(8,128)(2,1)S(1)}, bf16[1040,128]{1,0:T(8,128)(2,1)S(1)}, u32[]{:S(2)}, u32[]{:S(2)}) collective-permute-start(bf16[1040,128]{1,0:T(8,128)(2,1)S(1)} %get-tuple-element.29), channel_id=1, source_target_pairs={{0,1},{1,2},{2,3},{3,7},{7,6},{6,5},{5,4},{4,8},{8,9},{9,10},{10,1... | collective-permute-start | bytes 798728 | tf_op jit(solution)/shard_map/ppermute | solution.py:248
  37.7 3.7 %collective-permute-start.5 = (bf16[2,4,64,128]{3,2,1,0:T(8,128)(2,1)S(1)}, bf16[2,4,64,128]{3,2,1,0:T(8,128)(2,1)S(1)}, u32[]{:S(2)}, u32[]{:S(2)}) collective-permute-start(bf16[2,4,64,128]{3,2,1,0:T(8,128)(2,1)S(1)} %get-tuple-element.27), channel_id=1, source_target_pairs={{0,3},{1,2},{2,1},{3,0},{4,7},{5,6},{6,5},{7,4},{8,11},{9,10},{10,... | collective-permute-start | bytes 393224 | tf_op jit(solution)/shard_map/ppermute | solution.py:202
  41.4 0.1 copy.20.table
  41.5 8.7 %collective-permute-done.5.refs_7_ = bf16[2,4,64,128]{3,2,1,0:T(8,128)(2,1)S(1)} collective-permute-done((bf16[2,4,64,128]{3,2,1,0:T(8,128)(2,1)S(1)}, bf16[2,4,64,128]{3,2,1,0:T(8,128)(2,1)S(1)}, u32[]{:S(2)}, u32[]{:S(2)}) %collective-permute-start.5) | collective-permute-done | bytes 131104 | tf_op jit(solution)/shard_map/ppermute | solution.py:202
  50.1 2.6 %shard_map.56 = (f32[4,128,128]{2,1,0:T(8,128)S(1)}, bf16[4,128,128]{2,1,0:T(8,128)(2,1)S(1)}, bf16[256,2048]{1,0:T(8,128)(2,1)S(1)}) custom-call(s32[2]{0:T(128)S(1)} %pad_add_fusion.place_of, f32[8,16]{1,0:T(8,128)S(1)} %copy.20.table, f32[16,128]{1,0:T(8,128)S(1)} %pad_maximum_fusion.cells, bf16[2,4,64,128]{3,2,1,0:T(8,128)(2,1)S(1)} %get-tuple-element.20.refs_0_, ...), custom_call_target="tpu_custom_call" | custom-call | flops 536870912 | bytes 4194304 | tf_op jit(solution)/shard_map/pallas_call | solution.py:224
  52.7 2.1 %shard_map.58 = (f32[4,256,128]{2,1,0:T(8,128)S(1)}, bf16[4,256,128]{2,1,0:T(8,128)(2,1)S(1)}) custom-call(s32[2]{0:T(128)S(1)} %pad_add_fusion.place_of, f32[8,128]{1,0:T(8,128)S(1)} %pad_maximum_fusion.1.speeds, bf16[256,2048]{1,0:T(8,128)(2,1)S(1)} %get-tuple-element.28.modes, bf16[1040,128]{1,0:T(8,128)(2,1)S(1)} %collective-permute-done.6.xr, ...), custom_call_target="tpu_custom_call" | custom-call | flops 805306368 | bytes 6291456 | tf_op jit(solution)/shard_map/pallas_call | solution.py:253
  54.8 4.2 %collective-permute-start.10 = (bf16[4,256,128]{2,1,0:T(8,128)(2,1)S(1)}, bf16[4,256,128]{2,1,0:T(8,128)(2,1)S(1)}, u32[]{:S(2)}, u32[]{:S(2)}) collective-permute-start(bf16[4,256,128]{2,1,0:T(8,128)(2,1)S(1)} %get-tuple-element.34), channel_id=1, source_target_pairs={{0,4},{4,0},{1,5},{5,1},{2,6},{6,2},{3,7},{7,3},{8,12},{12,8},{9,1... | collective-permute-start | bytes 786440 | tf_op jit(solution)/shard_map/ppermute | solution.py:264
  59.1 1.1 collective-permute-done.10
  60.2 0.1 add_convert_fusion
  60.3 31.1 %all_to_all.10 = bf16[256,4,128]{2,1,0:T(4,128)(2,1)S(1)} all-to-all(bf16[256,4,128]{2,1,0:T(4,128)(2,1)S(1)} %bitcast.37), channel_id=1, replica_groups=mesh['gx'=8,'y'=8,'core'=2,'ma'=4] {'ma','gx','y'}, dimensions={0} | all-to-all | bytes 524288 | tf_op jit(solution)/shard_map/all_to_all | solution.py:268
  91.4 0.3 convert_reduce_fusion
  91.7 24.0 %all_to_all.11 = bf16[128,4,128]{2,1,0:T(4,128)(2,1)S(1)} all-to-all(bf16[128,4,128]{2,1,0:T(4,128)(2,1)S(1)} %broadcast_in_dim.5), channel_id=1, replica_groups=mesh['gx'=8,'y'=8,'core'=2,'ma'=4] {'core','gx','y'}, dimensions={0} | all-to-all | bytes 262144 | tf_op jit(solution)/shard_map/all_to_all | solution.py:271
  115.7 0.7 copy_bitcast_fusion
  (23 shorter events, 0.1 us)
Async XLA Ops:
  2.0 20.6 %copy-start = (f32[3,2,8,128]{3,2,1,0:T(8,128)S(1)}, f32[3,2,8,128]{3,2,1,0:T(8,128)}, u32[]{:S(2)}) copy-start(f32[3,2,8,128]{3,2,1,0:T(8,128)} %param.6) | copy-start | bytes 73732
  2.6 21.5 %collective-permute-start = (bf16[2,4,64,128]{3,2,1,0:T(8,128)(2,1)S(1)}, bf16[2,4,64,128]{3,2,1,0:T(8,128)(2,1)S(1)}, u32[]{:S(2)}, u32[]{:S(2)}) collective-permute-start(bf16[2,4,64,128]{3,2,1,0:T(8,128)(2,1)S(1)} %get-tuple-element.21), channel_id=1, source_target_pairs={{0,1},{1,0},{2,3},{3,2},{4,5},{5,4},{6,7},{7,6},{8,9},{9,8},{10,11... | collective-permute-start | bytes 393224 | tf_op jit(solution)/shard_map/ppermute | solution.py:202
  7.5 16.7 %collective-permute-start.1 = (bf16[2,4,64,128]{3,2,1,0:T(8,128)(2,1)S(1)}, bf16[2,4,64,128]{3,2,1,0:T(8,128)(2,1)S(1)}, u32[]{:S(2)}, u32[]{:S(2)}) collective-permute-start(bf16[2,4,64,128]{3,2,1,0:T(8,128)(2,1)S(1)} %get-tuple-element.22), channel_id=1, source_target_pairs={{0,2},{1,3},{2,0},{3,1},{4,6},{5,7},{6,4},{7,5},{8,10},{9,11},{10,... | collective-permute-start | bytes 393224 | tf_op jit(solution)/shard_map/ppermute | solution.py:202
  13.3 10.9 %collective-permute-start.2 = (bf16[2,4,64,128]{3,2,1,0:T(8,128)(2,1)S(1)}, bf16[2,4,64,128]{3,2,1,0:T(8,128)(2,1)S(1)}, u32[]{:S(2)}, u32[]{:S(2)}) collective-permute-start(bf16[2,4,64,128]{3,2,1,0:T(8,128)(2,1)S(1)} %get-tuple-element.23), channel_id=1, source_target_pairs={{0,3},{1,2},{2,1},{3,0},{4,7},{5,6},{6,5},{7,4},{8,11},{9,10},{10,... | collective-permute-start | bytes 393224 | tf_op jit(solution)/shard_map/ppermute | solution.py:202
  15.2 18.3 %collective-permute-start.3 = (bf16[2,4,64,128]{3,2,1,0:T(8,128)(2,1)S(1)}, bf16[2,4,64,128]{3,2,1,0:T(8,128)(2,1)S(1)}, u32[]{:S(2)}, u32[]{:S(2)}) collective-permute-start(bf16[2,4,64,128]{3,2,1,0:T(8,128)(2,1)S(1)} %get-tuple-element.25), channel_id=1, source_target_pairs={{0,1},{1,0},{2,3},{3,2},{4,5},{5,4},{6,7},{7,6},{8,9},{9,8},{10,11... | collective-permute-start | bytes 393224 | tf_op jit(solution)/shard_map/ppermute | solution.py:202
  17.4 20.3 %collective-permute-start.4 = (bf16[2,4,64,128]{3,2,1,0:T(8,128)(2,1)S(1)}, bf16[2,4,64,128]{3,2,1,0:T(8,128)(2,1)S(1)}, u32[]{:S(2)}, u32[]{:S(2)}) collective-permute-start(bf16[2,4,64,128]{3,2,1,0:T(8,128)(2,1)S(1)} %get-tuple-element.26), channel_id=1, source_target_pairs={{0,2},{1,3},{2,0},{3,1},{4,6},{5,7},{6,4},{7,5},{8,10},{9,11},{10,... | collective-permute-start | bytes 393224 | tf_op jit(solution)/shard_map/ppermute | solution.py:202
  22.6 0.7 copy-start.2
  24.1 17.3 %copy-start.1 = (f32[8,4,4]{0,2,1:T(4,128)S(1)}, f32[8,4,4]{0,2,1:T(4,128)}, u32[]{:S(2)}) copy-start(f32[8,4,4]{0,2,1:T(4,128)} %param.9) | copy-start | bytes 1540
  24.7 28.0 %collective-permute-start.6 = (bf16[1040,128]{1,0:T(8,128)(2,1)S(1)}, bf16[1040,128]{1,0:T(8,128)(2,1)S(1)}, u32[]{:S(2)}, u32[]{:S(2)}) collective-permute-start(bf16[1040,128]{1,0:T(8,128)(2,1)S(1)} %get-tuple-element.29), channel_id=1, source_target_pairs={{64,0},{65,1},{66,2},{67,3},{128,64},{129,65},{130,66},{131,67},{1... | collective-permute-start | bytes 798728 | tf_op jit(solution)/shard_map/ppermute | solution.py:245
  26.0 26.7 %collective-permute-start.7 = (bf16[1040,128]{1,0:T(8,128)(2,1)S(1)}, bf16[1040,128]{1,0:T(8,128)(2,1)S(1)}, u32[]{:S(2)}, u32[]{:S(2)}) collective-permute-start(bf16[1040,128]{1,0:T(8,128)(2,1)S(1)} %get-tuple-element.30), channel_id=1, source_target_pairs={{0,64},{1,65},{2,66},{3,67},{64,128},{65,129},{66,130},{67,131},{1... | collective-permute-start | bytes 798728 | tf_op jit(solution)/shard_map/ppermute | solution.py:245
  30.0 22.7 %collective-permute-start.8 = (bf16[1040,128]{1,0:T(8,128)(2,1)S(1)}, bf16[1040,128]{1,0:T(8,128)(2,1)S(1)}, u32[]{:S(2)}, u32[]{:S(2)}) collective-permute-start(bf16[1040,128]{1,0:T(8,128)(2,1)S(1)} %get-tuple-element.30), channel_id=1, source_target_pairs={{1,0},{2,1},{3,2},{7,3},{6,7},{5,6},{4,5},{8,4},{9,8},{10,9},{11,1... | collective-permute-start | bytes 798728 | tf_op jit(solution)/shard_map/ppermute | solution.py:248
  33.5 19.2 %collective-permute-start.9 = (bf16[1040,128]{1,0:T(8,128)(2,1)S(1)}, bf16[1040,128]{1,0:T(8,128)(2,1)S(1)}, u32[]{:S(2)}, u32[]{:S(2)}) collective-permute-start(bf16[1040,128]{1,0:T(8,128)(2,1)S(1)} %get-tuple-element.29), channel_id=1, source_target_pairs={{0,1},{1,2},{2,3},{3,7},{7,6},{6,5},{5,4},{4,8},{8,9},{9,10},{10,1... | collective-permute-start | bytes 798728 | tf_op jit(solution)/shard_map/ppermute | solution.py:248
  37.7 12.4 %collective-permute-start.5 = (bf16[2,4,64,128]{3,2,1,0:T(8,128)(2,1)S(1)}, bf16[2,4,64,128]{3,2,1,0:T(8,128)(2,1)S(1)}, u32[]{:S(2)}, u32[]{:S(2)}) collective-permute-start(bf16[2,4,64,128]{3,2,1,0:T(8,128)(2,1)S(1)} %get-tuple-element.27), channel_id=1, source_target_pairs={{0,3},{1,2},{2,1},{3,0},{4,7},{5,6},{6,5},{7,4},{8,11},{9,10},{10,... | collective-permute-start | bytes 393224 | tf_op jit(solution)/shard_map/ppermute | solution.py:202
  54.8 5.4 %collective-permute-start.10 = (bf16[4,256,128]{2,1,0:T(8,128)(2,1)S(1)}, bf16[4,256,128]{2,1,0:T(8,128)(2,1)S(1)}, u32[]{:S(2)}, u32[]{:S(2)}) collective-permute-start(bf16[4,256,128]{2,1,0:T(8,128)(2,1)S(1)} %get-tuple-element.34), channel_id=1, source_target_pairs={{0,4},{4,0},{1,5},{5,1},{2,6},{6,2},{3,7},{7,3},{8,12},{12,8},{9,1... | collective-permute-start | bytes 786440 | tf_op jit(solution)/shard_map/ppermute | solution.py:264

commit v10 on v9

--- a/solution.py
+++ b/solution.py
@@ -148,7 +148,7 @@
     send[:, 2 * block :, :] = zc_send[...]
 
 
-def message_kernel(place_of, speeds, cells, *refs):
+def message_kernel(place_of, speeds, *refs):
     parts, messages = refs[:4], refs[4:]
     fields, block = parts[0].shape[1], parts[0].shape[2]
     body = 4 * fields * block
@@ -235,11 +235,11 @@
     first, second = pl.pallas_call(
         message_kernel,
         out_shape=(rows, rows),
-        in_specs=[smem] + [vmem] * 6,
+        in_specs=[smem] + [vmem] * 5,
         out_specs=(vmem, vmem),
         compiler_params=params,
         cost_estimate=pl.CostEstimate(flops=0, bytes_accessed=2**20, transcendentals=0),
-    )(place_of, speeds, cells, *early)
+    )(place_of, speeds, *early)
 
     def along_x(part, step):
         return lax.ppermute(part, ("gx", "ma"), steps_along_x(shape, step))

time: 117 us -> 117 us (level)
  blocking collectives: 55.1 us -> 64.3 us
  waiting for transfers between devices: 9.82 us -> 1.17 us
    all_to_all x1, blocking collectives: 31.1 us -> 40.3 us  [on_device(): received = lax.all_to_all(both, ('ma', 'gx', 'y'), 0, 0)]
    ppermute x6, waiting for transfers between devices: 8.67 us -> 0.02 us  [collected(): lax.ppermute(parts[t], 'ma', [(i, i ^ t) for i in range(ma_count)])]
    ppermute x6, starting transfers between devices: 23.6 us -> 21.8 us  [collected(): lax.ppermute(parts[t], 'ma', [(i, i ^ t) for i in range(ma_count)])]
    ppermute x1, starting transfers between devices: 4.23 us -> 5.73 us  [core_swap(): return lax.ppermute(part, 'core', [(i, 1 - i) for i in range(core_count)])]
  transfers between devices with their start and end apart: 11 -> 11, of which waited for: 2 -> 1; matrix products, arithmetic and copies ran while one was open for 1% -> 1% of each run, Pallas kernels for 3% -> 3%
where the time goes in v10:
time: 117 us; the launch traced here: 116 us
  blocking collectives  64.3 us (55%)
  starting transfers between devices  40.3 us (34%)
  Pallas kernels  5.85 us (5%)
  local copies, waits for them, and re-layouts  2.64 us (2%)
  other arithmetic  1.96 us (2%)
  waiting for transfers between devices  1.17 us (1%)
    all_to_all x1, blocking collectives, on_device(): received = lax.all_to_all(both, ('ma', 'gx', 'y'), 0, 0)  40.3 us
    all_to_all x1, blocking collectives, on_device(): whole = lax.all_to_all(spread, ('core', 'gx', 'y'), 0, 0)  24 us
    ppermute x6, starting transfers between devices, collected(): lax.ppermute(parts[t], 'ma', [(i, i ^ t) for i in range(ma_count)])  21.8 us
    ppermute x2, starting transfers between devices, along_y(): return lax.ppermute(part, names, steps_along_y(shape, step))  8.35 us
    ppermute x1, starting transfers between devices, core_swap(): return lax.ppermute(part, 'core', [(i, 1 - i) for i in range(core_count)])  5.73 us
    ppermute x2, starting transfers between devices, along_x(): return lax.ppermute(part, ('gx', 'ma'), steps_along_x(shape, step))  4.42 us
    pallas_call x1, Pallas kernels, on_device(): pl.pallas_call(local_kernel, out_shape=(*sums(2), jax.ShapeDtypeStruct((k...  2.57 us
  transfers between devices with their start and end apart: 11, of which 1 were waited for; matrix products, arithmetic and copies ran while one was open for 1% of the time, Pallas kernels for 3%

profile of v10, /device:TPU:1, one launch (start us, length us, event | category | flops | bytes accessed | tf_op | source)
XLA Modules:
  0.0 116.5 jit_solution(2875507049806917309)
XLA Ops:
  0.0 1.9 %copy.19 = bf16[8,2,4,64,128]{4,3,2,1,0:T(8,128)(2,1)S(1)} copy(bf16[8,2,4,64,128]{4,0,1,2,3:T(8,128)(2,1)} %bitcast.36) | data formatting | bytes 2097152 | tf_op jit(solution)/shard_map/transpose | solution.py:188
  1.9 0.1 broadcast_select_fusion.wanted
  2.0 0.6 shard_map.55
  2.6 4.8 %collective-permute-start = (bf16[2,4,64,128]{3,2,1,0:T(8,128)(2,1)S(1)}, bf16[2,4,64,128]{3,2,1,0:T(8,128)(2,1)S(1)}, u32[]{:S(2)}, u32[]{:S(2)}) collective-permute-start(bf16[2,4,64,128]{3,2,1,0:T(8,128)(2,1)S(1)} %get-tuple-element.21), channel_id=1, source_target_pairs={{0,1},{1,0},{2,3},{3,2},{4,5},{5,4},{6,7},{7,6},{8,9},{9,8},{10,11... | collective-permute-start | bytes 393224 | tf_op jit(solution)/shard_map/ppermute | solution.py:202
  7.5 5.8 %collective-permute-start.1 = (bf16[2,4,64,128]{3,2,1,0:T(8,128)(2,1)S(1)}, bf16[2,4,64,128]{3,2,1,0:T(8,128)(2,1)S(1)}, u32[]{:S(2)}, u32[]{:S(2)}) collective-permute-start(bf16[2,4,64,128]{3,2,1,0:T(8,128)(2,1)S(1)} %get-tuple-element.22), channel_id=1, source_target_pairs={{0,2},{1,3},{2,0},{3,1},{4,6},{5,7},{6,4},{7,5},{8,10},{9,11},{10,... | collective-permute-start | bytes 393224 | tf_op jit(solution)/shard_map/ppermute | solution.py:202
  13.3 1.9 %collective-permute-start.2 = (bf16[2,4,64,128]{3,2,1,0:T(8,128)(2,1)S(1)}, bf16[2,4,64,128]{3,2,1,0:T(8,128)(2,1)S(1)}, u32[]{:S(2)}, u32[]{:S(2)}) collective-permute-start(bf16[2,4,64,128]{3,2,1,0:T(8,128)(2,1)S(1)} %get-tuple-element.23), channel_id=1, source_target_pairs={{0,3},{1,2},{2,1},{3,0},{4,7},{5,6},{6,5},{7,4},{8,11},{9,10},{10,... | collective-permute-start | bytes 393224 | tf_op jit(solution)/shard_map/ppermute | solution.py:202
  15.2 2.2 %collective-permute-start.3 = (bf16[2,4,64,128]{3,2,1,0:T(8,128)(2,1)S(1)}, bf16[2,4,64,128]{3,2,1,0:T(8,128)(2,1)S(1)}, u32[]{:S(2)}, u32[]{:S(2)}) collective-permute-start(bf16[2,4,64,128]{3,2,1,0:T(8,128)(2,1)S(1)} %get-tuple-element.25), channel_id=1, source_target_pairs={{0,1},{1,0},{2,3},{3,2},{4,5},{5,4},{6,7},{7,6},{8,9},{9,8},{10,11... | collective-permute-start | bytes 393224 | tf_op jit(solution)/shard_map/ppermute | solution.py:202
  17.4 5.2 %collective-permute-start.4 = (bf16[2,4,64,128]{3,2,1,0:T(8,128)(2,1)S(1)}, bf16[2,4,64,128]{3,2,1,0:T(8,128)(2,1)S(1)}, u32[]{:S(2)}, u32[]{:S(2)}) collective-permute-start(bf16[2,4,64,128]{3,2,1,0:T(8,128)(2,1)S(1)} %get-tuple-element.26), channel_id=1, source_target_pairs={{0,2},{1,3},{2,0},{3,1},{4,6},{5,7},{6,4},{7,5},{8,10},{9,11},{10,... | collective-permute-start | bytes 393224 | tf_op jit(solution)/shard_map/ppermute | solution.py:202
  22.6 0.1 pad_add_fusion.place_of
  22.7 1.9 %collective-permute-start.5 = (bf16[2,4,64,128]{3,2,1,0:T(8,128)(2,1)S(1)}, bf16[2,4,64,128]{3,2,1,0:T(8,128)(2,1)S(1)}, u32[]{:S(2)}, u32[]{:S(2)}) collective-permute-start(bf16[2,4,64,128]{3,2,1,0:T(8,128)(2,1)S(1)} %get-tuple-element.27), channel_id=1, source_target_pairs={{0,3},{1,2},{2,1},{3,0},{4,7},{5,6},{6,5},{7,4},{8,11},{9,10},{10,... | collective-permute-start | bytes 393224 | tf_op jit(solution)/shard_map/ppermute | solution.py:202
  24.7 0.0 collective-permute-done.1.refs_2_
  24.7 0.6 shard_map.57
  25.3 0.0 copy-start.1
  25.3 3.1 %collective-permute-start.7 = (bf16[1040,128]{1,0:T(8,128)(2,1)S(1)}, bf16[1040,128]{1,0:T(8,128)(2,1)S(1)}, u32[]{:S(2)}, u32[]{:S(2)}) collective-permute-start(bf16[1040,128]{1,0:T(8,128)(2,1)S(1)} %get-tuple-element.30), channel_id=1, source_target_pairs={{0,64},{1,65},{2,66},{3,67},{64,128},{65,129},{66,130},{67,131},{1... | collective-permute-start | bytes 798728 | tf_op jit(solution)/shard_map/ppermute | solution.py:245
  28.4 3.2 %collective-permute-start.8 = (bf16[1040,128]{1,0:T(8,128)(2,1)S(1)}, bf16[1040,128]{1,0:T(8,128)(2,1)S(1)}, u32[]{:S(2)}, u32[]{:S(2)}) collective-permute-start(bf16[1040,128]{1,0:T(8,128)(2,1)S(1)} %get-tuple-element.30), channel_id=1, source_target_pairs={{1,0},{2,1},{3,2},{7,3},{6,7},{5,6},{4,5},{8,4},{9,8},{10,9},{11,1... | collective-permute-start | bytes 798728 | tf_op jit(solution)/shard_map/ppermute | solution.py:248
  31.6 0.0 collective-permute-done.3.refs_5_
  31.6 1.3 %collective-permute-start.6 = (bf16[1040,128]{1,0:T(8,128)(2,1)S(1)}, bf16[1040,128]{1,0:T(8,128)(2,1)S(1)}, u32[]{:S(2)}, u32[]{:S(2)}) collective-permute-start(bf16[1040,128]{1,0:T(8,128)(2,1)S(1)} %get-tuple-element.29), channel_id=1, source_target_pairs={{64,0},{65,1},{66,2},{67,3},{128,64},{129,65},{130,66},{131,67},{1... | collective-permute-start | bytes 798728 | tf_op jit(solution)/shard_map/ppermute | solution.py:245
  32.9 5.2 %collective-permute-start.9 = (bf16[1040,128]{1,0:T(8,128)(2,1)S(1)}, bf16[1040,128]{1,0:T(8,128)(2,1)S(1)}, u32[]{:S(2)}, u32[]{:S(2)}) collective-permute-start(bf16[1040,128]{1,0:T(8,128)(2,1)S(1)} %get-tuple-element.29), channel_id=1, source_target_pairs={{0,1},{1,2},{2,3},{3,7},{7,6},{6,5},{5,4},{4,8},{8,9},{9,10},{10,1... | collective-permute-start | bytes 798728 | tf_op jit(solution)/shard_map/ppermute | solution.py:248
  38.1 0.7 fusion
  38.8 0.1 copy.20.table
  38.9 0.6 copy-done.2
  39.5 0.0 collective-permute-done.5.refs_7_
  39.5 2.6 %shard_map.56 = (f32[4,128,128]{2,1,0:T(8,128)S(1)}, bf16[4,128,128]{2,1,0:T(8,128)(2,1)S(1)}, bf16[256,2048]{1,0:T(8,128)(2,1)S(1)}) custom-call(s32[2]{0:T(128)S(1)} %pad_add_fusion.place_of, f32[8,16]{1,0:T(8,128)S(1)} %copy.20.table, f32[16,128]{1,0:T(8,128)S(1)} %pad_maximum_fusion.cells, bf16[2,4,64,128]{3,2,1,0:T(8,128)(2,1)S(1)} %get-tuple-element.20.refs_0_, ...), custom_call_target="tpu_custom_call" | custom-call | flops 536870912 | bytes 4194304 | tf_op jit(solution)/shard_map/pallas_call | solution.py:224
  42.1 0.0 collective-permute-done.8.yr
  42.1 2.1 %shard_map.58 = (f32[4,256,128]{2,1,0:T(8,128)S(1)}, bf16[4,256,128]{2,1,0:T(8,128)(2,1)S(1)}) custom-call(s32[2]{0:T(128)S(1)} %pad_add_fusion.place_of, f32[8,128]{1,0:T(8,128)S(1)} %pad_maximum_fusion.1.speeds, bf16[256,2048]{1,0:T(8,128)(2,1)S(1)} %get-tuple-element.28.modes, bf16[1040,128]{1,0:T(8,128)(2,1)S(1)} %collective-permute-done.6.xr, ...), custom_call_target="tpu_custom_call" | custom-call | flops 805306368 | bytes 6291456 | tf_op jit(solution)/shard_map/pallas_call | solution.py:253
  44.2 5.7 %collective-permute-start.10 = (bf16[4,256,128]{2,1,0:T(8,128)(2,1)S(1)}, bf16[4,256,128]{2,1,0:T(8,128)(2,1)S(1)}, u32[]{:S(2)}, u32[]{:S(2)}) collective-permute-start(bf16[4,256,128]{2,1,0:T(8,128)(2,1)S(1)} %get-tuple-element.34), channel_id=1, source_target_pairs={{0,4},{4,0},{1,5},{5,1},{2,6},{6,2},{3,7},{7,3},{8,12},{12,8},{9,1... | collective-permute-start | bytes 786440 | tf_op jit(solution)/shard_map/ppermute | solution.py:264
  50.0 1.1 collective-permute-done.10
  51.1 0.1 add_convert_fusion
  51.2 40.3 %all_to_all.10 = bf16[256,4,128]{2,1,0:T(4,128)(2,1)S(1)} all-to-all(bf16[256,4,128]{2,1,0:T(4,128)(2,1)S(1)} %bitcast.37), channel_id=1, replica_groups=mesh['gx'=8,'y'=8,'core'=2,'ma'=4] {'ma','gx','y'}, dimensions={0} | all-to-all | bytes 524288 | tf_op jit(solution)/shard_map/all_to_all | solution.py:268
  91.5 0.3 convert_reduce_fusion
  91.8 24.0 %all_to_all.11 = bf16[128,4,128]{2,1,0:T(4,128)(2,1)S(1)} all-to-all(bf16[128,4,128]{2,1,0:T(4,128)(2,1)S(1)} %broadcast_in_dim.5), channel_id=1, replica_groups=mesh['gx'=8,'y'=8,'core'=2,'ma'=4] {'core','gx','y'}, dimensions={0} | all-to-all | bytes 262144 | tf_op jit(solution)/shard_map/all_to_all | solution.py:271
  115.8 0.7 copy_bitcast_fusion
  (23 shorter events, 0.1 us)
Async XLA Ops:
  2.0 20.6 %copy-start = (f32[3,2,8,128]{3,2,1,0:T(8,128)S(1)}, f32[3,2,8,128]{3,2,1,0:T(8,128)}, u32[]{:S(2)}) copy-start(f32[3,2,8,128]{3,2,1,0:T(8,128)} %param.6) | copy-start | bytes 73732
  2.6 20.1 %collective-permute-start = (bf16[2,4,64,128]{3,2,1,0:T(8,128)(2,1)S(1)}, bf16[2,4,64,128]{3,2,1,0:T(8,128)(2,1)S(1)}, u32[]{:S(2)}, u32[]{:S(2)}) collective-permute-start(bf16[2,4,64,128]{3,2,1,0:T(8,128)(2,1)S(1)} %get-tuple-element.21), channel_id=1, source_target_pairs={{0,1},{1,0},{2,3},{3,2},{4,5},{5,4},{6,7},{7,6},{8,9},{9,8},{10,11... | collective-permute-start | bytes 393224 | tf_op jit(solution)/shard_map/ppermute | solution.py:202
  7.5 17.2 %collective-permute-start.1 = (bf16[2,4,64,128]{3,2,1,0:T(8,128)(2,1)S(1)}, bf16[2,4,64,128]{3,2,1,0:T(8,128)(2,1)S(1)}, u32[]{:S(2)}, u32[]{:S(2)}) collective-permute-start(bf16[2,4,64,128]{3,2,1,0:T(8,128)(2,1)S(1)} %get-tuple-element.22), channel_id=1, source_target_pairs={{0,2},{1,3},{2,0},{3,1},{4,6},{5,7},{6,4},{7,5},{8,10},{9,11},{10,... | collective-permute-start | bytes 393224 | tf_op jit(solution)/shard_map/ppermute | solution.py:202
  13.3 11.4 %collective-permute-start.2 = (bf16[2,4,64,128]{3,2,1,0:T(8,128)(2,1)S(1)}, bf16[2,4,64,128]{3,2,1,0:T(8,128)(2,1)S(1)}, u32[]{:S(2)}, u32[]{:S(2)}) collective-permute-start(bf16[2,4,64,128]{3,2,1,0:T(8,128)(2,1)S(1)} %get-tuple-element.23), channel_id=1, source_target_pairs={{0,3},{1,2},{2,1},{3,0},{4,7},{5,6},{6,5},{7,4},{8,11},{9,10},{10,... | collective-permute-start | bytes 393224 | tf_op jit(solution)/shard_map/ppermute | solution.py:202
  15.2 16.4 %collective-permute-start.3 = (bf16[2,4,64,128]{3,2,1,0:T(8,128)(2,1)S(1)}, bf16[2,4,64,128]{3,2,1,0:T(8,128)(2,1)S(1)}, u32[]{:S(2)}, u32[]{:S(2)}) collective-permute-start(bf16[2,4,64,128]{3,2,1,0:T(8,128)(2,1)S(1)} %get-tuple-element.25), channel_id=1, source_target_pairs={{0,1},{1,0},{2,3},{3,2},{4,5},{5,4},{6,7},{7,6},{8,9},{9,8},{10,11... | collective-permute-start | bytes 393224 | tf_op jit(solution)/shard_map/ppermute | solution.py:202
  17.4 15.5 %collective-permute-start.4 = (bf16[2,4,64,128]{3,2,1,0:T(8,128)(2,1)S(1)}, bf16[2,4,64,128]{3,2,1,0:T(8,128)(2,1)S(1)}, u32[]{:S(2)}, u32[]{:S(2)}) collective-permute-start(bf16[2,4,64,128]{3,2,1,0:T(8,128)(2,1)S(1)} %get-tuple-element.26), channel_id=1, source_target_pairs={{0,2},{1,3},{2,0},{3,1},{4,6},{5,7},{6,4},{7,5},{8,10},{9,11},{10,... | collective-permute-start | bytes 393224 | tf_op jit(solution)/shard_map/ppermute | solution.py:202
  22.7 16.8 %collective-permute-start.5 = (bf16[2,4,64,128]{3,2,1,0:T(8,128)(2,1)S(1)}, bf16[2,4,64,128]{3,2,1,0:T(8,128)(2,1)S(1)}, u32[]{:S(2)}, u32[]{:S(2)}) collective-permute-start(bf16[2,4,64,128]{3,2,1,0:T(8,128)(2,1)S(1)} %get-tuple-element.27), channel_id=1, source_target_pairs={{0,3},{1,2},{2,1},{3,0},{4,7},{5,6},{6,5},{7,4},{8,11},{9,10},{10,... | collective-permute-start | bytes 393224 | tf_op jit(solution)/shard_map/ppermute | solution.py:202
  25.3 13.6 %copy-start.1 = (f32[8,4,4]{0,2,1:T(4,128)S(1)}, f32[8,4,4]{0,2,1:T(4,128)}, u32[]{:S(2)}) copy-start(f32[8,4,4]{0,2,1:T(4,128)} %param.9) | copy-start | bytes 1540
  25.3 16.8 %collective-permute-start.7 = (bf16[1040,128]{1,0:T(8,128)(2,1)S(1)}, bf16[1040,128]{1,0:T(8,128)(2,1)S(1)}, u32[]{:S(2)}, u32[]{:S(2)}) collective-permute-start(bf16[1040,128]{1,0:T(8,128)(2,1)S(1)} %get-tuple-element.30), channel_id=1, source_target_pairs={{0,64},{1,65},{2,66},{3,67},{64,128},{65,129},{66,130},{67,131},{1... | collective-permute-start | bytes 798728 | tf_op jit(solution)/shard_map/ppermute | solution.py:245
  28.4 13.7 %collective-permute-start.8 = (bf16[1040,128]{1,0:T(8,128)(2,1)S(1)}, bf16[1040,128]{1,0:T(8,128)(2,1)S(1)}, u32[]{:S(2)}, u32[]{:S(2)}) collective-permute-start(bf16[1040,128]{1,0:T(8,128)(2,1)S(1)} %get-tuple-element.30), channel_id=1, source_target_pairs={{1,0},{2,1},{3,2},{7,3},{6,7},{5,6},{4,5},{8,4},{9,8},{10,9},{11,1... | collective-permute-start | bytes 798728 | tf_op jit(solution)/shard_map/ppermute | solution.py:248
  31.6 10.5 %collective-permute-start.6 = (bf16[1040,128]{1,0:T(8,128)(2,1)S(1)}, bf16[1040,128]{1,0:T(8,128)(2,1)S(1)}, u32[]{:S(2)}, u32[]{:S(2)}) collective-permute-start(bf16[1040,128]{1,0:T(8,128)(2,1)S(1)} %get-tuple-element.29), channel_id=1, source_target_pairs={{64,0},{65,1},{66,2},{67,3},{128,64},{129,65},{130,66},{131,67},{1... | collective-permute-start | bytes 798728 | tf_op jit(solution)/shard_map/ppermute | solution.py:245
  32.9 9.2 %collective-permute-start.9 = (bf16[1040,128]{1,0:T(8,128)(2,1)S(1)}, bf16[1040,128]{1,0:T(8,128)(2,1)S(1)}, u32[]{:S(2)}, u32[]{:S(2)}) collective-permute-start(bf16[1040,128]{1,0:T(8,128)(2,1)S(1)} %get-tuple-element.29), channel_id=1, source_target_pairs={{0,1},{1,2},{2,3},{3,7},{7,6},{6,5},{5,4},{4,8},{8,9},{9,10},{10,1... | collective-permute-start | bytes 798728 | tf_op jit(solution)/shard_map/ppermute | solution.py:248
  38.8 0.7 copy-start.2
  44.2 6.9 %collective-permute-start.10 = (bf16[4,256,128]{2,1,0:T(8,128)(2,1)S(1)}, bf16[4,256,128]{2,1,0:T(8,128)(2,1)S(1)}, u32[]{:S(2)}, u32[]{:S(2)}) collective-permute-start(bf16[4,256,128]{2,1,0:T(8,128)(2,1)S(1)} %get-tuple-element.34), channel_id=1, source_target_pairs={{0,4},{4,0},{1,5},{5,1},{2,6},{6,2},{3,7},{7,3},{8,12},{12,8},{9,1... | collective-permute-start | bytes 786440 | tf_op jit(solution)/shard_map/ppermute | solution.py:264

commit v11 on v10

--- a/solution.py
+++ b/solution.py
@@ -52,8 +52,30 @@
             outs[4 + t][number] = pieces[wanted[t], row, 1 - xi]
 
 
-def local_kernel(place_of, table, cells, *refs):
-    early, late, (keep, send, modes, z_image, c_image) = refs[:4], refs[4:8], refs[8:]
+def write_messages(axis, place_of, speeds, parts, messages):
+    fields, block = parts[0].shape[1], parts[0].shape[2]
+    body = 4 * fields * block
+    for number, message in enumerate(messages):
+        for t in range(4):
+            for f in range(fields):
+                start = ((place_of[1] ^ t) * fields + f) * block
+                message[pl.ds(pl.multiple_of(start, block), block), :] = parts[t][number, f]
+        rows = []
+        rest = speeds[4 * axis + 1 + number : 4 * axis + 2 + number, :]
+        for _ in range(3):
+            rows.append(rest.astype(BF16).astype(F32))
+            rest = rest - rows[-1]
+        rows.append(jnp.zeros((13, LANES), F32))
+        message[body:, :] = jnp.concatenate(rows).astype(BF16)
+
+
+def message_kernel(place_of, speeds, *refs):
+    write_messages(0, place_of, speeds, refs[:4], refs[4:])
+
+
+def local_kernel(place_of, table, cells, speeds, *refs):
+    early, late, (keep, send, modes, first, second, z_image, c_image) = refs[:4], refs[4:8], refs[8:]
+    write_messages(1, place_of, speeds, early, (first, second))
     fields, block = early[0].shape[1], early[0].shape[2]
     planes = lax.broadcasted_iota(jnp.int32, (LANES, LANES), 0).astype(F32)
     speed_z, region, partner = cells[:4, :], cells[4:8, :], cells[8:9, :]
@@ -98,73 +120,64 @@
         send[j, rows, :] = jnp.where(place_of[0] == 0, second, first).astype(BF16)
 
 
-def edge_kernel(place_of, speeds, modes, xr, xl, yr, yl, zc_keep, zc_send, keep, send, x_image, x_edge, x_side, y_image, y_edge, y_side):
+def edge_image(axis, speeds, modes, after, before, image, edge, side):
     fields, block = 4, modes.shape[0] // 4
     body = 4 * fields * block
+    base = 4 * axis
     half_speeds = 0.5 * speeds[...]
 
-    def beside_speed(message, axis):
-        rows = message[body:, :].astype(F32)[3 * axis : 3 * axis + 3]
+    def beside_speed(message):
+        rows = message[body:, :].astype(F32)
         return 0.5 * (rows[0:1] + rows[1:2] + rows[2:3])
+
+    def col(line, end):
+        return 2 * line + end if axis == 0 else 2 * end + line
 
     def lane_chunk(index):
         return slice(index * LANES, (index + 1) * LANES)
 
-    axes = (
-        (0, xr, xl, x_image, x_edge, x_side, lambda line, end: 2 * line + end),
-        (4, yr, yl, y_image, y_edge, y_side, lambda line, end: 2 * end + line),
-    )
-    for axis, (base, after, before, image, edge, side, col) in enumerate(axes):
-        for line, message in enumerate((before, after)):
-            near_speed = half_speeds[base + col(line, 0) : base + col(line, 0) + 1]
-            far_speed = half_speeds[base + col(line, 1) : base + col(line, 1) + 1]
-            their_speed = beside_speed(message, axis)
-            for j in range(4):
-                rows = slice(j * block, (j + 1) * block)
-                for f in range(fields):
-                    near, far = (lane_chunk(col(line, end) * fields + f) for end in range(2))
-                    extra = lane_chunk(line * fields + f)
-                    m0 = modes[rows, near].astype(F32)
-                    m1 = modes[rows, far].astype(F32)
-                    start = (j * fields + f) * block
-                    beside = message[start : start + block, :]
-                    at_near = near_speed * m1
-                    at_far = -far_speed * m0
-                    if line == 1:
-                        at_far = far_speed * beside.astype(F32) + at_far
-                        at_side = -their_speed * m1
-                    else:
-                        at_near = at_near - near_speed * beside.astype(F32)
-                        at_side = their_speed * m0
-                    image[rows, near] = at_near.astype(BF16)
-                    image[rows, far] = at_far.astype(BF16)
-                    edge[rows, extra] = at_side.astype(BF16)
-                    side[rows, extra] = beside
-    for q, (_, _, _, image, edge, side, _) in enumerate(axes):
-        total = lax.dot_general(image[...], modes[...], CONTRACT_LAST, preferred_element_type=F32)
-        total += lax.dot_general(edge[...], side[...], CONTRACT_LAST, preferred_element_type=F32)
-        place(place_of, keep, send, q, total, block)
+    for line, message in enumerate((before, after)):
+        near_speed = half_speeds[base + col(line, 0) : base + col(line, 0) + 1]
+        far_speed = half_speeds[base + col(line, 1) : base + col(line, 1) + 1]
+        their_speed = beside_speed(message)
+        for j in range(4):
+            rows = slice(j * block, (j + 1) * block)
+            for f in range(fields):
+                near, far = (lane_chunk(col(line, end) * fields + f) for end in range(2))
+                extra = lane_chunk(line * fields + f)
+                m0 = modes[rows, near].astype(F32)
+                m1 = modes[rows, far].astype(F32)
+                start = (j * fields + f) * block
+                beside = message[start : start + block, :]
+                at_near = near_speed * m1
+                at_far = -far_speed * m0
+                if line == 1:
+                    at_far = far_speed * beside.astype(F32) + at_far
+                    at_side = -their_speed * m1
+                else:
+                    at_near = at_near - near_speed * beside.astype(F32)
+                    at_side = their_speed * m0
+                image[rows, near] = at_near.astype(BF16)
+                image[rows, far] = at_far.astype(BF16)
+                edge[rows, extra] = at_side.astype(BF16)
+                side[rows, extra] = beside
+    total = lax.dot_general(image[...], modes[...], CONTRACT_LAST, preferred_element_type=F32)
+    return total + lax.dot_general(edge[...], side[...], CONTRACT_LAST, preferred_element_type=F32)
+
+
+def x_kernel(place_of, speeds, modes, after, before, keep, send, image, edge, side):
+    total = edge_image(0, speeds, modes, after, before, image, edge, side)
+    place(place_of, keep, send, 0, total, modes.shape[0] // 4)
+
+
+def y_kernel(place_of, speeds, modes, after, before, x_keep, x_send, zc_keep, zc_send, keep, send, image, edge, side):
+    block = modes.shape[0] // 4
+    total = edge_image(1, speeds, modes, after, before, image, edge, side)
+    place(place_of, keep, send, 1, total, block)
+    keep[:, :block, :] = x_keep[...]
+    send[:, :block, :] = x_send[...]
     keep[:, 2 * block :, :] = zc_keep[...]
     send[:, 2 * block :, :] = zc_send[...]
-
-
-def message_kernel(place_of, speeds, *refs):
-    parts, messages = refs[:4], refs[4:]
-    fields, block = parts[0].shape[1], parts[0].shape[2]
-    body = 4 * fields * block
-    for number, message in enumerate(messages):
-        for t in range(4):
-            for f in range(fields):
-                start = ((place_of[1] ^ t) * fields + f) * block
-                message[pl.ds(pl.multiple_of(start, block), block), :] = parts[t][number, f]
-        rows = []
-        for axis in range(2):
-            rest = speeds[4 * axis + 1 + number : 4 * axis + 2 + number, :]
-            for _ in range(3):
-                rows.append(rest.astype(BF16).astype(F32))
-                rest = rest - rows[-1]
-        rows.append(jnp.zeros((10, LANES), F32))
-        message[body:, :] = jnp.concatenate(rows).astype(BF16)
 
 
 def on_device(pod_modes, velocity, region, partner, coupling_table):
@@ -221,16 +234,6 @@
         rows = (ma_count, terms * block, LANES)
         return jax.ShapeDtypeStruct(rows, F32), jax.ShapeDtypeStruct(rows, BF16)
 
-    zc_keep, zc_send, modes = pl.pallas_call(
-        local_kernel,
-        out_shape=(*sums(2), jax.ShapeDtypeStruct((kinds, width), BF16)),
-        in_specs=[smem, smem] + [vmem] * 9,
-        out_specs=(vmem, vmem, vmem),
-        scratch_shapes=[wide, wide],
-        compiler_params=params,
-        cost_estimate=pl.CostEstimate(flops=2 * 2 * kinds * kinds * width, bytes_accessed=4 * 2**20, transcendentals=0),
-    )(place_of, coupling_table.reshape(-1, fields * fields), cells, *early, *late)
-
     rows = jax.ShapeDtypeStruct((4 * fields * block + 16, LANES), BF16)
     first, second = pl.pallas_call(
         message_kernel,
@@ -241,6 +244,16 @@
         cost_estimate=pl.CostEstimate(flops=0, bytes_accessed=2**20, transcendentals=0),
     )(place_of, speeds, *early)
 
+    zc_keep, zc_send, modes, y_first, y_second = pl.pallas_call(
+        local_kernel,
+        out_shape=(*sums(2), jax.ShapeDtypeStruct((kinds, width), BF16), rows, rows),
+        in_specs=[smem, smem] + [vmem] * 10,
+        out_specs=(vmem,) * 5,
+        scratch_shapes=[wide, wide],
+        compiler_params=params,
+        cost_estimate=pl.CostEstimate(flops=2 * 2 * kinds * kinds * width, bytes_accessed=4 * 2**20, transcendentals=0),
+    )(place_of, coupling_table.reshape(-1, fields * fields), cells, speeds, *early, *late)
+
     def along_x(part, step):
         return lax.ppermute(part, ("gx", "ma"), steps_along_x(shape, step))
 
@@ -248,17 +261,28 @@
         return lax.ppermute(part, names, steps_along_y(shape, step))
 
     xr, xl = along_x(second, -1), along_x(first, 1)
-    yr, yl = along_y(first, -1), along_y(second, 1)
-
+    yr, yl = along_y(y_first, -1), along_y(y_second, 1)
+
+    flops = 2 * kinds * kinds * width * 3 // 2
+    cost = pl.CostEstimate(flops=flops, bytes_accessed=3 * 2**20, transcendentals=0)
+    x_sums = pl.pallas_call(
+        x_kernel,
+        out_shape=sums(1),
+        in_specs=[smem] + [vmem] * 4,
+        out_specs=(vmem, vmem),
+        scratch_shapes=[wide, narrow, narrow],
+        compiler_params=params,
+        cost_estimate=cost,
+    )(place_of, speeds, modes, xr, xl)
     keep, send = pl.pallas_call(
-        edge_kernel,
+        y_kernel,
         out_shape=sums(4),
         in_specs=[smem] + [vmem] * 8,
         out_specs=(vmem, vmem),
-        scratch_shapes=[wide, narrow, narrow, wide, narrow, narrow],
-        compiler_params=params,
-        cost_estimate=pl.CostEstimate(flops=2 * 3 * kinds * kinds * width, bytes_accessed=6 * 2**20, transcendentals=0),
-    )(place_of, speeds, modes, xr, xl, yr, yl, zc_keep, zc_send)
+        scratch_shapes=[wide, narrow, narrow],
+        compiler_params=params,
+        cost_estimate=cost,
+    )(place_of, speeds, modes, yr, yl, *x_sums, zc_keep, zc_send)
 
     def core_swap(part):
         return lax.ppermute(part, "core", [(i, 1 - i) for i in range(core_count)])

time: 117 us -> 117 us (level)
  waiting for transfers between devices: 1.17 us -> 7.72 us
  blocking collectives: 64.3 us -> 59.1 us
  starting transfers between devices: 40.3 us -> 37.7 us
    ppermute x2, waiting for transfers between devices: 0.01 us -> 6.56 us  [along_y(): return lax.ppermute(part, names, steps_along_y(shape, step))]
    all_to_all x1, blocking collectives: 40.3 us -> 35.2 us  [on_device(): received = lax.all_to_all(both, ('ma', 'gx', 'y'), 0, 0)]
    ppermute x1, starting transfers between devices: 5.73 us -> 2.53 us  [core_swap(): return lax.ppermute(part, 'core', [(i, 1 - i) for i in range(core_count)])]
    pallas_call x1 -> x2, Pallas kernels: 2.09 us -> 3.06 us  [the longest x1 1.54 us: on_device(): pl.pallas_call(x_kernel, out_shape=sums(1), in_specs=[smem] + [vmem] * 4,...]
  transfers between devices with their start and end apart: 11 -> 11, of which waited for: 1 -> 3; matrix products, arithmetic and copies ran while one was open for 1% -> 1% of each run, Pallas kernels for 3% -> 4%
where the time goes in v11:
time: 117 us; the launch traced here: 116 us
  blocking collectives  59.1 us (51%)
  starting transfers between devices  37.7 us (32%)
  waiting for transfers between devices  7.72 us (7%)
  Pallas kernels  6.9 us (6%)
  local copies, waits for them, and re-layouts  2.63 us (2%)
  other arithmetic  1.96 us (2%)
    all_to_all x1, blocking collectives, on_device(): received = lax.all_to_all(both, ('ma', 'gx', 'y'), 0, 0)  35.2 us
    all_to_all x1, blocking collectives, on_device(): whole = lax.all_to_all(spread, ('core', 'gx', 'y'), 0, 0)  24 us
    ppermute x6, starting transfers between devices, collected(): lax.ppermute(parts[t], 'ma', [(i, i ^ t) for i in range(ma_count)])  21.8 us
    ppermute x2, starting transfers between devices, along_y(): return lax.ppermute(part, names, steps_along_y(shape, step))  8.01 us
    ppermute x2, waiting for transfers between devices, along_y(): return lax.ppermute(part, names, steps_along_y(shape, step))  6.56 us
    ppermute x2, starting transfers between devices, along_x(): return lax.ppermute(part, ('gx', 'ma'), steps_along_x(shape, step))  5.29 us
    pallas_call x1, Pallas kernels, on_device(): pl.pallas_call(local_kernel, out_shape=(*sums(2), jax.ShapeDtypeStruct((k...  2.64 us
    ppermute x1, starting transfers between devices, core_swap(): return lax.ppermute(part, 'core', [(i, 1 - i) for i in range(core_count)])  2.53 us
  transfers between devices with their start and end apart: 11, of which 3 were waited for; matrix products, arithmetic and copies ran while one was open for 1% of the time, Pallas kernels for 4%

profile of v11, /device:TPU:1, one launch (start us, length us, event | category | flops | bytes accessed | tf_op | source)
XLA Modules:
  0.0 116.3 jit_solution(9781338147406694684)
XLA Ops:
  0.0 1.9 %copy.19 = bf16[8,2,4,64,128]{4,3,2,1,0:T(8,128)(2,1)S(1)} copy(bf16[8,2,4,64,128]{4,0,1,2,3:T(8,128)(2,1)} %bitcast.36) | data formatting | bytes 2097152 | tf_op jit(solution)/shard_map/transpose | solution.py:201
  1.9 0.1 broadcast_select_fusion.wanted
  2.0 0.6 shard_map.55
  2.6 4.8 %collective-permute-start = (bf16[2,4,64,128]{3,2,1,0:T(8,128)(2,1)S(1)}, bf16[2,4,64,128]{3,2,1,0:T(8,128)(2,1)S(1)}, u32[]{:S(2)}, u32[]{:S(2)}) collective-permute-start(bf16[2,4,64,128]{3,2,1,0:T(8,128)(2,1)S(1)} %get-tuple-element.25), channel_id=1, source_target_pairs={{0,1},{1,0},{2,3},{3,2},{4,5},{5,4},{6,7},{7,6},{8,9},{9,8},{10,11... | collective-permute-start | bytes 393224 | tf_op jit(solution)/shard_map/ppermute | solution.py:215
  7.5 5.8 %collective-permute-start.1 = (bf16[2,4,64,128]{3,2,1,0:T(8,128)(2,1)S(1)}, bf16[2,4,64,128]{3,2,1,0:T(8,128)(2,1)S(1)}, u32[]{:S(2)}, u32[]{:S(2)}) collective-permute-start(bf16[2,4,64,128]{3,2,1,0:T(8,128)(2,1)S(1)} %get-tuple-element.26), channel_id=1, source_target_pairs={{0,2},{1,3},{2,0},{3,1},{4,6},{5,7},{6,4},{7,5},{8,10},{9,11},{10,... | collective-permute-start | bytes 393224 | tf_op jit(solution)/shard_map/ppermute | solution.py:215
  13.3 1.9 %collective-permute-start.2 = (bf16[2,4,64,128]{3,2,1,0:T(8,128)(2,1)S(1)}, bf16[2,4,64,128]{3,2,1,0:T(8,128)(2,1)S(1)}, u32[]{:S(2)}, u32[]{:S(2)}) collective-permute-start(bf16[2,4,64,128]{3,2,1,0:T(8,128)(2,1)S(1)} %get-tuple-element.27), channel_id=1, source_target_pairs={{0,3},{1,2},{2,1},{3,0},{4,7},{5,6},{6,5},{7,4},{8,11},{9,10},{10,... | collective-permute-start | bytes 393224 | tf_op jit(solution)/shard_map/ppermute | solution.py:215
  15.2 2.2 %collective-permute-start.3 = (bf16[2,4,64,128]{3,2,1,0:T(8,128)(2,1)S(1)}, bf16[2,4,64,128]{3,2,1,0:T(8,128)(2,1)S(1)}, u32[]{:S(2)}, u32[]{:S(2)}) collective-permute-start(bf16[2,4,64,128]{3,2,1,0:T(8,128)(2,1)S(1)} %get-tuple-element.29), channel_id=1, source_target_pairs={{0,1},{1,0},{2,3},{3,2},{4,5},{5,4},{6,7},{7,6},{8,9},{9,8},{10,11... | collective-permute-start | bytes 393224 | tf_op jit(solution)/shard_map/ppermute | solution.py:215
  17.4 5.2 %collective-permute-start.4 = (bf16[2,4,64,128]{3,2,1,0:T(8,128)(2,1)S(1)}, bf16[2,4,64,128]{3,2,1,0:T(8,128)(2,1)S(1)}, u32[]{:S(2)}, u32[]{:S(2)}) collective-permute-start(bf16[2,4,64,128]{3,2,1,0:T(8,128)(2,1)S(1)} %get-tuple-element.30), channel_id=1, source_target_pairs={{0,2},{1,3},{2,0},{3,1},{4,6},{5,7},{6,4},{7,5},{8,10},{9,11},{10,... | collective-permute-start | bytes 393224 | tf_op jit(solution)/shard_map/ppermute | solution.py:215
  22.6 0.7 fusion
  23.4 1.9 %collective-permute-start.5 = (bf16[2,4,64,128]{3,2,1,0:T(8,128)(2,1)S(1)}, bf16[2,4,64,128]{3,2,1,0:T(8,128)(2,1)S(1)}, u32[]{:S(2)}, u32[]{:S(2)}) collective-permute-start(bf16[2,4,64,128]{3,2,1,0:T(8,128)(2,1)S(1)} %get-tuple-element.31), channel_id=1, source_target_pairs={{0,3},{1,2},{2,1},{3,0},{4,7},{5,6},{6,5},{7,4},{8,11},{9,10},{10,... | collective-permute-start | bytes 393224 | tf_op jit(solution)/shard_map/ppermute | solution.py:215
  25.3 0.1 pad_add_fusion.place_of
  25.4 0.1 copy.20.table
  25.4 0.6 copy-done.2
  26.1 0.0 collective-permute-done.2.refs_3_
  26.1 0.6 shard_map.57
  26.7 1.3 %collective-permute-start.8 = (bf16[1040,128]{1,0:T(8,128)(2,1)S(1)}, bf16[1040,128]{1,0:T(8,128)(2,1)S(1)}, u32[]{:S(2)}, u32[]{:S(2)}) collective-permute-start(bf16[1040,128]{1,0:T(8,128)(2,1)S(1)} %get-tuple-element.35), channel_id=1, source_target_pairs={{64,0},{65,1},{66,2},{67,3},{128,64},{129,65},{130,66},{131,67},{1... | collective-permute-start | bytes 798728 | tf_op jit(solution)/shard_map/ppermute | solution.py:258
  28.0 4.0 %collective-permute-start.9 = (bf16[1040,128]{1,0:T(8,128)(2,1)S(1)}, bf16[1040,128]{1,0:T(8,128)(2,1)S(1)}, u32[]{:S(2)}, u32[]{:S(2)}) collective-permute-start(bf16[1040,128]{1,0:T(8,128)(2,1)S(1)} %get-tuple-element.36), channel_id=1, source_target_pairs={{0,64},{1,65},{2,66},{3,67},{64,128},{65,129},{66,130},{67,131},{1... | collective-permute-start | bytes 798728 | tf_op jit(solution)/shard_map/ppermute | solution.py:258
  32.0 0.0 collective-permute-done.4.refs_6_
  32.0 2.6 %shard_map.56 = (f32[4,128,128]{2,1,0:T(8,128)S(1)}, bf16[4,128,128]{2,1,0:T(8,128)(2,1)S(1)}, bf16[256,2048]{1,0:T(8,128)(2,1)S(1)}, bf16[1040,128]{1,0:T(8,128)(2,1)S(1)}, bf16[1040,128]{1,0:T(8,128)(2,1)S(1)}) custom-call(s32[2]{0:T(128)S(1)} %pad_add_fusion.place_of, f32[8,16]{1,0:T(8,128)S(1)} %copy.20.table, f32[16,128]{1,0:T(8,128)S(1)} %pad_maximum_fusion.cells, ...), custom_call_target="tpu_custom_call" | custom-call | flops 536870912 | bytes 4194304 | tf_op jit(solution)/shard_map/pallas_call | solution.py:247
  34.7 6.1 %collective-permute-start.6 = (bf16[1040,128]{1,0:T(8,128)(2,1)S(1)}, bf16[1040,128]{1,0:T(8,128)(2,1)S(1)}, u32[]{:S(2)}, u32[]{:S(2)}) collective-permute-start(bf16[1040,128]{1,0:T(8,128)(2,1)S(1)} %get-tuple-element.33), channel_id=1, source_target_pairs={{1,0},{2,1},{3,2},{7,3},{6,7},{5,6},{4,5},{8,4},{9,8},{10,9},{11,1... | collective-permute-start | bytes 798728 | tf_op jit(solution)/shard_map/ppermute | solution.py:261
  40.7 1.9 %collective-permute-start.7 = (bf16[1040,128]{1,0:T(8,128)(2,1)S(1)}, bf16[1040,128]{1,0:T(8,128)(2,1)S(1)}, u32[]{:S(2)}, u32[]{:S(2)}) collective-permute-start(bf16[1040,128]{1,0:T(8,128)(2,1)S(1)} %get-tuple-element.34), channel_id=1, source_target_pairs={{0,1},{1,2},{2,3},{3,7},{7,6},{6,5},{5,4},{4,8},{8,9},{9,10},{10,1... | collective-permute-start | bytes 798728 | tf_op jit(solution)/shard_map/ppermute | solution.py:261
  42.7 1.5 %shard_map.58 = (f32[4,64,128]{2,1,0:T(8,128)S(1)}, bf16[4,64,128]{2,1,0:T(8,128)(2,1)S(1)}) custom-call(s32[2]{0:T(128)S(1)} %pad_add_fusion.place_of, f32[8,128]{1,0:T(8,128)S(1)} %pad_maximum_fusion.1.speeds, bf16[256,2048]{1,0:T(8,128)(2,1)S(1)} %get-tuple-element.32.modes, bf16[1040,128]{1,0:T(8,128)(2,1)S(1)} %collective-permute-done.8.after, ...), custom_call_target="tpu_custom_call" | custom-call | flops 402653184 | bytes 3145728 | tf_op jit(solution)/shard_map/pallas_call | solution.py:268
  44.3 2.5 %collective-permute-done.6.after = bf16[1040,128]{1,0:T(8,128)(2,1)S(1)} collective-permute-done((bf16[1040,128]{1,0:T(8,128)(2,1)S(1)}, bf16[1040,128]{1,0:T(8,128)(2,1)S(1)}, u32[]{:S(2)}, u32[]{:S(2)}) %collective-permute-start.6) | collective-permute-done | bytes 266272 | tf_op jit(solution)/shard_map/ppermute | solution.py:261
  46.8 4.0 %collective-permute-done.7.before = bf16[1040,128]{1,0:T(8,128)(2,1)S(1)} collective-permute-done((bf16[1040,128]{1,0:T(8,128)(2,1)S(1)}, bf16[1040,128]{1,0:T(8,128)(2,1)S(1)}, u32[]{:S(2)}, u32[]{:S(2)}) %collective-permute-start.7) | collective-permute-done | bytes 266272 | tf_op jit(solution)/shard_map/ppermute | solution.py:261
  50.8 1.5 %shard_map.59 = (f32[4,256,128]{2,1,0:T(8,128)S(1)}, bf16[4,256,128]{2,1,0:T(8,128)(2,1)S(1)}) custom-call(s32[2]{0:T(128)S(1)} %pad_add_fusion.place_of, f32[8,128]{1,0:T(8,128)S(1)} %pad_maximum_fusion.1.speeds, bf16[256,2048]{1,0:T(8,128)(2,1)S(1)} %get-tuple-element.32.modes, bf16[1040,128]{1,0:T(8,128)(2,1)S(1)} %collective-permute-done.6.after, ...), custom_call_target="tpu_custom_call" | custom-call | flops 402653184 | bytes 3145728 | tf_op jit(solution)/shard_map/pallas_call | solution.py:277
  52.3 2.5 %collective-permute-start.10 = (bf16[4,256,128]{2,1,0:T(8,128)(2,1)S(1)}, bf16[4,256,128]{2,1,0:T(8,128)(2,1)S(1)}, u32[]{:S(2)}, u32[]{:S(2)}) collective-permute-start(bf16[4,256,128]{2,1,0:T(8,128)(2,1)S(1)} %get-tuple-element.42), channel_id=1, source_target_pairs={{0,4},{4,0},{1,5},{5,1},{2,6},{6,2},{3,7},{7,3},{8,12},{12,8},{9,1... | collective-permute-start | bytes 786440 | tf_op jit(solution)/shard_map/ppermute | solution.py:288
  54.9 1.1 collective-permute-done.10
  56.0 0.1 add_convert_fusion
  56.1 35.2 %all_to_all.10 = bf16[256,4,128]{2,1,0:T(4,128)(2,1)S(1)} all-to-all(bf16[256,4,128]{2,1,0:T(4,128)(2,1)S(1)} %bitcast.37), channel_id=1, replica_groups=mesh['gx'=8,'y'=8,'core'=2,'ma'=4] {'ma','gx','y'}, dimensions={0} | all-to-all | bytes 524288 | tf_op jit(solution)/shard_map/all_to_all | solution.py:292
  91.3 0.3 convert_reduce_fusion
  91.6 24.0 %all_to_all.11 = bf16[128,4,128]{2,1,0:T(4,128)(2,1)S(1)} all-to-all(bf16[128,4,128]{2,1,0:T(4,128)(2,1)S(1)} %broadcast_in_dim.5), channel_id=1, replica_groups=mesh['gx'=8,'y'=8,'core'=2,'ma'=4] {'core','gx','y'}, dimensions={0} | all-to-all | bytes 262144 | tf_op jit(solution)/shard_map/all_to_all | solution.py:295
  115.6 0.7 copy_bitcast_fusion
  (24 shorter events, 0.1 us)
Async XLA Ops:
  2.0 20.6 %copy-start = (f32[3,2,8,128]{3,2,1,0:T(8,128)S(1)}, f32[3,2,8,128]{3,2,1,0:T(8,128)}, u32[]{:S(2)}) copy-start(f32[3,2,8,128]{3,2,1,0:T(8,128)} %param.6) | copy-start | bytes 73732
  2.6 20.8 %collective-permute-start = (bf16[2,4,64,128]{3,2,1,0:T(8,128)(2,1)S(1)}, bf16[2,4,64,128]{3,2,1,0:T(8,128)(2,1)S(1)}, u32[]{:S(2)}, u32[]{:S(2)}) collective-permute-start(bf16[2,4,64,128]{3,2,1,0:T(8,128)(2,1)S(1)} %get-tuple-element.25), channel_id=1, source_target_pairs={{0,1},{1,0},{2,3},{3,2},{4,5},{5,4},{6,7},{7,6},{8,9},{9,8},{10,11... | collective-permute-start | bytes 393224 | tf_op jit(solution)/shard_map/ppermute | solution.py:215
  7.5 18.6 %collective-permute-start.1 = (bf16[2,4,64,128]{3,2,1,0:T(8,128)(2,1)S(1)}, bf16[2,4,64,128]{3,2,1,0:T(8,128)(2,1)S(1)}, u32[]{:S(2)}, u32[]{:S(2)}) collective-permute-start(bf16[2,4,64,128]{3,2,1,0:T(8,128)(2,1)S(1)} %get-tuple-element.26), channel_id=1, source_target_pairs={{0,2},{1,3},{2,0},{3,1},{4,6},{5,7},{6,4},{7,5},{8,10},{9,11},{10,... | collective-permute-start | bytes 393224 | tf_op jit(solution)/shard_map/ppermute | solution.py:215
  13.3 12.8 %collective-permute-start.2 = (bf16[2,4,64,128]{3,2,1,0:T(8,128)(2,1)S(1)}, bf16[2,4,64,128]{3,2,1,0:T(8,128)(2,1)S(1)}, u32[]{:S(2)}, u32[]{:S(2)}) collective-permute-start(bf16[2,4,64,128]{3,2,1,0:T(8,128)(2,1)S(1)} %get-tuple-element.27), channel_id=1, source_target_pairs={{0,3},{1,2},{2,1},{3,0},{4,7},{5,6},{6,5},{7,4},{8,11},{9,10},{10,... | collective-permute-start | bytes 393224 | tf_op jit(solution)/shard_map/ppermute | solution.py:215
  15.2 16.8 %collective-permute-start.3 = (bf16[2,4,64,128]{3,2,1,0:T(8,128)(2,1)S(1)}, bf16[2,4,64,128]{3,2,1,0:T(8,128)(2,1)S(1)}, u32[]{:S(2)}, u32[]{:S(2)}) collective-permute-start(bf16[2,4,64,128]{3,2,1,0:T(8,128)(2,1)S(1)} %get-tuple-element.29), channel_id=1, source_target_pairs={{0,1},{1,0},{2,3},{3,2},{4,5},{5,4},{6,7},{7,6},{8,9},{9,8},{10,11... | collective-permute-start | bytes 393224 | tf_op jit(solution)/shard_map/ppermute | solution.py:215
  17.4 14.6 %collective-permute-start.4 = (bf16[2,4,64,128]{3,2,1,0:T(8,128)(2,1)S(1)}, bf16[2,4,64,128]{3,2,1,0:T(8,128)(2,1)S(1)}, u32[]{:S(2)}, u32[]{:S(2)}) collective-permute-start(bf16[2,4,64,128]{3,2,1,0:T(8,128)(2,1)S(1)} %get-tuple-element.30), channel_id=1, source_target_pairs={{0,2},{1,3},{2,0},{3,1},{4,6},{5,7},{6,4},{7,5},{8,10},{9,11},{10,... | collective-permute-start | bytes 393224 | tf_op jit(solution)/shard_map/ppermute | solution.py:215
  23.3 2.0 %copy-start.1 = (f32[8,4,4]{0,2,1:T(4,128)S(1)}, f32[8,4,4]{0,2,1:T(4,128)}, u32[]{:S(2)}) copy-start(f32[8,4,4]{0,2,1:T(4,128)} %param.9) | copy-start | bytes 1540
  23.4 8.6 %collective-permute-start.5 = (bf16[2,4,64,128]{3,2,1,0:T(8,128)(2,1)S(1)}, bf16[2,4,64,128]{3,2,1,0:T(8,128)(2,1)S(1)}, u32[]{:S(2)}, u32[]{:S(2)}) collective-permute-start(bf16[2,4,64,128]{3,2,1,0:T(8,128)(2,1)S(1)} %get-tuple-element.31), channel_id=1, source_target_pairs={{0,3},{1,2},{2,1},{3,0},{4,7},{5,6},{6,5},{7,4},{8,11},{9,10},{10,... | collective-permute-start | bytes 393224 | tf_op jit(solution)/shard_map/ppermute | solution.py:215
  25.4 0.7 copy-start.2
  26.7 16.0 %collective-permute-start.8 = (bf16[1040,128]{1,0:T(8,128)(2,1)S(1)}, bf16[1040,128]{1,0:T(8,128)(2,1)S(1)}, u32[]{:S(2)}, u32[]{:S(2)}) collective-permute-start(bf16[1040,128]{1,0:T(8,128)(2,1)S(1)} %get-tuple-element.35), channel_id=1, source_target_pairs={{64,0},{65,1},{66,2},{67,3},{128,64},{129,65},{130,66},{131,67},{1... | collective-permute-start | bytes 798728 | tf_op jit(solution)/shard_map/ppermute | solution.py:258
  28.0 14.7 %collective-permute-start.9 = (bf16[1040,128]{1,0:T(8,128)(2,1)S(1)}, bf16[1040,128]{1,0:T(8,128)(2,1)S(1)}, u32[]{:S(2)}, u32[]{:S(2)}) collective-permute-start(bf16[1040,128]{1,0:T(8,128)(2,1)S(1)} %get-tuple-element.36), channel_id=1, source_target_pairs={{0,64},{1,65},{2,66},{3,67},{64,128},{65,129},{66,130},{67,131},{1... | collective-permute-start | bytes 798728 | tf_op jit(solution)/shard_map/ppermute | solution.py:258
  34.7 12.1 %collective-permute-start.6 = (bf16[1040,128]{1,0:T(8,128)(2,1)S(1)}, bf16[1040,128]{1,0:T(8,128)(2,1)S(1)}, u32[]{:S(2)}, u32[]{:S(2)}) collective-permute-start(bf16[1040,128]{1,0:T(8,128)(2,1)S(1)} %get-tuple-element.33), channel_id=1, source_target_pairs={{1,0},{2,1},{3,2},{7,3},{6,7},{5,6},{4,5},{8,4},{9,8},{10,9},{11,1... | collective-permute-start | bytes 798728 | tf_op jit(solution)/shard_map/ppermute | solution.py:261
  40.7 10.1 %collective-permute-start.7 = (bf16[1040,128]{1,0:T(8,128)(2,1)S(1)}, bf16[1040,128]{1,0:T(8,128)(2,1)S(1)}, u32[]{:S(2)}, u32[]{:S(2)}) collective-permute-start(bf16[1040,128]{1,0:T(8,128)(2,1)S(1)} %get-tuple-element.34), channel_id=1, source_target_pairs={{0,1},{1,2},{2,3},{3,7},{7,6},{6,5},{5,4},{4,8},{8,9},{9,10},{10,1... | collective-permute-start | bytes 798728 | tf_op jit(solution)/shard_map/ppermute | solution.py:261
  52.3 3.7 %collective-permute-start.10 = (bf16[4,256,128]{2,1,0:T(8,128)(2,1)S(1)}, bf16[4,256,128]{2,1,0:T(8,128)(2,1)S(1)}, u32[]{:S(2)}, u32[]{:S(2)}) collective-permute-start(bf16[4,256,128]{2,1,0:T(8,128)(2,1)S(1)} %get-tuple-element.42), channel_id=1, source_target_pairs={{0,4},{4,0},{1,5},{5,1},{2,6},{6,2},{3,7},{7,3},{8,12},{12,8},{9,1... | collective-permute-start | bytes 786440 | tf_op jit(solution)/shard_map/ppermute | solution.py:288

commit v12 on v11

--- a/solution.py
+++ b/solution.py
@@ -45,21 +45,26 @@
     ]
 
 
-def pack_kernel(wanted, pieces, *outs):
+def pack_early(wanted, pieces, early):
     for t in range(4):
         for number, (row, xi) in enumerate(((0, 1), (1, 0))):
-            outs[t][number] = pieces[wanted[t], row, xi]
-            outs[4 + t][number] = pieces[wanted[t], row, 1 - xi]
-
-
-def write_messages(axis, place_of, speeds, parts, messages):
-    fields, block = parts[0].shape[1], parts[0].shape[2]
+            early[t, number] = pieces[wanted[4 + t], row, xi]
+
+
+def pack_late(wanted, pieces, early, *late):
+    for t in range(4):
+        for number in range(2):
+            late[t][number] = pieces[wanted[t], number, number]
+
+
+def write_messages(axis, speeds, early, messages):
+    fields, block = early.shape[2], early.shape[3]
     body = 4 * fields * block
     for number, message in enumerate(messages):
-        for t in range(4):
+        for j in range(4):
             for f in range(fields):
-                start = ((place_of[1] ^ t) * fields + f) * block
-                message[pl.ds(pl.multiple_of(start, block), block), :] = parts[t][number, f]
+                start = (j * fields + f) * block
+                message[start : start + block, :] = early[j, number, f]
         rows = []
         rest = speeds[4 * axis + 1 + number : 4 * axis + 2 + number, :]
         for _ in range(3):
@@ -69,14 +74,14 @@
         message[body:, :] = jnp.concatenate(rows).astype(BF16)
 
 
-def message_kernel(place_of, speeds, *refs):
-    write_messages(0, place_of, speeds, refs[:4], refs[4:])
-
-
-def local_kernel(place_of, table, cells, speeds, *refs):
-    early, late, (keep, send, modes, first, second, z_image, c_image) = refs[:4], refs[4:8], refs[8:]
-    write_messages(1, place_of, speeds, early, (first, second))
-    fields, block = early[0].shape[1], early[0].shape[2]
+def message_kernel(speeds, early, *messages):
+    write_messages(0, speeds, early, messages)
+
+
+def local_kernel(place_of, table, cells, speeds, early, *refs):
+    late, (keep, send, modes, first, second, z_image, c_image) = refs[:4], refs[4:]
+    write_messages(1, speeds, early, (first, second))
+    fields, block = early.shape[2], early.shape[3]
     planes = lax.broadcasted_iota(jnp.int32, (LANES, LANES), 0).astype(F32)
     speed_z, region, partner = cells[:4, :], cells[4:8, :], cells[8:9, :]
     pick = (planes == partner).astype(F32).astype(BF16)
@@ -90,9 +95,12 @@
                 coupling[f, g] = chosen
     for col in range(4):
         for t in range(4):
-            rows = pl.ds(pl.multiple_of((place_of[1] ^ t) * block, block), block)
-            cell = (early if col in (1, 2) else late)[t]
-            here = [cell[col // 2, f] for f in range(fields)]
+            if col in (1, 2):
+                rows = slice(t * block, (t + 1) * block)
+                here = [early[t, col - 1, f] for f in range(fields)]
+            else:
+                rows = pl.ds(pl.multiple_of((place_of[1] ^ t) * block, block), block)
+                here = [late[t][col // 2, f] for f in range(fields)]
             moved = jnp.dot(jnp.concatenate(here, axis=0), pick, preferred_element_type=F32)
             centre = [cells_f.astype(F32) for cells_f in here]
             for f in range(fields):
@@ -193,29 +201,34 @@
     reverse = (gx // (gx_count // 2) + gy) % 2 == 1
     k = jnp.where(reverse, ma_count - 1 - ma, ma)
 
-    homes = jnp.stack([ma ^ t for t in range(ma_count)])
+    homes = jnp.stack([ma ^ t for t in range(ma_count)] + [jnp.asarray(m, ma.dtype) for m in range(ma_count)])
     wanted = jnp.where(reverse, ma_count - 1 - homes, homes).astype(jnp.int32)
     vmem = pl.BlockSpec(memory_space=pltpu.VMEM)
     smem = pl.BlockSpec(memory_space=pltpu.SMEM)
     params = pltpu.CompilerParams(vmem_limit_bytes=40 * 2**20)
     pieces = jnp.transpose(pod_modes, (3, 2, 1, 0, 4)).reshape(ma_count, 2, cells_x, fields, block, planes)
-    piece = jax.ShapeDtypeStruct((2, fields, block, planes), BF16)
-    packed = pl.pallas_call(
-        pack_kernel,
-        out_shape=(piece,) * (2 * ma_count),
+    piece = (2, fields, block, planes)
+    cost = pl.CostEstimate(flops=0, bytes_accessed=2**20, transcendentals=0)
+    early = pl.pallas_call(
+        pack_early,
+        out_shape=jax.ShapeDtypeStruct((ma_count, *piece), BF16),
         in_specs=[smem, vmem],
-        out_specs=(vmem,) * (2 * ma_count),
-        compiler_params=params,
-        cost_estimate=pl.CostEstimate(flops=0, bytes_accessed=2 * 2**20, transcendentals=0),
+        out_specs=vmem,
+        compiler_params=params,
+        cost_estimate=cost,
     )(wanted, pieces)
-
-    def collected(parts):
-        blocks = {0: parts[0]}
-        for t in (2, 3, 1):
-            blocks[t] = lax.ppermute(parts[t], "ma", [(i, i ^ t) for i in range(ma_count)])
-        return [blocks[t] for t in range(ma_count)]
-
-    early, late = collected(packed[:ma_count]), collected(packed[ma_count:])
+    late = pl.pallas_call(
+        pack_late,
+        out_shape=(jax.ShapeDtypeStruct(piece, BF16),) * ma_count,
+        in_specs=[smem, vmem, pl.BlockSpec(memory_space=pl.ANY)],
+        out_specs=(vmem,) * ma_count,
+        compiler_params=params,
+        cost_estimate=cost,
+    )(wanted, pieces, early)
+    late = list(late)
+    early = lax.all_to_all(early, "ma", 0, 0)
+    for t in (2, 3, 1):
+        late[t] = lax.ppermute(late[t], "ma", [(i, i ^ t) for i in range(ma_count)])
 
     def columns(part):
         return lax.dynamic_slice_in_dim(part, 2 * k, 2, 1).transpose(1, 0, 2).reshape(4, planes)
@@ -238,21 +251,21 @@
     first, second = pl.pallas_call(
         message_kernel,
         out_shape=(rows, rows),
-        in_specs=[smem] + [vmem] * 5,
+        in_specs=[vmem] * 2,
         out_specs=(vmem, vmem),
         compiler_params=params,
         cost_estimate=pl.CostEstimate(flops=0, bytes_accessed=2**20, transcendentals=0),
-    )(place_of, speeds, *early)
+    )(speeds, early)
 
     zc_keep, zc_send, modes, y_first, y_second = pl.pallas_call(
         local_kernel,
         out_shape=(*sums(2), jax.ShapeDtypeStruct((kinds, width), BF16), rows, rows),
-        in_specs=[smem, smem] + [vmem] * 10,
+        in_specs=[smem, smem] + [vmem] * 7,
         out_specs=(vmem,) * 5,
         scratch_shapes=[wide, wide],
         compiler_params=params,
         cost_estimate=pl.CostEstimate(flops=2 * 2 * kinds * kinds * width, bytes_accessed=4 * 2**20, transcendentals=0),
-    )(place_of, coupling_table.reshape(-1, fields * fields), cells, speeds, *early, *late)
+    )(place_of, coupling_table.reshape(-1, fields * fields), cells, speeds, early, *late)
 
     def along_x(part, step):
         return lax.ppermute(part, ("gx", "ma"), steps_along_x(shape, step))

time: 117 us -> 115 us (0.983)
  blocking collectives: 59.1 us -> 56.8 us
  waiting for transfers between devices: 7.72 us -> 6.43 us
  starting transfers between devices: 37.7 us -> 38.9 us
    ppermute x6 -> x3, starting transfers between devices: 21.8 us -> 9.28 us  [on_device(): late[t] = lax.ppermute(late[t], 'ma', [(i, i ^ t) for i in range(ma_count)])]
    all_to_all x0 -> x1, starting transfers between devices: none -> 7.81 us  [on_device(): early = lax.all_to_all(early, 'ma', 0, 0)]
    ppermute x2, waiting for transfers between devices: 6.56 us -> 1.77 us  [along_y(): return lax.ppermute(part, names, steps_along_y(shape, step))]
    ppermute x6 -> x3, waiting for transfers between devices: 0.02 us -> 3.34 us  [on_device(): late[t] = lax.ppermute(late[t], 'ma', [(i, i ^ t) for i in range(ma_count)])]
    ppermute x2, starting transfers between devices: 8.01 us -> 11.2 us  [along_y(): return lax.ppermute(part, names, steps_along_y(shape, step))]
    all_to_all x1, blocking collectives: 35.2 us -> 32.8 us  [on_device(): received = lax.all_to_all(both, ('ma', 'gx', 'y'), 0, 0)]
    ppermute x2, starting transfers between devices: 5.29 us -> 6.72 us  [along_x(): return lax.ppermute(part, ('gx', 'ma'), steps_along_x(shape, step))]
    ppermute x1, starting transfers between devices: 2.53 us -> 3.89 us  [core_swap(): return lax.ppermute(part, 'core', [(i, 1 - i) for i in range(core_count)])]
  transfers between devices with their start and end apart: 11 -> 9, of which waited for: 3 -> 5; matrix products, arithmetic and copies ran while one was open for 1% -> 1% of each run, Pallas kernels for 4% -> 4%
where the time goes in v12:
time: 115 us
  blocking collectives  56.8 us (49%)
  starting transfers between devices  38.9 us (34%)
  Pallas kernels  7.61 us (7%)
  waiting for transfers between devices  6.43 us (6%)
  local copies, waits for them, and re-layouts  2.8 us (2%)
  other arithmetic  1.89 us (2%)
    all_to_all x1, blocking collectives, on_device(): received = lax.all_to_all(both, ('ma', 'gx', 'y'), 0, 0)  32.8 us
    all_to_all x1, blocking collectives, on_device(): whole = lax.all_to_all(spread, ('core', 'gx', 'y'), 0, 0)  24 us
    ppermute x2, starting transfers between devices, along_y(): return lax.ppermute(part, names, steps_along_y(shape, step))  11.2 us
    ppermute x3, starting transfers between devices, on_device(): late[t] = lax.ppermute(late[t], 'ma', [(i, i ^ t) for i in range(ma_count)])  9.28 us
    all_to_all x1, starting transfers between devices, on_device(): early = lax.all_to_all(early, 'ma', 0, 0)  7.81 us
    ppermute x2, starting transfers between devices, along_x(): return lax.ppermute(part, ('gx', 'ma'), steps_along_x(shape, step))  6.72 us
    ppermute x1, starting transfers between devices, core_swap(): return lax.ppermute(part, 'core', [(i, 1 - i) for i in range(core_count)])  3.89 us
    ppermute x3, waiting for transfers between devices, on_device(): late[t] = lax.ppermute(late[t], 'ma', [(i, i ^ t) for i in range(ma_count)])  3.34 us
  transfers between devices with their start and end apart: 9, of which 5 were waited for; matrix products, arithmetic and copies ran while one was open for 1% of the time, Pallas kernels for 4%

profile of v12, /device:TPU:1, one launch (start us, length us, event | category | flops | bytes accessed | tf_op | source)
XLA Modules:
  0.0 114.7 jit_solution(5238696737033068404)
XLA Ops:
  0.0 1.9 %copy.19 = bf16[8,2,4,64,128]{4,3,2,1,0:T(8,128)(2,1)S(1)} copy(bf16[8,2,4,64,128]{4,0,1,2,3:T(8,128)(2,1)} %bitcast.37) | data formatting | bytes 2097152 | tf_op jit(solution)/shard_map/transpose | solution.py:209
  1.9 0.1 stack.28
  2.0 1.4 %shard_map.55.early = bf16[4,2,4,64,128]{4,3,2,1,0:T(8,128)(2,1)} custom-call(s32[8]{0:T(128)S(1)} %broadcast_select_fusion.wanted, bf16[4,2,2,4,64,128]{5,4,3,2,1,0:T(8,128)(2,1)S(1)} %bitcast.35), custom_call_target="tpu_custom_call" | custom-call | bytes 1048576 | tf_op jit(solution)/shard_map/pallas_call | solution.py:212
  3.4 7.8 %all-to-all-start = ((bf16[4,2,4,64,128]{4,3,2,1,0:T(8,128)(2,1)}), bf16[4,2,4,64,128]{4,3,2,1,0:T(8,128)(2,1)S(1)}, u32[]{:S(2)}, u32[]{:S(2)}) async-start(bf16[4,2,4,64,128]{4,3,2,1,0:T(8,128)(2,1)} %shard_map.55.early), calls=%async_computation | async-start | bytes 1048576 | tf_op jit(solution)/shard_map/all_to_all | solution.py:229
  11.2 0.6 shard_map.56
  11.8 3.4 %collective-permute-start = (bf16[2,4,64,128]{3,2,1,0:T(8,128)(2,1)S(1)}, bf16[2,4,64,128]{3,2,1,0:T(8,128)(2,1)S(1)}, u32[]{:S(2)}, u32[]{:S(2)}) collective-permute-start(bf16[2,4,64,128]{3,2,1,0:T(8,128)(2,1)S(1)} %get-tuple-element.21), channel_id=1, source_target_pairs={{0,1},{1,0},{2,3},{3,2},{4,5},{5,4},{6,7},{7,6},{8,9},{9,8},{10,11... | collective-permute-start | bytes 393224 | tf_op jit(solution)/shard_map/ppermute | solution.py:231
  15.2 4.0 %collective-permute-start.1 = (bf16[2,4,64,128]{3,2,1,0:T(8,128)(2,1)S(1)}, bf16[2,4,64,128]{3,2,1,0:T(8,128)(2,1)S(1)}, u32[]{:S(2)}, u32[]{:S(2)}) collective-permute-start(bf16[2,4,64,128]{3,2,1,0:T(8,128)(2,1)S(1)} %get-tuple-element.22), channel_id=1, source_target_pairs={{0,2},{1,3},{2,0},{3,1},{4,6},{5,7},{6,4},{7,5},{8,10},{9,11},{10,... | collective-permute-start | bytes 393224 | tf_op jit(solution)/shard_map/ppermute | solution.py:231
  19.1 1.9 %collective-permute-start.2 = (bf16[2,4,64,128]{3,2,1,0:T(8,128)(2,1)S(1)}, bf16[2,4,64,128]{3,2,1,0:T(8,128)(2,1)S(1)}, u32[]{:S(2)}, u32[]{:S(2)}) collective-permute-start(bf16[2,4,64,128]{3,2,1,0:T(8,128)(2,1)S(1)} %get-tuple-element.23), channel_id=1, source_target_pairs={{0,3},{1,2},{2,1},{3,0},{4,7},{5,6},{6,5},{7,4},{8,11},{9,10},{10,... | collective-permute-start | bytes 393224 | tf_op jit(solution)/shard_map/ppermute | solution.py:231
  21.2 0.7 fusion
  21.9 0.0 copy-start.1
  21.9 0.1 pad_add_fusion.place_of
  22.0 0.7 copy-done.2
  22.6 0.1 copy.20.table
  22.7 0.2 all-to-all-done.early
  22.9 1.3 %collective-permute-start.5 = (bf16[1040,128]{1,0:T(8,128)(2,1)S(1)}, bf16[1040,128]{1,0:T(8,128)(2,1)S(1)}, u32[]{:S(2)}, u32[]{:S(2)}) collective-permute-start(bf16[1040,128]{1,0:T(8,128)(2,1)S(1)} %get-tuple-element.27), channel_id=1, source_target_pairs={{64,0},{65,1},{66,2},{67,3},{128,64},{129,65},{130,66},{131,67},{1... | collective-permute-start | bytes 798728 | tf_op jit(solution)/shard_map/ppermute | solution.py:271
  24.2 5.4 %collective-permute-start.6 = (bf16[1040,128]{1,0:T(8,128)(2,1)S(1)}, bf16[1040,128]{1,0:T(8,128)(2,1)S(1)}, u32[]{:S(2)}, u32[]{:S(2)}) collective-permute-start(bf16[1040,128]{1,0:T(8,128)(2,1)S(1)} %get-tuple-element.28), channel_id=1, source_target_pairs={{0,64},{1,65},{2,66},{3,67},{64,128},{65,129},{66,130},{67,131},{1... | collective-permute-start | bytes 798728 | tf_op jit(solution)/shard_map/ppermute | solution.py:271
  29.7 0.0 collective-permute-done.refs_1_
  29.7 3.3 %collective-permute-done.1.refs_2_ = bf16[2,4,64,128]{3,2,1,0:T(8,128)(2,1)S(1)} collective-permute-done((bf16[2,4,64,128]{3,2,1,0:T(8,128)(2,1)S(1)}, bf16[2,4,64,128]{3,2,1,0:T(8,128)(2,1)S(1)}, u32[]{:S(2)}, u32[]{:S(2)}) %collective-permute-start.1) | collective-permute-done | bytes 131104 | tf_op jit(solution)/shard_map/ppermute | solution.py:231
  33.0 2.6 %shard_map.57 = (f32[4,128,128]{2,1,0:T(8,128)S(1)}, bf16[4,128,128]{2,1,0:T(8,128)(2,1)S(1)}, bf16[256,2048]{1,0:T(8,128)(2,1)S(1)}, bf16[1040,128]{1,0:T(8,128)(2,1)S(1)}, bf16[1040,128]{1,0:T(8,128)(2,1)S(1)}) custom-call(s32[2]{0:T(128)S(1)} %pad_add_fusion.place_of, f32[8,16]{1,0:T(8,128)S(1)} %copy.20.table, f32[16,128]{1,0:T(8,128)S(1)} %pad_maximum_fusion.cells, ...), custom_call_target="tpu_custom_call" | custom-call | flops 536870912 | bytes 4194304 | tf_op jit(solution)/shard_map/pallas_call | solution.py:260
  35.6 4.7 %collective-permute-start.3 = (bf16[1040,128]{1,0:T(8,128)(2,1)S(1)}, bf16[1040,128]{1,0:T(8,128)(2,1)S(1)}, u32[]{:S(2)}, u32[]{:S(2)}) collective-permute-start(bf16[1040,128]{1,0:T(8,128)(2,1)S(1)} %get-tuple-element.25), channel_id=1, source_target_pairs={{1,0},{2,1},{3,2},{7,3},{6,7},{5,6},{4,5},{8,4},{9,8},{10,9},{11,1... | collective-permute-start | bytes 798728 | tf_op jit(solution)/shard_map/ppermute | solution.py:274
  40.3 6.5 %collective-permute-start.4 = (bf16[1040,128]{1,0:T(8,128)(2,1)S(1)}, bf16[1040,128]{1,0:T(8,128)(2,1)S(1)}, u32[]{:S(2)}, u32[]{:S(2)}) collective-permute-start(bf16[1040,128]{1,0:T(8,128)(2,1)S(1)} %get-tuple-element.26), channel_id=1, source_target_pairs={{0,1},{1,2},{2,3},{3,7},{7,6},{6,5},{5,4},{4,8},{8,9},{9,10},{10,1... | collective-permute-start | bytes 798728 | tf_op jit(solution)/shard_map/ppermute | solution.py:274
  46.9 1.5 %shard_map.59 = (f32[4,64,128]{2,1,0:T(8,128)S(1)}, bf16[4,64,128]{2,1,0:T(8,128)(2,1)S(1)}) custom-call(s32[2]{0:T(128)S(1)} %pad_add_fusion.place_of, f32[8,128]{1,0:T(8,128)S(1)} %pad_maximum_fusion.1.speeds, bf16[256,2048]{1,0:T(8,128)(2,1)S(1)} %get-tuple-element.24.modes, bf16[1040,128]{1,0:T(8,128)(2,1)S(1)} %collective-permute-done.5.after, ...), custom_call_target="tpu_custom_call" | custom-call | flops 402653184 | bytes 3145728 | tf_op jit(solution)/shard_map/pallas_call | solution.py:281
  48.4 0.9 collective-permute-done.3.after
  49.3 0.9 collective-permute-done.4.before
  50.2 1.5 %shard_map.60 = (f32[4,256,128]{2,1,0:T(8,128)S(1)}, bf16[4,256,128]{2,1,0:T(8,128)(2,1)S(1)}) custom-call(s32[2]{0:T(128)S(1)} %pad_add_fusion.place_of, f32[8,128]{1,0:T(8,128)S(1)} %pad_maximum_fusion.1.speeds, bf16[256,2048]{1,0:T(8,128)(2,1)S(1)} %get-tuple-element.24.modes, bf16[1040,128]{1,0:T(8,128)(2,1)S(1)} %collective-permute-done.3.after, ...), custom_call_target="tpu_custom_call" | custom-call | flops 402653184 | bytes 3145728 | tf_op jit(solution)/shard_map/pallas_call | solution.py:290
  51.7 3.9 %collective-permute-start.7 = (bf16[4,256,128]{2,1,0:T(8,128)(2,1)S(1)}, bf16[4,256,128]{2,1,0:T(8,128)(2,1)S(1)}, u32[]{:S(2)}, u32[]{:S(2)}) collective-permute-start(bf16[4,256,128]{2,1,0:T(8,128)(2,1)S(1)} %get-tuple-element.34), channel_id=1, source_target_pairs={{0,4},{4,0},{1,5},{5,1},{2,6},{6,2},{3,7},{7,3},{8,12},{12,8},{9,1... | collective-permute-start | bytes 786440 | tf_op jit(solution)/shard_map/ppermute | solution.py:301
  55.6 1.1 collective-permute-done.7
  56.7 0.1 add_convert_fusion
  56.8 32.8 %all_to_all.15 = bf16[256,4,128]{2,1,0:T(4,128)(2,1)S(1)} all-to-all(bf16[256,4,128]{2,1,0:T(4,128)(2,1)S(1)} %bitcast.38), channel_id=1, replica_groups=mesh['gx'=8,'y'=8,'core'=2,'ma'=4] {'ma','gx','y'}, dimensions={0} | all-to-all | bytes 524288 | tf_op jit(solution)/shard_map/all_to_all | solution.py:305
  89.6 0.3 convert_reduce_fusion
  90.0 24.0 %all_to_all.16 = bf16[128,4,128]{2,1,0:T(4,128)(2,1)S(1)} all-to-all(bf16[128,4,128]{2,1,0:T(4,128)(2,1)S(1)} %broadcast_in_dim.5), channel_id=1, replica_groups=mesh['gx'=8,'y'=8,'core'=2,'ma'=4] {'core','gx','y'}, dimensions={0} | all-to-all | bytes 262144 | tf_op jit(solution)/shard_map/all_to_all | solution.py:308
  113.9 0.7 copy_bitcast_fusion
  (22 shorter events, 0.2 us)
Async XLA Ops:
  3.4 19.5 %all-to-all-start = ((bf16[4,2,4,64,128]{4,3,2,1,0:T(8,128)(2,1)}), bf16[4,2,4,64,128]{4,3,2,1,0:T(8,128)(2,1)S(1)}, u32[]{:S(2)}, u32[]{:S(2)}) async-start(bf16[4,2,4,64,128]{4,3,2,1,0:T(8,128)(2,1)} %shard_map.55.early), calls=%async_computation | async-start | bytes 1048576 | tf_op jit(solution)/shard_map/all_to_all | solution.py:229
  11.2 9.9 %copy-start = (f32[3,2,8,128]{3,2,1,0:T(8,128)S(1)}, f32[3,2,8,128]{3,2,1,0:T(8,128)}, u32[]{:S(2)}) copy-start(f32[3,2,8,128]{3,2,1,0:T(8,128)} %param.6) | copy-start | bytes 73732
  11.8 17.9 %collective-permute-start = (bf16[2,4,64,128]{3,2,1,0:T(8,128)(2,1)S(1)}, bf16[2,4,64,128]{3,2,1,0:T(8,128)(2,1)S(1)}, u32[]{:S(2)}, u32[]{:S(2)}) collective-permute-start(bf16[2,4,64,128]{3,2,1,0:T(8,128)(2,1)S(1)} %get-tuple-element.21), channel_id=1, source_target_pairs={{0,1},{1,0},{2,3},{3,2},{4,5},{5,4},{6,7},{7,6},{8,9},{9,8},{10,11... | collective-permute-start | bytes 393224 | tf_op jit(solution)/shard_map/ppermute | solution.py:231
  15.2 17.9 %collective-permute-start.1 = (bf16[2,4,64,128]{3,2,1,0:T(8,128)(2,1)S(1)}, bf16[2,4,64,128]{3,2,1,0:T(8,128)(2,1)S(1)}, u32[]{:S(2)}, u32[]{:S(2)}) collective-permute-start(bf16[2,4,64,128]{3,2,1,0:T(8,128)(2,1)S(1)} %get-tuple-element.22), channel_id=1, source_target_pairs={{0,2},{1,3},{2,0},{3,1},{4,6},{5,7},{6,4},{7,5},{8,10},{9,11},{10,... | collective-permute-start | bytes 393224 | tf_op jit(solution)/shard_map/ppermute | solution.py:231
  19.1 13.9 %collective-permute-start.2 = (bf16[2,4,64,128]{3,2,1,0:T(8,128)(2,1)S(1)}, bf16[2,4,64,128]{3,2,1,0:T(8,128)(2,1)S(1)}, u32[]{:S(2)}, u32[]{:S(2)}) collective-permute-start(bf16[2,4,64,128]{3,2,1,0:T(8,128)(2,1)S(1)} %get-tuple-element.23), channel_id=1, source_target_pairs={{0,3},{1,2},{2,1},{3,0},{4,7},{5,6},{6,5},{7,4},{8,11},{9,10},{10,... | collective-permute-start | bytes 393224 | tf_op jit(solution)/shard_map/ppermute | solution.py:231
  21.9 0.8 copy-start.1
  22.0 0.7 copy-start.2
  22.9 23.9 %collective-permute-start.5 = (bf16[1040,128]{1,0:T(8,128)(2,1)S(1)}, bf16[1040,128]{1,0:T(8,128)(2,1)S(1)}, u32[]{:S(2)}, u32[]{:S(2)}) collective-permute-start(bf16[1040,128]{1,0:T(8,128)(2,1)S(1)} %get-tuple-element.27), channel_id=1, source_target_pairs={{64,0},{65,1},{66,2},{67,3},{128,64},{129,65},{130,66},{131,67},{1... | collective-permute-start | bytes 798728 | tf_op jit(solution)/shard_map/ppermute | solution.py:271
  24.2 22.6 %collective-permute-start.6 = (bf16[1040,128]{1,0:T(8,128)(2,1)S(1)}, bf16[1040,128]{1,0:T(8,128)(2,1)S(1)}, u32[]{:S(2)}, u32[]{:S(2)}) collective-permute-start(bf16[1040,128]{1,0:T(8,128)(2,1)S(1)} %get-tuple-element.28), channel_id=1, source_target_pairs={{0,64},{1,65},{2,66},{3,67},{64,128},{65,129},{66,130},{67,131},{1... | collective-permute-start | bytes 798728 | tf_op jit(solution)/shard_map/ppermute | solution.py:271
  35.6 13.7 %collective-permute-start.3 = (bf16[1040,128]{1,0:T(8,128)(2,1)S(1)}, bf16[1040,128]{1,0:T(8,128)(2,1)S(1)}, u32[]{:S(2)}, u32[]{:S(2)}) collective-permute-start(bf16[1040,128]{1,0:T(8,128)(2,1)S(1)} %get-tuple-element.25), channel_id=1, source_target_pairs={{1,0},{2,1},{3,2},{7,3},{6,7},{5,6},{4,5},{8,4},{9,8},{10,9},{11,1... | collective-permute-start | bytes 798728 | tf_op jit(solution)/shard_map/ppermute | solution.py:274
  40.3 9.9 %collective-permute-start.4 = (bf16[1040,128]{1,0:T(8,128)(2,1)S(1)}, bf16[1040,128]{1,0:T(8,128)(2,1)S(1)}, u32[]{:S(2)}, u32[]{:S(2)}) collective-permute-start(bf16[1040,128]{1,0:T(8,128)(2,1)S(1)} %get-tuple-element.26), channel_id=1, source_target_pairs={{0,1},{1,2},{2,3},{3,7},{7,6},{6,5},{5,4},{4,8},{8,9},{9,10},{10,1... | collective-permute-start | bytes 798728 | tf_op jit(solution)/shard_map/ppermute | solution.py:274
  51.7 5.0 %collective-permute-start.7 = (bf16[4,256,128]{2,1,0:T(8,128)(2,1)S(1)}, bf16[4,256,128]{2,1,0:T(8,128)(2,1)S(1)}, u32[]{:S(2)}, u32[]{:S(2)}) collective-permute-start(bf16[4,256,128]{2,1,0:T(8,128)(2,1)S(1)} %get-tuple-element.34), channel_id=1, source_target_pairs={{0,4},{4,0},{1,5},{5,1},{2,6},{6,2},{3,7},{7,3},{8,12},{12,8},{9,1... | collective-permute-start | bytes 786440 | tf_op jit(solution)/shard_map/ppermute | solution.py:301

commit v13 on v12

--- a/solution.py
+++ b/solution.py
@@ -188,6 +188,13 @@
     send[:, 2 * block :, :] = zc_send[...]
 
 
+def order_kernel(whole, out):
+    rows = whole.shape[1]
+    for number in range(whole.shape[0]):
+        start = number // 2 * rows
+        out[number % 2, start : start + rows, :] = whole[number].astype(F32)
+
+
 def on_device(pod_modes, velocity, region, partner, coupling_table):
     block, fields, cells_x, cells_y, planes = pod_modes.shape
     names = ("gx", "y", "core", "ma")
@@ -305,8 +312,15 @@
     received = lax.all_to_all(both, ("ma", "gx", "y"), 0, 0)
     share = jnp.sum(received.astype(F32), axis=0) * scaling
     spread = jnp.broadcast_to(share.astype(BF16)[None], (shares * core_count,) + share.shape)
-    whole = lax.all_to_all(spread, ("core", "gx", "y"), 0, 0)
-    return whole.reshape(core_count, 4, block, LANES).transpose(1, 0, 3, 2).reshape(4, kinds, block).astype(F32)
+    whole = lax.all_to_all(spread, ("gx", "y", "core"), 0, 0)
+    whole = pl.pallas_call(
+        order_kernel,
+        out_shape=jax.ShapeDtypeStruct((core_count, 4 * block, LANES), F32),
+        in_specs=[vmem],
+        out_specs=vmem,
+        compiler_params=params,
+    )(whole)
+    return whole.reshape(core_count, 4, block, LANES).transpose(1, 0, 3, 2).reshape(4, kinds, block)
 
 
 def solution(mesh):

time: 115 us -> 115 us (level)
  no operation moved by 1% of the time
where the time goes in v13:
time: 115 us; the launch traced here: 114 us
  blocking collectives  56.5 us (49%)
  starting transfers between devices  38.9 us (34%)
  Pallas kernels  7.64 us (7%)
  waiting for transfers between devices  6.43 us (6%)
  local copies, waits for them, and re-layouts  3.52 us (3%)
  other arithmetic  1.17 us (1%)
    all_to_all x1, blocking collectives, on_device(): received = lax.all_to_all(both, ('ma', 'gx', 'y'), 0, 0)  32.8 us
    all_to_all x1, blocking collectives, on_device(): whole = lax.all_to_all(spread, ('gx', 'y', 'core'), 0, 0)  23.7 us
    ppermute x2, starting transfers between devices, along_y(): return lax.ppermute(part, names, steps_along_y(shape, step))  11.2 us
    ppermute x3, starting transfers between devices, on_device(): late[t] = lax.ppermute(late[t], 'ma', [(i, i ^ t) for i in range(ma_count)])  9.28 us
    all_to_all x1, starting transfers between devices, on_device(): early = lax.all_to_all(early, 'ma', 0, 0)  7.81 us
    ppermute x2, starting transfers between devices, along_x(): return lax.ppermute(part, ('gx', 'ma'), steps_along_x(shape, step))  6.72 us
    ppermute x1, starting transfers between devices, core_swap(): return lax.ppermute(part, 'core', [(i, 1 - i) for i in range(core_count)])  3.89 us
    ppermute x3, waiting for transfers between devices, on_device(): late[t] = lax.ppermute(late[t], 'ma', [(i, i ^ t) for i in range(ma_count)])  3.34 us
  transfers between devices with their start and end apart: 9, of which 5 were waited for; matrix products, arithmetic and copies ran while one was open for 1% of the time, Pallas kernels for 4%

profile of v13, /device:TPU:1, one launch (start us, length us, event | category | flops | bytes accessed | tf_op | source)
XLA Modules:
  0.0 114.4 jit_solution(5154372149915104299)
XLA Ops:
  0.0 1.9 %copy.14 = bf16[8,2,4,64,128]{4,3,2,1,0:T(8,128)(2,1)S(1)} copy(bf16[8,2,4,64,128]{4,0,1,2,3:T(8,128)(2,1)} %bitcast.37) | data formatting | bytes 2097152 | tf_op jit(solution)/shard_map/transpose | solution.py:216
  1.9 0.1 stack.28
  2.0 1.4 %shard_map.55.early = bf16[4,2,4,64,128]{4,3,2,1,0:T(8,128)(2,1)} custom-call(s32[8]{0:T(128)S(1)} %broadcast_select_fusion.wanted, bf16[4,2,2,4,64,128]{5,4,3,2,1,0:T(8,128)(2,1)S(1)} %bitcast.34), custom_call_target="tpu_custom_call" | custom-call | bytes 1048576 | tf_op jit(solution)/shard_map/pallas_call | solution.py:219
  3.4 7.8 %all-to-all-start = ((bf16[4,2,4,64,128]{4,3,2,1,0:T(8,128)(2,1)}), bf16[4,2,4,64,128]{4,3,2,1,0:T(8,128)(2,1)S(1)}, u32[]{:S(2)}, u32[]{:S(2)}) async-start(bf16[4,2,4,64,128]{4,3,2,1,0:T(8,128)(2,1)} %shard_map.55.early), calls=%async_computation | async-start | bytes 1048576 | tf_op jit(solution)/shard_map/all_to_all | solution.py:236
  11.2 0.6 shard_map.56
  11.8 3.4 %collective-permute-start = (bf16[2,4,64,128]{3,2,1,0:T(8,128)(2,1)S(1)}, bf16[2,4,64,128]{3,2,1,0:T(8,128)(2,1)S(1)}, u32[]{:S(2)}, u32[]{:S(2)}) collective-permute-start(bf16[2,4,64,128]{3,2,1,0:T(8,128)(2,1)S(1)} %get-tuple-element.21), channel_id=1, source_target_pairs={{0,1},{1,0},{2,3},{3,2},{4,5},{5,4},{6,7},{7,6},{8,9},{9,8},{10,11... | collective-permute-start | bytes 393224 | tf_op jit(solution)/shard_map/ppermute | solution.py:238
  15.2 4.0 %collective-permute-start.1 = (bf16[2,4,64,128]{3,2,1,0:T(8,128)(2,1)S(1)}, bf16[2,4,64,128]{3,2,1,0:T(8,128)(2,1)S(1)}, u32[]{:S(2)}, u32[]{:S(2)}) collective-permute-start(bf16[2,4,64,128]{3,2,1,0:T(8,128)(2,1)S(1)} %get-tuple-element.22), channel_id=1, source_target_pairs={{0,2},{1,3},{2,0},{3,1},{4,6},{5,7},{6,4},{7,5},{8,10},{9,11},{10,... | collective-permute-start | bytes 393224 | tf_op jit(solution)/shard_map/ppermute | solution.py:238
  19.1 1.9 %collective-permute-start.2 = (bf16[2,4,64,128]{3,2,1,0:T(8,128)(2,1)S(1)}, bf16[2,4,64,128]{3,2,1,0:T(8,128)(2,1)S(1)}, u32[]{:S(2)}, u32[]{:S(2)}) collective-permute-start(bf16[2,4,64,128]{3,2,1,0:T(8,128)(2,1)S(1)} %get-tuple-element.23), channel_id=1, source_target_pairs={{0,3},{1,2},{2,1},{3,0},{4,7},{5,6},{6,5},{7,4},{8,11},{9,10},{10,... | collective-permute-start | bytes 393224 | tf_op jit(solution)/shard_map/ppermute | solution.py:238
  21.2 0.7 fusion
  21.9 0.0 copy-start.1
  21.9 0.1 pad_add_fusion.place_of
  22.0 0.7 copy-done.2
  22.6 0.1 copy.15.table
  22.7 0.2 all-to-all-done.early
  22.9 1.3 %collective-permute-start.5 = (bf16[1040,128]{1,0:T(8,128)(2,1)S(1)}, bf16[1040,128]{1,0:T(8,128)(2,1)S(1)}, u32[]{:S(2)}, u32[]{:S(2)}) collective-permute-start(bf16[1040,128]{1,0:T(8,128)(2,1)S(1)} %get-tuple-element.27), channel_id=1, source_target_pairs={{64,0},{65,1},{66,2},{67,3},{128,64},{129,65},{130,66},{131,67},{1... | collective-permute-start | bytes 798728 | tf_op jit(solution)/shard_map/ppermute | solution.py:278
  24.2 5.4 %collective-permute-start.6 = (bf16[1040,128]{1,0:T(8,128)(2,1)S(1)}, bf16[1040,128]{1,0:T(8,128)(2,1)S(1)}, u32[]{:S(2)}, u32[]{:S(2)}) collective-permute-start(bf16[1040,128]{1,0:T(8,128)(2,1)S(1)} %get-tuple-element.28), channel_id=1, source_target_pairs={{0,64},{1,65},{2,66},{3,67},{64,128},{65,129},{66,130},{67,131},{1... | collective-permute-start | bytes 798728 | tf_op jit(solution)/shard_map/ppermute | solution.py:278
  29.7 0.0 collective-permute-done.refs_1_
  29.7 3.3 %collective-permute-done.1.refs_2_ = bf16[2,4,64,128]{3,2,1,0:T(8,128)(2,1)S(1)} collective-permute-done((bf16[2,4,64,128]{3,2,1,0:T(8,128)(2,1)S(1)}, bf16[2,4,64,128]{3,2,1,0:T(8,128)(2,1)S(1)}, u32[]{:S(2)}, u32[]{:S(2)}) %collective-permute-start.1) | collective-permute-done | bytes 131104 | tf_op jit(solution)/shard_map/ppermute | solution.py:238
  33.0 2.6 %shard_map.57 = (f32[4,128,128]{2,1,0:T(8,128)S(1)}, bf16[4,128,128]{2,1,0:T(8,128)(2,1)S(1)}, bf16[256,2048]{1,0:T(8,128)(2,1)S(1)}, bf16[1040,128]{1,0:T(8,128)(2,1)S(1)}, bf16[1040,128]{1,0:T(8,128)(2,1)S(1)}) custom-call(s32[2]{0:T(128)S(1)} %pad_add_fusion.place_of, f32[8,16]{1,0:T(8,128)S(1)} %copy.15.table, f32[16,128]{1,0:T(8,128)S(1)} %pad_maximum_fusion.cells, ...), custom_call_target="tpu_custom_call" | custom-call | flops 536870912 | bytes 4194304 | tf_op jit(solution)/shard_map/pallas_call | solution.py:267
  35.6 4.7 %collective-permute-start.3 = (bf16[1040,128]{1,0:T(8,128)(2,1)S(1)}, bf16[1040,128]{1,0:T(8,128)(2,1)S(1)}, u32[]{:S(2)}, u32[]{:S(2)}) collective-permute-start(bf16[1040,128]{1,0:T(8,128)(2,1)S(1)} %get-tuple-element.25), channel_id=1, source_target_pairs={{1,0},{2,1},{3,2},{7,3},{6,7},{5,6},{4,5},{8,4},{9,8},{10,9},{11,1... | collective-permute-start | bytes 798728 | tf_op jit(solution)/shard_map/ppermute | solution.py:281
  40.3 6.5 %collective-permute-start.4 = (bf16[1040,128]{1,0:T(8,128)(2,1)S(1)}, bf16[1040,128]{1,0:T(8,128)(2,1)S(1)}, u32[]{:S(2)}, u32[]{:S(2)}) collective-permute-start(bf16[1040,128]{1,0:T(8,128)(2,1)S(1)} %get-tuple-element.26), channel_id=1, source_target_pairs={{0,1},{1,2},{2,3},{3,7},{7,6},{6,5},{5,4},{4,8},{8,9},{9,10},{10,1... | collective-permute-start | bytes 798728 | tf_op jit(solution)/shard_map/ppermute | solution.py:281
  46.9 1.5 %shard_map.59 = (f32[4,64,128]{2,1,0:T(8,128)S(1)}, bf16[4,64,128]{2,1,0:T(8,128)(2,1)S(1)}) custom-call(s32[2]{0:T(128)S(1)} %pad_add_fusion.place_of, f32[8,128]{1,0:T(8,128)S(1)} %pad_maximum_fusion.1.speeds, bf16[256,2048]{1,0:T(8,128)(2,1)S(1)} %get-tuple-element.24.modes, bf16[1040,128]{1,0:T(8,128)(2,1)S(1)} %collective-permute-done.5.after, ...), custom_call_target="tpu_custom_call" | custom-call | flops 402653184 | bytes 3145728 | tf_op jit(solution)/shard_map/pallas_call | solution.py:288
  48.4 0.9 collective-permute-done.3.after
  49.3 0.9 collective-permute-done.4.before
  50.2 1.5 %shard_map.60 = (f32[4,256,128]{2,1,0:T(8,128)S(1)}, bf16[4,256,128]{2,1,0:T(8,128)(2,1)S(1)}) custom-call(s32[2]{0:T(128)S(1)} %pad_add_fusion.place_of, f32[8,128]{1,0:T(8,128)S(1)} %pad_maximum_fusion.1.speeds, bf16[256,2048]{1,0:T(8,128)(2,1)S(1)} %get-tuple-element.24.modes, bf16[1040,128]{1,0:T(8,128)(2,1)S(1)} %collective-permute-done.3.after, ...), custom_call_target="tpu_custom_call" | custom-call | flops 402653184 | bytes 3145728 | tf_op jit(solution)/shard_map/pallas_call | solution.py:297
  51.7 3.9 %collective-permute-start.7 = (bf16[4,256,128]{2,1,0:T(8,128)(2,1)S(1)}, bf16[4,256,128]{2,1,0:T(8,128)(2,1)S(1)}, u32[]{:S(2)}, u32[]{:S(2)}) collective-permute-start(bf16[4,256,128]{2,1,0:T(8,128)(2,1)S(1)} %get-tuple-element.34), channel_id=1, source_target_pairs={{0,4},{4,0},{1,5},{5,1},{2,6},{6,2},{3,7},{7,3},{8,12},{12,8},{9,1... | collective-permute-start | bytes 786440 | tf_op jit(solution)/shard_map/ppermute | solution.py:308
  55.6 1.1 collective-permute-done.7
  56.7 0.1 add_convert_fusion
  56.8 32.8 %all_to_all.15 = bf16[256,4,128]{2,1,0:T(4,128)(2,1)S(1)} all-to-all(bf16[256,4,128]{2,1,0:T(4,128)(2,1)S(1)} %bitcast.38), channel_id=1, replica_groups=mesh['gx'=8,'y'=8,'core'=2,'ma'=4] {'ma','gx','y'}, dimensions={0} | all-to-all | bytes 524288 | tf_op jit(solution)/shard_map/all_to_all | solution.py:312
  89.6 0.3 convert_reduce_fusion
  90.0 23.7 %all_to_all.16.whole = bf16[128,4,128]{2,1,0:T(4,128)(2,1)S(1)} all-to-all(bf16[128,4,128]{2,1,0:T(4,128)(2,1)S(1)} %broadcast_in_dim.5), channel_id=1, replica_groups=mesh['gx'=8,'y'=8,'core'=2,'ma'=4] {'gx','y','core'}, dimensions={0} | all-to-all | bytes 262144 | tf_op jit(solution)/shard_map/all_to_all | solution.py:315
  113.7 0.7 copy.19
  (23 shorter events, 0.2 us)
Async XLA Ops:
  3.4 19.5 %all-to-all-start = ((bf16[4,2,4,64,128]{4,3,2,1,0:T(8,128)(2,1)}), bf16[4,2,4,64,128]{4,3,2,1,0:T(8,128)(2,1)S(1)}, u32[]{:S(2)}, u32[]{:S(2)}) async-start(bf16[4,2,4,64,128]{4,3,2,1,0:T(8,128)(2,1)} %shard_map.55.early), calls=%async_computation | async-start | bytes 1048576 | tf_op jit(solution)/shard_map/all_to_all | solution.py:236
  11.2 9.9 %copy-start = (f32[3,2,8,128]{3,2,1,0:T(8,128)S(1)}, f32[3,2,8,128]{3,2,1,0:T(8,128)}, u32[]{:S(2)}) copy-start(f32[3,2,8,128]{3,2,1,0:T(8,128)} %param.6) | copy-start | bytes 73732
  11.8 17.9 %collective-permute-start = (bf16[2,4,64,128]{3,2,1,0:T(8,128)(2,1)S(1)}, bf16[2,4,64,128]{3,2,1,0:T(8,128)(2,1)S(1)}, u32[]{:S(2)}, u32[]{:S(2)}) collective-permute-start(bf16[2,4,64,128]{3,2,1,0:T(8,128)(2,1)S(1)} %get-tuple-element.21), channel_id=1, source_target_pairs={{0,1},{1,0},{2,3},{3,2},{4,5},{5,4},{6,7},{7,6},{8,9},{9,8},{10,11... | collective-permute-start | bytes 393224 | tf_op jit(solution)/shard_map/ppermute | solution.py:238
  15.2 17.9 %collective-permute-start.1 = (bf16[2,4,64,128]{3,2,1,0:T(8,128)(2,1)S(1)}, bf16[2,4,64,128]{3,2,1,0:T(8,128)(2,1)S(1)}, u32[]{:S(2)}, u32[]{:S(2)}) collective-permute-start(bf16[2,4,64,128]{3,2,1,0:T(8,128)(2,1)S(1)} %get-tuple-element.22), channel_id=1, source_target_pairs={{0,2},{1,3},{2,0},{3,1},{4,6},{5,7},{6,4},{7,5},{8,10},{9,11},{10,... | collective-permute-start | bytes 393224 | tf_op jit(solution)/shard_map/ppermute | solution.py:238
  19.1 13.9 %collective-permute-start.2 = (bf16[2,4,64,128]{3,2,1,0:T(8,128)(2,1)S(1)}, bf16[2,4,64,128]{3,2,1,0:T(8,128)(2,1)S(1)}, u32[]{:S(2)}, u32[]{:S(2)}) collective-permute-start(bf16[2,4,64,128]{3,2,1,0:T(8,128)(2,1)S(1)} %get-tuple-element.23), channel_id=1, source_target_pairs={{0,3},{1,2},{2,1},{3,0},{4,7},{5,6},{6,5},{7,4},{8,11},{9,10},{10,... | collective-permute-start | bytes 393224 | tf_op jit(solution)/shard_map/ppermute | solution.py:238
  21.9 0.8 copy-start.1
  22.0 0.7 copy-start.2
  22.9 23.9 %collective-permute-start.5 = (bf16[1040,128]{1,0:T(8,128)(2,1)S(1)}, bf16[1040,128]{1,0:T(8,128)(2,1)S(1)}, u32[]{:S(2)}, u32[]{:S(2)}) collective-permute-start(bf16[1040,128]{1,0:T(8,128)(2,1)S(1)} %get-tuple-element.27), channel_id=1, source_target_pairs={{64,0},{65,1},{66,2},{67,3},{128,64},{129,65},{130,66},{131,67},{1... | collective-permute-start | bytes 798728 | tf_op jit(solution)/shard_map/ppermute | solution.py:278
  24.2 22.6 %collective-permute-start.6 = (bf16[1040,128]{1,0:T(8,128)(2,1)S(1)}, bf16[1040,128]{1,0:T(8,128)(2,1)S(1)}, u32[]{:S(2)}, u32[]{:S(2)}) collective-permute-start(bf16[1040,128]{1,0:T(8,128)(2,1)S(1)} %get-tuple-element.28), channel_id=1, source_target_pairs={{0,64},{1,65},{2,66},{3,67},{64,128},{65,129},{66,130},{67,131},{1... | collective-permute-start | bytes 798728 | tf_op jit(solution)/shard_map/ppermute | solution.py:278
  35.6 13.7 %collective-permute-start.3 = (bf16[1040,128]{1,0:T(8,128)(2,1)S(1)}, bf16[1040,128]{1,0:T(8,128)(2,1)S(1)}, u32[]{:S(2)}, u32[]{:S(2)}) collective-permute-start(bf16[1040,128]{1,0:T(8,128)(2,1)S(1)} %get-tuple-element.25), channel_id=1, source_target_pairs={{1,0},{2,1},{3,2},{7,3},{6,7},{5,6},{4,5},{8,4},{9,8},{10,9},{11,1... | collective-permute-start | bytes 798728 | tf_op jit(solution)/shard_map/ppermute | solution.py:281
  40.3 9.9 %collective-permute-start.4 = (bf16[1040,128]{1,0:T(8,128)(2,1)S(1)}, bf16[1040,128]{1,0:T(8,128)(2,1)S(1)}, u32[]{:S(2)}, u32[]{:S(2)}) collective-permute-start(bf16[1040,128]{1,0:T(8,128)(2,1)S(1)} %get-tuple-element.26), channel_id=1, source_target_pairs={{0,1},{1,2},{2,3},{3,7},{7,6},{6,5},{5,4},{4,8},{8,9},{9,10},{10,1... | collective-permute-start | bytes 798728 | tf_op jit(solution)/shard_map/ppermute | solution.py:281
  51.7 5.0 %collective-permute-start.7 = (bf16[4,256,128]{2,1,0:T(8,128)(2,1)S(1)}, bf16[4,256,128]{2,1,0:T(8,128)(2,1)S(1)}, u32[]{:S(2)}, u32[]{:S(2)}) collective-permute-start(bf16[4,256,128]{2,1,0:T(8,128)(2,1)S(1)} %get-tuple-element.34), channel_id=1, source_target_pairs={{0,4},{4,0},{1,5},{5,1},{2,6},{6,2},{3,7},{7,3},{8,12},{12,8},{9,1... | collective-permute-start | bytes 786440 | tf_op jit(solution)/shard_map/ppermute | solution.py:308
